TPU v7x, 512 devices: a whole 4x8x8 slice. The times are simulated.
512 devices in a mesh: dp: 16 (over y_lo, x), ctx: 32 (over z, y_hi, core).
Axes of the slice: x: 4, y: 8 (y_hi: 2, y_lo: 4; y = y_hi * 4 + y_lo), z: 8, core: 2. Of those that a mesh axis runs over, the one named last changes fastest.
Arguments:
- tokens: bfloat16 [65536, 1024], P(('dp', 'ctx')), may hold values from -6 to 6
- grad_out: bfloat16 [65536, 1024], P(('dp', 'ctx')), may hold values from -6 to 6
- gates: bfloat16 [65536, 8], P(('dp', 'ctx')), may hold values from 0.049804688 to 0.5
- expert_ids: int32 [65536, 8], P(('dp', 'ctx')), may hold values from 0 to 63, all different within a row; in each aligned block of 128 rows (0 to 127, 128 to 255, ...) at most 18 rows name the same one
- w_up: bfloat16 [64, 1024, 384], P('ctx', 'dp'), may hold values from -0.1875 to 0.1875
- w_down: bfloat16 [64, 384, 1024], P('ctx', None, 'dp'), may hold values from -0.3125 to 0.3125
Outputs:
- grad_tokens: bfloat16 [65536, 1024], P(('dp', 'ctx'))
- grad_gates: bfloat16 [65536, 8], P(('dp', 'ctx'))
- grad_up: bfloat16 [64, 1024, 384], P('ctx', 'dp')
- grad_down: bfloat16 [64, 384, 1024], P('ctx', None, 'dp')
Inputs may be any that keep to these rules, and one draw needn't show every extreme that they name: `expert_ids`: each row names 8 different experts. Among the 128 rows of one device no expert is named more than 18 times, and in every draw some expert is named exactly 18 times in some device's rows.
All inputs are finite; a program needn't handle non-finite values.
Results may differ from a plain program's by a relative error of at most 0.023.
Values may be sent and summed in bfloat16 or wider, within the bound.
No kernel may reach another device: no remote copies, remote signals or barrier semaphores. Data moves between devices by JAX's collectives and lax.ppermute only.
A program may use at most 64 MiB of HBM per device.

v0:
```python
import jax
import jax.numpy as jnp
from jax import lax
from jax.sharding import PartitionSpec as P


def swish_grad(pre_act, sigmoid_a):
    return sigmoid_a * (1.0 + pre_act * (1.0 - sigmoid_a))


def per_device(tokens, grad_out, gates, expert_ids, w_up, w_down):
    tok_rows, width = tokens.shape
    top_count = expert_ids.shape[1]
    ctx_count = lax.axis_size("ctx")
    exp_local = w_up.shape[0]
    experts_all = exp_local * ctx_count
    capacity = tok_rows * top_count * 9 // (8 * experts_all)
    flat_ids = expert_ids.reshape(-1)
    onehot = (flat_ids[:, None] == jnp.arange(experts_all, dtype=jnp.int32)[None, :]).astype(
        jnp.int32
    )
    earlier = jnp.cumsum(onehot, axis=0) - onehot
    slot_pos = jnp.sum(earlier * onehot, axis=1)
    owner = flat_ids // exp_local
    local_idx = flat_ids % exp_local
    target = (local_idx * ctx_count + owner) * capacity + slot_pos
    token_pos = jnp.arange(tok_rows * top_count, dtype=jnp.int32) // top_count
    buffer_len = experts_all * capacity
    source_row = jnp.full((buffer_len,), tok_rows, jnp.int32).at[target].set(token_pos)
    paired = jnp.concatenate((tokens, grad_out), axis=1)
    send_pair = jnp.take(paired, source_row, axis=0, mode="fill", fill_value=0)
    send_gate = jnp.zeros((buffer_len,), jnp.bfloat16).at[target].set(gates.reshape(-1))
    block_shape = (exp_local, ctx_count, capacity, width)
    slot_shape = (exp_local, ctx_count, capacity)
    recv_pair, recv_gate = (
        lax.all_to_all(
            send_pair.reshape(exp_local, ctx_count, capacity, 2 * width),
            "ctx",
            split_axis=1,
            concat_axis=1,
            tiled=True,
        ),
        lax.all_to_all(
            send_gate.reshape(slot_shape), "ctx", split_axis=1, concat_axis=1, tiled=True
        ),
    )
    row_len = ctx_count * capacity
    rows_pair = recv_pair.reshape(exp_local, row_len, 2 * width)
    rows_x = rows_pair[:, :, :width]
    rows_grad = rows_pair[:, :, width:]
    rows_gate = recv_gate.reshape(exp_local, row_len)
    up_full, down_full = (
        lax.all_gather(w_up, "dp", axis=1, tiled=True),
        lax.all_gather(w_down, "dp", axis=2, tiled=True),
    )
    pre_act = jnp.einsum("erd,edf->erf", rows_x, up_full, preferred_element_type=jnp.float32)
    sigmoid_a = jax.nn.sigmoid(pre_act)
    hidden = (pre_act * sigmoid_a).astype(jnp.bfloat16)
    outputs = jnp.einsum(
        "erf,efd->erd", hidden, down_full, preferred_element_type=jnp.float32
    ).astype(jnp.bfloat16)
    grad_y = (rows_gate[:, :, None].astype(jnp.float32) * rows_grad).astype(jnp.bfloat16)
    grad_h = jnp.einsum("erd,efd->erf", grad_y, down_full, preferred_element_type=jnp.float32)
    grad_a = (grad_h * swish_grad(pre_act, sigmoid_a)).astype(jnp.bfloat16)
    grad_rows = jnp.einsum(
        "erf,edf->erd", grad_a, up_full, preferred_element_type=jnp.float32
    ).astype(jnp.bfloat16)
    back_rows = lax.all_to_all(
        grad_rows.reshape(block_shape), "ctx", split_axis=1, concat_axis=1, tiled=True
    )
    back_out = lax.all_to_all(
        outputs.reshape(block_shape), "ctx", split_axis=1, concat_axis=1, tiled=True
    )
    picked_out = back_out.reshape(-1, width)[target].reshape(tok_rows, top_count, width)
    picked_scores = jnp.einsum(
        "td,tkd->tk", grad_out, picked_out, preferred_element_type=jnp.float32
    ).astype(jnp.bfloat16)
    picked_rows = back_rows.reshape(-1, width)[target].reshape(tok_rows, top_count, width)
    grad_tokens = jnp.sum(picked_rows.astype(jnp.float32), axis=1).astype(jnp.bfloat16)
    grad_tokens, grad_gates = (grad_tokens, picked_scores)
    up_part = jnp.einsum("erc,erf->cef", rows_x, grad_a, preferred_element_type=jnp.float32)
    down_part = jnp.einsum("erf,erc->cef", hidden, grad_y, preferred_element_type=jnp.float32)
    summed = lax.psum_scatter(
        jnp.stack((up_part, down_part), axis=1).astype(jnp.bfloat16),
        "dp",
        scatter_dimension=0,
        tiled=True,
    ).astype(jnp.float32)
    grad_up = jnp.transpose(summed[:, 0], (1, 0, 2)).astype(jnp.bfloat16)
    grad_down = jnp.transpose(summed[:, 1], (1, 2, 0)).astype(jnp.bfloat16)
    grad_up, grad_down = (grad_up, grad_down)
    return (grad_tokens, grad_gates, grad_up, grad_down)


def solution(mesh):
    in_specs = (
        P(("dp", "ctx"), None),
        P(("dp", "ctx"), None),
        P(("dp", "ctx"), None),
        P(("dp", "ctx"), None),
        P("ctx", "dp", None),
        P("ctx", None, "dp"),
    )
    out_specs = (
        P(("dp", "ctx"), None),
        P(("dp", "ctx"), None),
        P("ctx", "dp", None),
        P("ctx", None, "dp"),
    )
    return jax.shard_map(
        per_device, mesh=mesh, in_specs=in_specs, out_specs=out_specs, check_vma=False
    )
```

profile of v0, /device:TPU:64, one launch (start us, length us, event | category | flops | bytes accessed | tf_op | source)
XLA Modules:
  0.0 740.7 jit_solution(15632867575689190050)
XLA Ops:
  7.2 0.8 copy.52
  8.3 18.0 %reduce-window.6 = s32[64,8,128]{2,1,0:T(8,128)S(1)} reduce-window(s32[64,8,128]{2,1,0:T(8,128)S(1)} %fusion.20, s32[]{:T(128)} %constant.60.clone.1), window={size=1x1x128 pad=0_0x0_0x127_0}, to_apply=%region_0.0 | reduce-window | flops 8323072 | bytes 524292 | tf_op jit(solution)/shard_map/reduce-window
  27.3 7.6 %scatter_custom_fusion = bf16[1152]{0:T(1024)(128)(2,1)S(1)} fusion(s32[1024]{0:T(1024)S(1)} %bitcast.59, bf16[1024]{0:T(1024)(128)(2,1)S(1)} %reshape.238, bf16[]{:T(256)} %constant.59.clone.1), kind=kCustom, calls=%fused_computation.60 | custom fusion | bytes 2306 | tf_op jit(solution)/shard_map/scatter | solution.py:32
  34.9 0.1 reshape.201
  35.0 0.6 copy.58
  35.6 15.4 %all-to-all-start = ((bf16[2,32,18]{2,0,1:T(2,128)(2,1)}), bf16[2,32,18]{2,0,1:T(2,128)(2,1)S(1)}, u32[]{:S(2)}, u32[]{:S(2)}) async-start(bf16[2,32,18]{2,0,1:T(2,128)(2,1)} %copy.58), calls=%async_computation | async-start | bytes 32768 | tf_op jit(solution)/shard_map/all_to_all | solution.py:43
  51.0 4.8 scatter_custom_fusion.1
  55.9 6.0 gather_fusion
  62.0 7.5 %gather.13 = bf16[2,32,18,2048]{3,2,1,0:T(8,128)(2,1)} reshape(bf16[1152,2048]{1,0:T(8,128)(2,1)} %gather_fusion) | data formatting | bytes 9437184 | tf_op jit(solution)/shard_map/jit(_take)/gather | solution.py:31
  69.5 0.1 broadcast_in_dim.27
  69.6 6.0 broadcast_select_fusion
  75.6 9.9 %copy.61 = bf16[2,32,18,2048]{3,0,2,1:T(2,128)(2,1)} copy(bf16[2,32,18,2048]{3,2,1,0:T(8,128)(2,1)} %broadcast_select_fusion) | data formatting | bytes 9437184 | tf_op jit(solution)/shard_map/jit(_take)/select_n | solution.py:31
  85.5 12.2 %all-to-all-start.1 = ((bf16[2,32,18,2048]{3,0,2,1:T(2,128)(2,1)}), bf16[2,32,18,2048]{3,0,2,1:T(2,128)(2,1)}, u32[]{:S(2)}, u32[]{:S(2)}) async-start(bf16[2,32,18,2048]{3,0,2,1:T(2,128)(2,1)} %copy.61), calls=%async_computation.1 | async-start | bytes 9437184 | tf_op jit(solution)/shard_map/all_to_all | solution.py:36
  97.8 0.7 all-gather.5.cloned.1.call-update
  98.5 0.2 all-gather.3.cloned.1.call-start
  98.7 0.5 all-gather.3.cloned.1.call-update
  99.6 142.2 %all-to-all-done.1 = bf16[2,32,18,2048]{3,0,2,1:T(2,128)(2,1)} async-done(((bf16[2,32,18,2048]{3,0,2,1:T(2,128)(2,1)}), bf16[2,32,18,2048]{3,0,2,1:T(2,128)(2,1)}, u32[]{:S(2)}, u32[]{:S(2)}) %all-to-all-start.1) | async-done | bytes 4718624 | tf_op jit(solution)/shard_map/all_to_all | solution.py:36
  241.7 7.1 fusion.30
  248.9 32.6 %all-gather.5.cloned.1.call-done = bf16[2,1024,384]{2,1,0:T(8,128)(2,1)} async-done(((bf16[2,64,384]{2,1,0:T(8,128)(2,1)}), bf16[2,1024,384]{2,1,0:T(8,128)(2,1)}) %all-gather.5.cloned.1.call-update) | async-done | bytes 1572880 | tf_op jit(solution)/shard_map/all_gather | solution.py:53
  281.5 4.7 fusion.4
  286.2 99.7 %all-gather.3.cloned.1.call-done = bf16[2,384,1024]{1,2,0:T(8,128)(2,1)} async-done(((bf16[2,384,64]{1,2,0:T(8,128)(2,1)}), bf16[2,384,1024]{1,2,0:T(8,128)(2,1)}) %all-gather.3.cloned.1.call-update) | async-done | bytes 1572880 | tf_op jit(solution)/shard_map/all_gather | solution.py:54
  385.9 3.9 multiply_convert_fusion.4
  389.8 1.4 convolution_convert_fusion.1
  391.3 3.9 copy.64
  395.2 12.6 %all-to-all-start.2 = ((bf16[2,32,18,1024]{3,0,2,1:T(2,128)(2,1)}), bf16[2,32,18,1024]{3,0,2,1:T(2,128)(2,1)S(1)}, u32[]{:S(2)}, u32[]{:S(2)}) async-start(bf16[2,32,18,1024]{3,0,2,1:T(2,128)(2,1)} %bitcast.5), calls=%async_computation.2 | async-start | bytes 4718592 | tf_op jit(solution)/shard_map/all_to_all | solution.py:68
  407.8 3.4 convolution_convert_fusion
  411.2 3.9 copy.66
  415.1 52.4 %all-to-all-done.2 = bf16[2,32,18,1024]{3,0,2,1:T(2,128)(2,1)S(1)} async-done(((bf16[2,32,18,1024]{3,0,2,1:T(2,128)(2,1)}), bf16[2,32,18,1024]{3,0,2,1:T(2,128)(2,1)S(1)}, u32[]{:S(2)}, u32[]{:S(2)}) %all-to-all-start.2) | async-done | bytes 2359328 | tf_op jit(solution)/shard_map/all_to_all | solution.py:68
  467.5 1.4 copy-done
  468.8 18.3 %all-to-all-start.3 = ((bf16[2,32,18,1024]{3,0,2,1:T(2,128)(2,1)}), bf16[2,32,18,1024]{3,0,2,1:T(2,128)(2,1)}, u32[]{:S(2)}, u32[]{:S(2)}) async-start(bf16[2,32,18,1024]{3,0,2,1:T(2,128)(2,1)} %bitcast.7), calls=%async_computation.3 | async-start | bytes 4718592 | tf_op jit(solution)/shard_map/all_to_all | solution.py:71
  487.2 3.4 fusion.12
  490.6 1.8 fusion.15
  492.4 0.3 pad_maximum_fusion
  492.7 5.9 copy.69
  498.7 1.4 dynamic-slice
  500.7 200.3 %all-reduce.3.cloned.1.call-done = bf16[1024,2,2,384]{3,2,1,0:T(2,128)(2,1)} async-done(((bf16[1024,2,2,384]{3,2,1,0:T(2,128)(2,1)}), bf16[1024,2,2,384]{3,2,1,0:T(2,128)(2,1)}) %all-reduce.3.cloned.1.call-update) | async-done | bytes 3145744
  701.0 1.1 dynamic-slice_bitcast_fusion
  702.1 0.7 copy.70
  702.8 0.7 copy.71
  703.4 2.5 copy.65
  705.9 2.9 reshape.204
  708.9 5.4 gather_fusion.1
  714.2 3.7 bitcast_reduce_fusion
  718.0 4.2 copy.67
  722.1 2.9 reshape.207
  725.1 5.4 gather_fusion.2
  730.4 2.8 fusion
  733.3 0.7 copy.73
  (45 shorter events, 1.7 us)
Async XLA Ops:
  7.2 19.7 %copy-start.7 = (bf16[128,8]{0,1:T(8,128)(2,1)S(1)}, bf16[128,8]{0,1:T(8,128)(2,1)}, u32[]{:S(2)}) copy-start(bf16[128,8]{0,1:T(8,128)(2,1)} %param.8) | copy-start | bytes 6148
  7.2 48.7 %copy-start.5 = (bf16[128,1024]{1,0:T(8,128)(2,1)S(1)}, bf16[128,1024]{1,0:T(8,128)(2,1)}, u32[]{:S(2)}) copy-start(bf16[128,1024]{1,0:T(8,128)(2,1)} %param.6) | copy-start | bytes 786436
  7.2 48.7 %copy-start.6 = (bf16[128,1024]{1,0:T(8,128)(2,1)S(1)}, bf16[128,1024]{1,0:T(8,128)(2,1)}, u32[]{:S(2)}) copy-start(bf16[128,1024]{1,0:T(8,128)(2,1)} %param.7) | copy-start | bytes 786436
  35.6 49.9 %all-to-all-start = ((bf16[2,32,18]{2,0,1:T(2,128)(2,1)}), bf16[2,32,18]{2,0,1:T(2,128)(2,1)S(1)}, u32[]{:S(2)}, u32[]{:S(2)}) async-start(bf16[2,32,18]{2,0,1:T(2,128)(2,1)} %copy.58), calls=%async_computation | async-start | bytes 32768 | tf_op jit(solution)/shard_map/all_to_all | solution.py:43
  85.5 156.2 %all-to-all-start.1 = ((bf16[2,32,18,2048]{3,0,2,1:T(2,128)(2,1)}), bf16[2,32,18,2048]{3,0,2,1:T(2,128)(2,1)}, u32[]{:S(2)}, u32[]{:S(2)}) async-start(bf16[2,32,18,2048]{3,0,2,1:T(2,128)(2,1)} %copy.61), calls=%async_computation.1 | async-start | bytes 9437184 | tf_op jit(solution)/shard_map/all_to_all | solution.py:36
  97.8 183.7 %all-gather.5.cloned.1.call-start = ((), (), s32[]{:S(2)}) async-start(), calls=%async_computation.5 | async-start | bytes 1671168 | tf_op jit(solution)/shard_map/all_gather | solution.py:53
  98.5 287.4 %all-gather.3.cloned.1.call-start = ((), (), s32[]{:S(2)}) async-start(), calls=%async_computation.4 | async-start | bytes 1671168 | tf_op jit(solution)/shard_map/all_gather | solution.py:54
  248.9 137.1 %copy-start.2 = (bf16[2,576,1024]{2,0,1:T(2,128)(2,1)}, bf16[2,576,1024]{2,0,1:T(2,128)(2,1)S(1)}, u32[]{:S(2)}) copy-start(bf16[2,576,1024]{2,0,1:T(2,128)(2,1)S(1)} %get-tuple-element.20) | copy-start | bytes 7077892
  385.9 3.9 copy-start.4
  395.2 72.3 %all-to-all-start.2 = ((bf16[2,32,18,1024]{3,0,2,1:T(2,128)(2,1)}), bf16[2,32,18,1024]{3,0,2,1:T(2,128)(2,1)S(1)}, u32[]{:S(2)}, u32[]{:S(2)}) async-start(bf16[2,32,18,1024]{3,0,2,1:T(2,128)(2,1)} %bitcast.5), calls=%async_computation.2 | async-start | bytes 4718592 | tf_op jit(solution)/shard_map/all_to_all | solution.py:68
  467.5 1.4 copy-start
  468.8 249.1 %all-to-all-start.3 = ((bf16[2,32,18,1024]{3,0,2,1:T(2,128)(2,1)}), bf16[2,32,18,1024]{3,0,2,1:T(2,128)(2,1)}, u32[]{:S(2)}, u32[]{:S(2)}) async-start(bf16[2,32,18,1024]{3,0,2,1:T(2,128)(2,1)} %bitcast.7), calls=%async_computation.3 | async-start | bytes 4718592 | tf_op jit(solution)/shard_map/all_to_all | solution.py:71
  487.1 3.5 copy-start.3
  487.1 213.9 %all-reduce.3.cloned.1.call-start = ((), (), s32[]{:S(2)}) async-start(), calls=%async_computation.6 | async-start | bytes 6291456
  487.2 3.4 copy-start.8
  498.6 204.8 %copy-start.1 = (bf16[2,32,18,1024]{3,0,2,1:T(2,128)(2,1)S(1)}, bf16[2,32,18,1024]{3,0,2,1:T(2,128)(2,1)}, u32[]{:S(2)}) copy-start(bf16[2,32,18,1024]{3,0,2,1:T(2,128)(2,1)} %copy-done) | copy-start | bytes 7077892
Sparse Core Ops, SparseCore 0:
  100.7 180.7 all-gather.4
  283.6 102.3 all-gather.2
  498.8 202.2 all-reduce.2
where the time goes:
time: 746 us; the launch traced here: 741 us
  waiting for transfers between devices  528 us (71%)
  local copies, waits for them, and re-layouts  88.7 us (12%)
  starting transfers between devices  58.8 us (8%)
  other arithmetic  28.3 us (4%)
  matrix products  21.4 us (3%)
  between operations  14.9 us (2%)
    unnamed x4, waiting for transfers between devices  202 us
    all_to_all x1, waiting for transfers between devices, per_device(): lax.all_to_all(send_pair.reshape(exp_local, ctx_count, capacity, 2 * widt...  142 us
    all_gather x1, waiting for transfers between devices, per_device(): lax.all_gather(w_down, 'dp', axis=2, tiled=True)  99.7 us
    all_to_all x1, waiting for transfers between devices, per_device(): lax.all_to_all(grad_rows.reshape(block_shape), 'ctx', split_axis=1, conca...  52.4 us
    all_gather x1, waiting for transfers between devices, per_device(): lax.all_gather(w_up, 'dp', axis=1, tiled=True)  32.6 us
    all_to_all x1, starting transfers between devices, per_device(): lax.all_to_all(outputs.reshape(block_shape), 'ctx', split_axis=1, concat_...  18.3 us
    another operation x3, other arithmetic  18.2 us
    all_to_all x1, starting transfers between devices, per_device(): lax.all_to_all(send_gate.reshape(slot_shape), 'ctx', split_axis=1, concat...  15.4 us
  transfers between devices with their start and end apart: 7, of which 5 were waited for; matrix products, arithmetic and copies ran while one was open for 11% of the time, Pallas kernels for 0%

commit v1 on v0

v1 whole, which is shorter than its diff:
```python
import functools

import jax
import jax.numpy as jnp
from jax import lax
from jax.experimental import pallas as pl
from jax.experimental.pallas import tpu as pltpu
from jax.sharding import Mesh, PartitionSpec as P

BF, F32 = jnp.bfloat16, jnp.float32
HALF = 64
SLOTS = 40


def params(mebibytes):
    return pltpu.CompilerParams(vmem_limit_bytes=mebibytes * 1024 * 1024)


def vmem(count):
    return [pl.BlockSpec(memory_space=pltpu.VMEM)] * count


def dot(a, b, ca=1, cb=0):
    return lax.dot_general(a, b, (((ca,), (cb,)), ((), ())), preferred_element_type=F32)


def iota(shape, dim):
    return lax.broadcasted_iota(jnp.int32, shape, dim)


def prepare_kernel(tok, gout, gates, ids, pay, table):
    rows, width = tok.shape
    lane = iota((rows, 128), 1)
    expert = jnp.where(lane < HALF, lane, lane - HALF)
    gate = gates[...].astype(F32)
    chosen = ids[...]
    gate_of = jnp.zeros((rows, 128), F32)
    named = jnp.zeros((rows, 128), F32)
    for k in range(ids.shape[1]):
        hit = chosen[:, k : k + 1] == expert
        gate_of = gate_of + jnp.where(hit, gate[:, k : k + 1], 0.0)
        named = named + jnp.where(hit, 1.0, 0.0)
    before = jnp.where(iota((rows, rows), 0) > iota((rows, rows), 1), 1.0, 0.0).astype(BF)
    place = named * (dot(before, named.astype(BF)) + 1.0)
    both = jnp.where(lane < HALF, gate_of, place)
    table[...] = both
    pay[:, :width] = tok[...]
    pay[:, width : 2 * width] = gout[...]
    pay[:, 2 * width :] = both.T.astype(BF)


def pick_kernel(cap, gath, sel, place, origin, own, sib):
    n_z, rows, lanes = gath.shape
    width = lanes - 128
    block = n_z * cap
    gates = gath[:, :HALF, width:].reshape(n_z * HALF, 128)
    places = gath[:, HALF:, width:].reshape(n_z * HALF, 128)
    for b in range(4):
        out = own if b < 2 else sib
        part = slice(b * block, (b + 1) * block)
        hit = dot(sel[part], places) == place[...]
        gate = jnp.sum(jnp.where(hit, dot(sel[part], gates), 0.0), axis=1, keepdims=True)
        ones = jnp.where(hit, 1.0, 0.0)
        pick = jnp.concatenate(
            [jnp.where(origin[...] == s, ones, 0.0).astype(BF) for s in range(n_z)], axis=1
        )
        step = min(width, 512)
        for c in range(0, width, step):
            data = gath[:, :, c : c + step].reshape(n_z * rows, step)
            out[b % 2, :, c : c + step] = dot(pick, data).astype(BF)
        out[b % 2, :, width:] = jnp.broadcast_to(gate, (block, 128)).astype(BF)


def expert_kernel(n_y, n_x, cap, spot, *refs):
    w_in = refs[:n_x]
    rows_in = refs[n_x : n_x + 4]
    perm_l, perm_r, perm_s, lane_of = refs[n_x + 4 : n_x + 8]
    g_out = refs[n_x + 8 : 2 * n_x + 8]
    back = refs[2 * n_x + 8]
    weights, parts, grads, marks = refs[2 * n_x + 9 :]
    at_y, at_x, at_b = spot[0], spot[1], spot[2]
    share = w_in[0].shape[2]
    width, hidden_len = weights.shape[1:]
    block = rows_in[0].shape[1]
    n_z = block // cap

    def spot_of(i, d):
        return lax.rem(at_y + i, n_y) * n_x + lax.rem(at_x + d, n_x)

    for i in range(n_y):
        for d in range(n_x):
            start = pl.multiple_of(spot_of(n_y - i, n_x - d) * share, share)
            for m in range(4):
                weights[m, pl.ds(start, share), :] = w_in[d][i, m]
    for e in range(2):
        up, down = weights[e], weights[2 + e]
        x = jnp.concatenate([r[e, :, :width] for r in rows_in], axis=0)
        g = jnp.concatenate([r[e, :, width : 2 * width] for r in rows_in], axis=0)
        gate = jnp.concatenate([r[e, :, 2 * width :] for r in rows_in], axis=0).astype(F32)[:, :1]
        pre = dot(x, up)
        q = dot(g, down)
        s = jax.nn.sigmoid(pre)
        hidden = pre * s
        score = jnp.sum(hidden.astype(BF).astype(F32) * q, axis=1, keepdims=True)
        grad_a = (gate * q * (s * (1.0 + pre * (1.0 - s)))).astype(BF)
        parts[:, e] = dot(x, grad_a, 0, 0).astype(BF).reshape(n_y * n_x, share, hidden_len)
        parts[:, 2 + e] = dot(g, (gate * hidden).astype(BF), 0, 0).astype(BF).reshape(
            n_y * n_x, share, hidden_len
        )
        rows = dot(grad_a, up, 1, 1).astype(BF)
        for b in range(4):
            part = slice(b * block, (b + 1) * block)
            to = slice(e * block, (e + 1) * block)
            grads[b, to] = rows[part]
            marks[b, to] = (score[part] * lane_of[to]).astype(BF)
    for d in range(n_x):
        for i in range(n_y):
            g_out[d][i] = parts[spot_of(i, d)]
    half = width // 2
    for b in range(4):
        left = dot(perm_l[...], grads[b, :, :half]) + dot(perm_r[...], grads[b, :, half:])
        first = left[:, :128] + dot(perm_s[...], marks[b])
        at = lax.bitwise_xor(at_b, b)
        back[:, at, :, :128] = first.astype(BF).reshape(n_z, 2 * SLOTS, 128)
        back[:, at, :, 128:] = left[:, 128:].astype(BF).reshape(n_z, 2 * SLOTS, half - 128)


def combine_kernel(cap, got, table, ids, sel, place_l, place_r, grad_tok, grad_gate):
    n_dev, _, half = got.shape
    rows = table.shape[0]
    places = table[...].astype(BF)
    at = dot(places, sel[...])
    data = got[...].reshape(n_dev * 2 * SLOTS, half)
    grad_tok[:, :half] = dot((at == place_l[...]).astype(F32).astype(BF), data).astype(BF)
    grad_tok[:, half:] = dot((at == place_r[...]).astype(F32).astype(BF), data).astype(BF)
    scores = got[:, 32:48, :128].reshape(n_dev * 16, 128)
    lane = iota((rows, 128), 1)
    column = iota((rows, n_dev * 16), 1)
    column_out = iota((rows, ids.shape[1]), 1)
    chosen = ids[...]
    total = jnp.zeros((rows, ids.shape[1]), F32)
    for k in range(ids.shape[1]):
        e = chosen[:, k : k + 1]
        rank = jnp.sum(jnp.where(lane == e + HALF, table[...], 0.0), axis=1, keepdims=True) - 1.0
        owner = lax.shift_right_logical(e, 1)
        slot = rank.astype(jnp.int32) + (e & 1) * cap
        line = dot(jnp.where(column == owner * 16 + 4, 1.0, 0.0).astype(BF), scores)
        score = jnp.sum(jnp.where(lane == slot, line, 0.0), axis=1, keepdims=True)
        total = total + jnp.where(column_out == k, score, 0.0)
    grad_gate[...] = total.astype(BF)


def shift(value, axis, by):
    n = lax.axis_size(axis)
    return lax.ppermute(value, axis, [(i, (i + by) % n) for i in range(n)])


def per_device(tokens, grad_out, gates, expert_ids, w_up, w_down):
    rows, width = tokens.shape
    top = expert_ids.shape[1]
    n_y, n_x, n_z = lax.axis_size("yl"), lax.axis_size("x"), lax.axis_size("z")
    n_dev = 4 * n_z
    experts = 2 * n_dev
    cap = rows * top * 9 // (8 * experts)
    block = n_z * cap
    share, hidden_len = w_up.shape[1:]
    half = width // 2
    yl, x, z, yh, c = [lax.axis_index(a) for a in ("yl", "x", "z", "yh", "c")]
    shape = jax.ShapeDtypeStruct

    pay, table = pl.pallas_call(
        prepare_kernel,
        out_shape=(shape((rows, 2 * width + 128), BF), shape((rows, 128), F32)),
        in_specs=vmem(4),
        out_specs=tuple(vmem(2)),
        compiler_params=params(8),
    )(tokens, grad_out, gates, expert_ids)
    pay_other = shift(pay, "yh", 1)
    w_mine = jnp.concatenate((w_up, jnp.transpose(w_down, (0, 2, 1))), axis=0)
    w_line = jnp.stack([w_mine] + [shift(w_mine, "yl", d) for d in range(1, n_y)])
    gath_own = lax.all_gather(pay, "z", axis=0)
    gath_other = lax.all_gather(pay_other, "z", axis=0)
    gath_own, w_line = lax.optimization_barrier((gath_own, w_line))
    w_all = [w_line] + [shift(w_line, "x", d) for d in range(1, n_x)]
    gath_other, *w_all = lax.optimization_barrier((gath_other, *w_all))

    j = jnp.arange(4 * block)
    b_j, z_j, r_j = j // block, (j % block) // cap, j % cap
    core_j = jnp.where(b_j >= 2, 1 - c, c)
    e_j = ((z * 2 + yh) * 2 + core_j) * 2 + b_j % 2
    sel = ((z_j * HALF + e_j)[:, None] == jnp.arange(n_z * HALF)[None, :]).astype(BF)
    place = jnp.broadcast_to((r_j[:block, None] + 1).astype(F32), (block, 128))
    origin = jnp.broadcast_to(z_j[:block, None].astype(jnp.int32), (block, 128))

    def picked(gath):
        return pl.pallas_call(
            functools.partial(pick_kernel, cap),
            out_shape=(shape((2, block, 2 * width + 128), BF),) * 2,
            in_specs=vmem(4),
            out_specs=tuple(vmem(2)),
            compiler_params=params(20),
        )(gath, sel, place, origin)

    a_own, a_sib = picked(gath_own)
    a_got = shift(a_sib, "c", 1)
    b_own, b_sib = picked(gath_other)
    b_got = shift(b_sib, "c", 1)

    i = jnp.arange(2 * block)
    e_i, z_i, r_i = i // block, (i % block) // cap, i % cap
    p = jnp.arange(n_z * 2 * SLOTS)
    z_p, q_p = p // (2 * SLOTS), p % (2 * SLOTS)
    same = z_p[:, None] == z_i[None, :]
    slot_i = (e_i * cap + r_i)[None, :]
    perm_l = (same & (q_p[:, None] == slot_i)).astype(BF)
    perm_r = (same & (q_p[:, None] == slot_i + SLOTS)).astype(BF)
    perm_s = (same & (q_p[:, None] == 2 * cap)).astype(BF)
    lane_of = (slot_i.T == jnp.arange(128)[None, :]).astype(F32)
    spot = jnp.stack([yl, x, yh * 2 + c]).astype(jnp.int32)
    outs = pl.pallas_call(
        functools.partial(expert_kernel, n_y, n_x, cap),
        out_shape=(shape((n_y, 4, share, hidden_len), BF),) * n_x
        + (shape((n_z, 4, 2 * SLOTS, half), BF),),
        in_specs=[pl.BlockSpec(memory_space=pltpu.SMEM)] + vmem(n_x + 8),
        out_specs=tuple(vmem(n_x + 1)),
        scratch_shapes=[
            pltpu.VMEM((4, width, hidden_len), BF),
            pltpu.VMEM((n_y * n_x, 4, share, hidden_len), BF),
            pltpu.VMEM((4, 2 * block, width), BF),
            pltpu.VMEM((4, 2 * block, 128), BF),
        ],
        compiler_params=params(36),
    )(spot, *w_all, a_own, a_got, b_own, b_got, perm_l, perm_r, perm_s, lane_of)
    parts, back = outs[:n_x], outs[n_x]
    got = lax.all_to_all(
        back.reshape(n_dev, 2 * SLOTS, half), ("z", "yh", "c"), 0, 0, tiled=True
    )

    lines = [parts[0]] + [shift(parts[d], "x", d) for d in range(1, n_x)]
    line = sum(v.astype(F32) for v in lines).astype(BF)
    ends = [line[0]] + [shift(line[d], "yl", d) for d in range(1, n_y)]
    summed = sum(v.astype(F32) for v in ends).astype(BF)
    grad_up = summed[:2]
    grad_down = jnp.transpose(summed[2:], (0, 2, 1))

    dev_p, s_p = jnp.arange(n_dev * 2 * SLOTS) // (2 * SLOTS), jnp.arange(n_dev * 2 * SLOTS) % (2 * SLOTS)
    q = s_p % SLOTS
    sel_c = (jnp.arange(128)[:, None] == (HALF + dev_p * 2 + (q >= cap))[None, :]).astype(BF)
    tgt = jnp.where(q < 2 * cap, q % cap + 1, -1)
    place_l = jnp.where(s_p < SLOTS, tgt, -1).astype(F32)[None, :]
    place_r = jnp.where(s_p >= SLOTS, tgt, -1).astype(F32)[None, :]
    grad_tokens, grad_gates = pl.pallas_call(
        functools.partial(combine_kernel, cap),
        out_shape=(shape((rows, width), BF), shape((rows, top), BF)),
        in_specs=vmem(6),
        out_specs=tuple(vmem(2)),
        compiler_params=params(14),
    )(got, table, expert_ids, sel_c, place_l, place_r)
    return (grad_tokens, grad_gates, grad_up, grad_down)


def build(mesh):
    every, dp, ctx = ("yl", "x", "z", "yh", "c"), ("yl", "x"), ("z", "yh", "c")
    tok, up, down = P(every, None), P(ctx, dp, None), P(ctx, None, dp)
    return jax.shard_map(
        per_device,
        mesh=mesh,
        in_specs=(tok, tok, tok, tok, up, down),
        out_specs=(tok, tok, up, down),
        check_vma=False,
    )


def solution(mesh):
    return build(Mesh(mesh.devices.reshape(4, 4, 8, 2, 2), ("yl", "x", "z", "yh", "c")))
```

time: 746 us -> 274 us (0.37)
  the two profiles are of different devices: /device:TPU:64 before, /device:TPU:299 now
where the time goes in v1:
time: 274 us; the launch traced here: 273 us
  waiting for transfers between devices  157 us (57%)
  starting transfers between devices  57.8 us (21%)
  Pallas kernels  26.3 us (10%)
  local copies, waits for them, and re-layouts  14.7 us (5%)
  between operations  14.4 us (5%)
  other arithmetic  3.16 us (1%)
    ppermute x15, waiting for transfers between devices, shift(): return lax.ppermute(value, axis, [(i, (i + by) % n) for i in range(n)])  110 us
    ppermute x15, starting transfers between devices, shift(): return lax.ppermute(value, axis, [(i, (i + by) % n) for i in range(n)])  45.6 us
    all_gather x1, waiting for transfers between devices, per_device(): gath_other = lax.all_gather(pay_other, 'z', axis=0)  40.8 us
    pallas_call x1, Pallas kernels, per_device(): pl.pallas_call(functools.partial(expert_kernel, n_y, n_x, cap), out_shape...  14.2 us
    unnamed x33, local copies, waits for them, and re-layouts  13.8 us
    all_to_all x1, starting transfers between devices, per_device(): lax.all_to_all(back.reshape(n_dev, 2 * SLOTS, half), ('z', 'yh', 'c'), 0,...  12.2 us
    pallas_call x2, Pallas kernels, picked(): pl.pallas_call(functools.partial(pick_kernel, cap), out_shape=(shape((2,...  8.62 us
    all_gather x1, waiting for transfers between devices, per_device(): gath_own = lax.all_gather(pay, 'z', axis=0)  6 us
  transfers between devices with their start and end apart: 18, of which 11 were waited for; matrix products, arithmetic and copies ran while one was open for 1% of the time, Pallas kernels for 3%

profile of v1, /device:TPU:299, one launch (start us, length us, event | category | flops | bytes accessed | tf_op | source)
XLA Modules:
  0.0 273.0 jit_solution(2738870731048726024)
XLA Ops:
  7.2 0.8 copy.15.ids
  8.0 0.8 copy.14.gates
  8.8 0.9 copy-done.8
  9.8 0.9 copy-done.9
  10.7 1.3 shard_map.93
  12.1 2.6 collective-permute-start
  14.7 27.7 %collective-permute-done = bf16[128,2176]{1,0:T(8,128)(2,1)S(1)} collective-permute-done((bf16[128,2176]{1,0:T(8,128)(2,1)}, bf16[128,2176]{1,0:T(8,128)(2,1)S(1)}, u32[]{:S(2)}, u32[]{:S(2)}) %collective-permute-start) | collective-permute-done | bytes 557088 | tf_op jit(solution)/shard_map/ppermute | solution.py:155
  42.5 0.8 copy-done.12
  43.4 3.2 %collective-permute-start.1 = (bf16[4,64,384]{2,1,0:T(8,128)(2,1)S(1)}, bf16[4,64,384]{2,1,0:T(8,128)(2,1)S(1)}, u32[]{:S(2)}, u32[]{:S(2)}) collective-permute-start(bf16[4,64,384]{2,1,0:T(8,128)(2,1)S(1)} %get-tuple-element.58), channel_id=1, source_target_pairs={{0,128},{128,256},{256,384},{384,0},{1,129},{129,257},{257,385},{3... | collective-permute-start | bytes 589832 | tf_op jit(solution)/shard_map/ppermute | solution.py:155
  46.6 2.7 collective-permute-start.2
  49.3 3.4 %collective-permute-start.3 = (bf16[4,64,384]{2,1,0:T(8,128)(2,1)S(1)}, bf16[4,64,384]{2,1,0:T(8,128)(2,1)S(1)}, u32[]{:S(2)}, u32[]{:S(2)}) collective-permute-start(bf16[4,64,384]{2,1,0:T(8,128)(2,1)S(1)} %get-tuple-element.58), channel_id=1, source_target_pairs={{0,384},{128,0},{256,128},{384,256},{1,385},{129,1},{257,129},{385... | collective-permute-start | bytes 589832 | tf_op jit(solution)/shard_map/ppermute | solution.py:155
  52.6 9.7 %collective-permute-done.2 = bf16[4,64,384]{2,1,0:T(8,128)(2,1)S(1)} collective-permute-done((bf16[4,64,384]{2,1,0:T(8,128)(2,1)S(1)}, bf16[4,64,384]{2,1,0:T(8,128)(2,1)S(1)}, u32[]{:S(2)}, u32[]{:S(2)}) %collective-permute-start.2) | collective-permute-done | bytes 196640 | tf_op jit(solution)/shard_map/ppermute | solution.py:155
  62.3 2.5 collective-permute-done.3
  65.0 6.0 %all-gather.7.cloned.1.call-done = bf16[1024,2176]{1,0:T(8,128)(2,1)} async-done(((bf16[128,2176]{1,0:T(8,128)(2,1)}), bf16[1024,2176]{1,0:T(8,128)(2,1)}) %all-gather.7.cloned.1.call-update) | async-done | bytes 4456464 | tf_op jit(solution)/shard_map/all_gather | solution.py:181
  71.0 3.1 %collective-permute-start.4 = (bf16[4,4,64,384]{3,2,1,0:T(8,128)(2,1)S(1)}, bf16[4,4,64,384]{3,2,1,0:T(8,128)(2,1)S(1)}, u32[]{:S(2)}, u32[]{:S(2)}) collective-permute-start(bf16[4,4,64,384]{3,2,1,0:T(8,128)(2,1)S(1)} %pad_maximum_fusion.refs_0_), channel_id=1, source_target_pairs={{0,32},{32,64},{64,96},{96,0},{1,33},{33,65},{65,97},{97,1},{2,34}... | collective-permute-start | bytes 2359304 | tf_op jit(solution)/shard_map/ppermute | solution.py:155
  74.0 2.8 %collective-permute-start.5 = (bf16[4,4,64,384]{3,2,1,0:T(8,128)(2,1)S(1)}, bf16[4,4,64,384]{3,2,1,0:T(8,128)(2,1)}, u32[]{:S(2)}, u32[]{:S(2)}) collective-permute-start(bf16[4,4,64,384]{3,2,1,0:T(8,128)(2,1)S(1)} %pad_maximum_fusion.refs_0_), channel_id=1, source_target_pairs={{0,64},{32,96},{64,0},{96,32},{1,65},{33,97},{65,1},{97,33},{2,66}... | collective-permute-start | bytes 2359304 | tf_op jit(solution)/shard_map/ppermute | solution.py:155
  76.8 3.7 %collective-permute-start.6 = (bf16[4,4,64,384]{3,2,1,0:T(8,128)(2,1)S(1)}, bf16[4,4,64,384]{3,2,1,0:T(8,128)(2,1)}, u32[]{:S(2)}, u32[]{:S(2)}) collective-permute-start(bf16[4,4,64,384]{3,2,1,0:T(8,128)(2,1)S(1)} %pad_maximum_fusion.refs_0_), channel_id=1, source_target_pairs={{0,96},{32,0},{64,32},{96,64},{1,97},{33,1},{65,33},{97,65},{2,98}... | collective-permute-start | bytes 2359304 | tf_op jit(solution)/shard_map/ppermute | solution.py:155
  80.7 0.2 fusion.1.sel
  81.0 2.3 copy-done.1
  83.3 4.3 %shard_map.94 = (bf16[2,144,2176]{2,1,0:T(8,128)(2,1)S(1)}, bf16[2,144,2176]{2,1,0:T(8,128)(2,1)}) custom-call(bf16[8,128,2176]{2,1,0:T(8,128)(2,1)S(1)} %bitcast.26, bf16[576,512]{1,0:T(8,128)(2,1)S(1)} %fusion.1.sel, f32[144,128]{1,0:T(8,128)S(1)} %broadcast_in_dim.21.place, s32[144,128]{1,0:T(8,128)S(1)} %broadcast_in_dim.22.origin), custom_call_target="tpu_custom_call" | custom-call | tf_op jit(solution)/shard_map/pallas_call | solution.py:196
  87.6 3.4 %collective-permute-start.7 = (bf16[2,144,2176]{2,1,0:T(8,128)(2,1)}, bf16[2,144,2176]{2,1,0:T(8,128)(2,1)}, u32[]{:S(2)}, u32[]{:S(2)}) collective-permute-start(bf16[2,144,2176]{2,1,0:T(8,128)(2,1)} %get-tuple-element.32), channel_id=1, source_target_pairs={{0,1},{1,0},{2,3},{3,2},{4,5},{5,4},{6,7},{7,6},{8,9},{9,8},{10,11... | collective-permute-start | bytes 3760136 | tf_op jit(solution)/shard_map/ppermute | solution.py:155
  91.0 40.8 %all-gather.5.cloned.1.call-done = bf16[1024,2176]{1,0:T(8,128)(2,1)} async-done(((bf16[128,2176]{1,0:T(8,128)(2,1)}), bf16[1024,2176]{1,0:T(8,128)(2,1)}) %all-gather.5.cloned.1.call-update) | async-done | bytes 4456464 | tf_op jit(solution)/shard_map/all_gather | solution.py:182
  131.9 2.3 copy-done
  134.1 0.9 copy-done.7
  135.0 4.3 %shard_map.95 = (bf16[2,144,2176]{2,1,0:T(8,128)(2,1)S(1)}, bf16[2,144,2176]{2,1,0:T(8,128)(2,1)}) custom-call(bf16[8,128,2176]{2,1,0:T(8,128)(2,1)S(1)} %bitcast.25, bf16[576,512]{1,0:T(8,128)(2,1)S(1)} %fusion.1.sel, f32[144,128]{1,0:T(8,128)S(1)} %broadcast_in_dim.21.place, s32[144,128]{1,0:T(8,128)S(1)} %copy-done.7), custom_call_target="tpu_custom_call" | custom-call | tf_op jit(solution)/shard_map/pallas_call | solution.py:196
  139.3 1.1 copy-done.3
  140.3 2.8 %collective-permute-start.8 = (bf16[2,144,2176]{2,1,0:T(8,128)(2,1)}, bf16[2,144,2176]{2,1,0:T(8,128)(2,1)}, u32[]{:S(2)}, u32[]{:S(2)}) collective-permute-start(bf16[2,144,2176]{2,1,0:T(8,128)(2,1)} %get-tuple-element.35), channel_id=1, source_target_pairs={{0,1},{1,0},{2,3},{3,2},{4,5},{5,4},{6,7},{7,6},{8,9},{9,8},{10,11... | collective-permute-start | bytes 3760136 | tf_op jit(solution)/shard_map/ppermute | solution.py:155
  143.4 0.5 fusion.3
  143.9 1.9 collective-permute-done.8.refs_7_
  145.8 14.2 %shard_map.96 = (bf16[4,4,64,384]{3,2,1,0:T(8,128)(2,1)S(1)}, bf16[4,4,64,384]{3,2,1,0:T(8,128)(2,1)}, bf16[4,4,64,384]{3,2,1,0:T(8,128)(2,1)}, bf16[4,4,64,384]...) custom-call(s32[3]{0:T(128)S(1)} %pad_add_fusion.spot, bf16[4,4,64,384]{3,2,1,0:T(8,128)(2,1)S(1)} %pad_maximum_fusion.refs_0_, ...), custom_call_target="tpu_custom_call" | custom-call | tf_op jit(solution)/shard_map/pallas_call | solution.py:220
  160.0 1.5 copy-done.2
  161.5 0.9 copy-done.5
  162.4 12.2 %all-to-all-start = ((bf16[32,80,512]{2,1,0:T(8,128)(2,1)}), bf16[32,80,512]{2,1,0:T(8,128)(2,1)S(1)}, u32[]{:S(2)}, u32[]{:S(2)}) async-start(bf16[32,80,512]{2,1,0:T(8,128)(2,1)} %bitcast.27), calls=%async_computation | async-start | bytes 5242880 | tf_op jit(solution)/shard_map/all_to_all | solution.py:235
  174.6 3.7 %collective-permute-start.10 = (bf16[4,4,64,384]{3,2,1,0:T(8,128)(2,1)}, bf16[4,4,64,384]{3,2,1,0:T(8,128)(2,1)S(1)}, u32[]{:S(2)}, u32[]{:S(2)}) collective-permute-start(bf16[4,4,64,384]{3,2,1,0:T(8,128)(2,1)} %get-tuple-element.42), channel_id=1, source_target_pairs={{0,64},{32,96},{64,0},{96,32},{1,65},{33,97},{65,1},{97,33},{2,66}... | collective-permute-start | bytes 2359304 | tf_op jit(solution)/shard_map/ppermute | solution.py:155
  178.3 3.1 %collective-permute-start.11 = (bf16[4,4,64,384]{3,2,1,0:T(8,128)(2,1)}, bf16[4,4,64,384]{3,2,1,0:T(8,128)(2,1)S(1)}, u32[]{:S(2)}, u32[]{:S(2)}) collective-permute-start(bf16[4,4,64,384]{3,2,1,0:T(8,128)(2,1)} %get-tuple-element.43), channel_id=1, source_target_pairs={{0,96},{32,0},{64,32},{96,64},{1,97},{33,1},{65,33},{97,65},{2,98}... | collective-permute-start | bytes 2359304 | tf_op jit(solution)/shard_map/ppermute | solution.py:155
  181.4 2.2 collective-permute-start.9
  183.8 13.3 %collective-permute-done.10 = bf16[4,4,64,384]{3,2,1,0:T(8,128)(2,1)S(1)} collective-permute-done((bf16[4,4,64,384]{3,2,1,0:T(8,128)(2,1)}, bf16[4,4,64,384]{3,2,1,0:T(8,128)(2,1)S(1)}, u32[]{:S(2)}, u32[]{:S(2)}) %collective-permute-start.10) | collective-permute-done | bytes 786464 | tf_op jit(solution)/shard_map/ppermute | solution.py:155
  197.0 17.5 %collective-permute-done.11 = bf16[4,4,64,384]{3,2,1,0:T(8,128)(2,1)S(1)} collective-permute-done((bf16[4,4,64,384]{3,2,1,0:T(8,128)(2,1)}, bf16[4,4,64,384]{3,2,1,0:T(8,128)(2,1)S(1)}, u32[]{:S(2)}, u32[]{:S(2)}) %collective-permute-start.11) | collective-permute-done | bytes 786464 | tf_op jit(solution)/shard_map/ppermute | solution.py:155
  214.5 1.6 add_convert_fusion
  216.3 2.2 collective-permute-start.12
  218.5 4.9 %collective-permute-start.13 = (bf16[4,64,384]{2,1,0:T(8,128)(2,1)S(1)}, bf16[4,64,384]{2,1,0:T(8,128)(2,1)S(1)}, u32[]{:S(2)}, u32[]{:S(2)}) collective-permute-start(bf16[4,64,384]{2,1,0:T(8,128)(2,1)S(1)} %get-tuple-element.54), channel_id=1, source_target_pairs={{0,256},{128,384},{256,0},{384,128},{1,257},{129,385},{257,1},{385... | collective-permute-start | bytes 589832 | tf_op jit(solution)/shard_map/ppermute | solution.py:155
  223.3 1.9 collective-permute-start.14
  225.4 11.8 %collective-permute-done.12 = bf16[4,64,384]{2,1,0:T(8,128)(2,1)S(1)} collective-permute-done((bf16[4,64,384]{2,1,0:T(8,128)(2,1)S(1)}, bf16[4,64,384]{2,1,0:T(8,128)(2,1)S(1)}, u32[]{:S(2)}, u32[]{:S(2)}) %collective-permute-start.12) | collective-permute-done | bytes 196640 | tf_op jit(solution)/shard_map/ppermute | solution.py:155
  237.2 19.5 %collective-permute-done.13 = bf16[4,64,384]{2,1,0:T(8,128)(2,1)S(1)} collective-permute-done((bf16[4,64,384]{2,1,0:T(8,128)(2,1)S(1)}, bf16[4,64,384]{2,1,0:T(8,128)(2,1)S(1)}, u32[]{:S(2)}, u32[]{:S(2)}) %collective-permute-start.13) | collective-permute-done | bytes 196640 | tf_op jit(solution)/shard_map/ppermute | solution.py:155
  256.8 5.7 %collective-permute-done.14 = bf16[4,64,384]{2,1,0:T(8,128)(2,1)S(1)} collective-permute-done((bf16[4,64,384]{2,1,0:T(8,128)(2,1)S(1)}, bf16[4,64,384]{2,1,0:T(8,128)(2,1)S(1)}, u32[]{:S(2)}, u32[]{:S(2)}) %collective-permute-start.14) | collective-permute-done | bytes 196640 | tf_op jit(solution)/shard_map/ppermute | solution.py:155
  262.6 0.7 slice_bitcast_fusion.4
  263.3 2.2 shard_map.97
  265.5 0.7 copy.18
  (52 shorter events, 1.2 us)
Async XLA Ops:
  7.2 36.1 %copy-start.13 = (bf16[2,384,64]{1,2,0:T(8,128)(2,1)S(1)}, bf16[2,384,64]{1,2,0:T(8,128)(2,1)}, u32[]{:S(2)}) copy-start(bf16[2,384,64]{1,2,0:T(8,128)(2,1)} %param.11) | copy-start | bytes 294916
  7.2 63.8 %all-gather.7.cloned.1.call-start = ((), (), s32[]{:S(2)}) async-start(), calls=%async_computation.2 | async-start | bytes 5013504 | tf_op jit(solution)/shard_map/all_gather | solution.py:181
  8.8 1.0 copy-start.8
  9.8 0.9 copy-start.9
  10.7 32.6 %copy-start.14 = (bf16[2,64,384]{2,1,0:T(8,128)(2,1)S(1)}, bf16[2,64,384]{2,1,0:T(8,128)(2,1)}, u32[]{:S(2)}) copy-start(bf16[2,64,384]{2,1,0:T(8,128)(2,1)} %param.10) | copy-start | bytes 294916
  12.0 52.8 %copy-start.10 = (f32[128,128]{1,0:T(8,128)}, f32[128,128]{1,0:T(8,128)S(1)}, u32[]{:S(2)}) copy-start(f32[128,128]{1,0:T(8,128)S(1)} %get-tuple-element.37.table) | copy-start | bytes 196612
  12.1 119.8 %all-gather.5.cloned.1.call-start = ((), (), s32[]{:S(2)}) async-start(), calls=%async_computation.1 | async-start | bytes 5013504 | tf_op jit(solution)/shard_map/all_gather | solution.py:182
  12.1 30.4 %collective-permute-start = (bf16[128,2176]{1,0:T(8,128)(2,1)}, bf16[128,2176]{1,0:T(8,128)(2,1)S(1)}, u32[]{:S(2)}, u32[]{:S(2)}) collective-permute-start(bf16[128,2176]{1,0:T(8,128)(2,1)} %get-tuple-element.24), channel_id=1, source_target_pairs={{0,2},{2,0},{1,3},{3,1},{4,6},{6,4},{5,7},{7,5},{8,10},{10,8},{9,1... | collective-permute-start | bytes 1671176 | tf_op jit(solution)/shard_map/ppermute | solution.py:155
  42.5 0.8 copy-start.12
  43.4 9.3 %collective-permute-start.1 = (bf16[4,64,384]{2,1,0:T(8,128)(2,1)S(1)}, bf16[4,64,384]{2,1,0:T(8,128)(2,1)S(1)}, u32[]{:S(2)}, u32[]{:S(2)}) collective-permute-start(bf16[4,64,384]{2,1,0:T(8,128)(2,1)S(1)} %get-tuple-element.58), channel_id=1, source_target_pairs={{0,128},{128,256},{256,384},{384,0},{1,129},{129,257},{257,385},{3... | collective-permute-start | bytes 589832 | tf_op jit(solution)/shard_map/ppermute | solution.py:155
  46.6 15.8 %collective-permute-start.2 = (bf16[4,64,384]{2,1,0:T(8,128)(2,1)S(1)}, bf16[4,64,384]{2,1,0:T(8,128)(2,1)S(1)}, u32[]{:S(2)}, u32[]{:S(2)}) collective-permute-start(bf16[4,64,384]{2,1,0:T(8,128)(2,1)S(1)} %get-tuple-element.58), channel_id=1, source_target_pairs={{0,256},{128,384},{256,0},{384,128},{1,257},{129,385},{257,1},{385... | collective-permute-start | bytes 589832 | tf_op jit(solution)/shard_map/ppermute | solution.py:155
  49.3 15.6 %collective-permute-start.3 = (bf16[4,64,384]{2,1,0:T(8,128)(2,1)S(1)}, bf16[4,64,384]{2,1,0:T(8,128)(2,1)S(1)}, u32[]{:S(2)}, u32[]{:S(2)}) collective-permute-start(bf16[4,64,384]{2,1,0:T(8,128)(2,1)S(1)} %get-tuple-element.58), channel_id=1, source_target_pairs={{0,384},{128,0},{256,128},{384,256},{1,385},{129,1},{257,129},{385... | collective-permute-start | bytes 589832 | tf_op jit(solution)/shard_map/ppermute | solution.py:155
  71.0 60.9 %collective-permute-start.4 = (bf16[4,4,64,384]{3,2,1,0:T(8,128)(2,1)S(1)}, bf16[4,4,64,384]{3,2,1,0:T(8,128)(2,1)S(1)}, u32[]{:S(2)}, u32[]{:S(2)}) collective-permute-start(bf16[4,4,64,384]{3,2,1,0:T(8,128)(2,1)S(1)} %pad_maximum_fusion.refs_0_), channel_id=1, source_target_pairs={{0,32},{32,64},{64,96},{96,0},{1,33},{33,65},{65,97},{97,1},{2,34}... | collective-permute-start | bytes 2359304 | tf_op jit(solution)/shard_map/ppermute | solution.py:155
  74.0 57.8 %collective-permute-start.5 = (bf16[4,4,64,384]{3,2,1,0:T(8,128)(2,1)S(1)}, bf16[4,4,64,384]{3,2,1,0:T(8,128)(2,1)}, u32[]{:S(2)}, u32[]{:S(2)}) collective-permute-start(bf16[4,4,64,384]{3,2,1,0:T(8,128)(2,1)S(1)} %pad_maximum_fusion.refs_0_), channel_id=1, source_target_pairs={{0,64},{32,96},{64,0},{96,32},{1,65},{33,97},{65,1},{97,33},{2,66}... | collective-permute-start | bytes 2359304 | tf_op jit(solution)/shard_map/ppermute | solution.py:155
  76.8 55.0 %collective-permute-start.6 = (bf16[4,4,64,384]{3,2,1,0:T(8,128)(2,1)S(1)}, bf16[4,4,64,384]{3,2,1,0:T(8,128)(2,1)}, u32[]{:S(2)}, u32[]{:S(2)}) collective-permute-start(bf16[4,4,64,384]{3,2,1,0:T(8,128)(2,1)S(1)} %pad_maximum_fusion.refs_0_), channel_id=1, source_target_pairs={{0,96},{32,0},{64,32},{96,64},{1,97},{33,1},{65,33},{97,65},{2,98}... | collective-permute-start | bytes 2359304 | tf_op jit(solution)/shard_map/ppermute | solution.py:155
  81.0 2.3 copy-start.1
  83.3 4.3 %copy-start.6 = (s32[144,128]{1,0:T(8,128)}, s32[144,128]{1,0:T(8,128)S(1)}, u32[]{:S(2)}) copy-start(s32[144,128]{1,0:T(8,128)S(1)} %broadcast_in_dim.22.origin) | copy-start | bytes 221188
  87.6 56.3 %collective-permute-start.7 = (bf16[2,144,2176]{2,1,0:T(8,128)(2,1)}, bf16[2,144,2176]{2,1,0:T(8,128)(2,1)}, u32[]{:S(2)}, u32[]{:S(2)}) collective-permute-start(bf16[2,144,2176]{2,1,0:T(8,128)(2,1)} %get-tuple-element.32), channel_id=1, source_target_pairs={{0,1},{1,0},{2,3},{3,2},{4,5},{5,4},{6,7},{7,6},{8,9},{9,8},{10,11... | collective-permute-start | bytes 3760136 | tf_op jit(solution)/shard_map/ppermute | solution.py:155
  131.9 2.3 copy-start
  134.1 0.9 copy-start.7
  139.3 1.1 copy-start.3
  140.3 5.5 %collective-permute-start.8 = (bf16[2,144,2176]{2,1,0:T(8,128)(2,1)}, bf16[2,144,2176]{2,1,0:T(8,128)(2,1)}, u32[]{:S(2)}, u32[]{:S(2)}) collective-permute-start(bf16[2,144,2176]{2,1,0:T(8,128)(2,1)} %get-tuple-element.35), channel_id=1, source_target_pairs={{0,1},{1,0},{2,3},{3,2},{4,5},{5,4},{6,7},{7,6},{8,9},{9,8},{10,11... | collective-permute-start | bytes 3760136 | tf_op jit(solution)/shard_map/ppermute | solution.py:155
  143.1 2.7 copy-start.4
  160.0 1.5 copy-start.2
  161.5 0.9 copy-start.5
  162.4 100.9 %all-to-all-start = ((bf16[32,80,512]{2,1,0:T(8,128)(2,1)}), bf16[32,80,512]{2,1,0:T(8,128)(2,1)S(1)}, u32[]{:S(2)}, u32[]{:S(2)}) async-start(bf16[32,80,512]{2,1,0:T(8,128)(2,1)} %bitcast.27), calls=%async_computation | async-start | bytes 5242880 | tf_op jit(solution)/shard_map/all_to_all | solution.py:235
  174.6 22.4 %collective-permute-start.10 = (bf16[4,4,64,384]{3,2,1,0:T(8,128)(2,1)}, bf16[4,4,64,384]{3,2,1,0:T(8,128)(2,1)S(1)}, u32[]{:S(2)}, u32[]{:S(2)}) collective-permute-start(bf16[4,4,64,384]{3,2,1,0:T(8,128)(2,1)} %get-tuple-element.42), channel_id=1, source_target_pairs={{0,64},{32,96},{64,0},{96,32},{1,65},{33,97},{65,1},{97,33},{2,66}... | collective-permute-start | bytes 2359304 | tf_op jit(solution)/shard_map/ppermute | solution.py:155
  178.3 36.2 %collective-permute-start.11 = (bf16[4,4,64,384]{3,2,1,0:T(8,128)(2,1)}, bf16[4,4,64,384]{3,2,1,0:T(8,128)(2,1)S(1)}, u32[]{:S(2)}, u32[]{:S(2)}) collective-permute-start(bf16[4,4,64,384]{3,2,1,0:T(8,128)(2,1)} %get-tuple-element.43), channel_id=1, source_target_pairs={{0,96},{32,0},{64,32},{96,64},{1,97},{33,1},{65,33},{97,65},{2,98}... | collective-permute-start | bytes 2359304 | tf_op jit(solution)/shard_map/ppermute | solution.py:155
  181.4 33.1 %collective-permute-start.9 = (bf16[4,4,64,384]{3,2,1,0:T(8,128)(2,1)}, bf16[4,4,64,384]{3,2,1,0:T(8,128)(2,1)S(1)}, u32[]{:S(2)}, u32[]{:S(2)}) collective-permute-start(bf16[4,4,64,384]{3,2,1,0:T(8,128)(2,1)} %get-tuple-element.41), channel_id=1, source_target_pairs={{0,32},{32,64},{64,96},{96,0},{1,33},{33,65},{65,97},{97,1},{2,34}... | collective-permute-start | bytes 2359304 | tf_op jit(solution)/shard_map/ppermute | solution.py:155
  216.2 47.1 %copy-start.11 = (f32[128,128]{1,0:T(8,128)S(1)}, f32[128,128]{1,0:T(8,128)}, u32[]{:S(2)}) copy-start(f32[128,128]{1,0:T(8,128)} %copy-done.10) | copy-start | bytes 196612
  216.3 21.0 %collective-permute-start.12 = (bf16[4,64,384]{2,1,0:T(8,128)(2,1)S(1)}, bf16[4,64,384]{2,1,0:T(8,128)(2,1)S(1)}, u32[]{:S(2)}, u32[]{:S(2)}) collective-permute-start(bf16[4,64,384]{2,1,0:T(8,128)(2,1)S(1)} %get-tuple-element.52), channel_id=1, source_target_pairs={{0,128},{128,256},{256,384},{384,0},{1,129},{129,257},{257,385},{3... | collective-permute-start | bytes 589832 | tf_op jit(solution)/shard_map/ppermute | solution.py:155
  218.5 38.3 %collective-permute-start.13 = (bf16[4,64,384]{2,1,0:T(8,128)(2,1)S(1)}, bf16[4,64,384]{2,1,0:T(8,128)(2,1)S(1)}, u32[]{:S(2)}, u32[]{:S(2)}) collective-permute-start(bf16[4,64,384]{2,1,0:T(8,128)(2,1)S(1)} %get-tuple-element.54), channel_id=1, source_target_pairs={{0,256},{128,384},{256,0},{384,128},{1,257},{129,385},{257,1},{385... | collective-permute-start | bytes 589832 | tf_op jit(solution)/shard_map/ppermute | solution.py:155
  223.3 39.1 %collective-permute-start.14 = (bf16[4,64,384]{2,1,0:T(8,128)(2,1)S(1)}, bf16[4,64,384]{2,1,0:T(8,128)(2,1)S(1)}, u32[]{:S(2)}, u32[]{:S(2)}) collective-permute-start(bf16[4,64,384]{2,1,0:T(8,128)(2,1)S(1)} %get-tuple-element.53), channel_id=1, source_target_pairs={{0,384},{128,0},{256,128},{384,256},{1,385},{129,1},{257,129},{385... | collective-permute-start | bytes 589832 | tf_op jit(solution)/shard_map/ppermute | solution.py:155
Sparse Core Ops, SparseCore 0:
  12.2 58.7 all-gather.6
  73.0 58.7 all-gather.4

commit v2 on v1

v2 whole, which is shorter than its diff:
```python
import functools

import jax
import jax.numpy as jnp
from jax import lax
from jax.experimental import pallas as pl
from jax.experimental.pallas import tpu as pltpu
from jax.sharding import Mesh, PartitionSpec as P

BF, F32 = jnp.bfloat16, jnp.float32
HALF = 64
SLOTS = 40


def params(mebibytes):
    return pltpu.CompilerParams(vmem_limit_bytes=mebibytes * 1024 * 1024)


def cost(gflop, mebibytes):
    return pl.CostEstimate(
        flops=int(gflop * 1e9), bytes_accessed=int(mebibytes * 2**20), transcendentals=0
    )


def vmem(count):
    return [pl.BlockSpec(memory_space=pltpu.VMEM)] * count


def dot(a, b, ca=1, cb=0):
    return lax.dot_general(a, b, (((ca,), (cb,)), ((), ())), preferred_element_type=F32)


def iota(shape, dim):
    return lax.broadcasted_iota(jnp.int32, shape, dim)


def prepare_kernel(tok, gout, gates, ids, pay, table):
    rows, width = tok.shape
    lane = iota((rows, 128), 1)
    expert = jnp.where(lane < HALF, lane, lane - HALF)
    gate = gates[...].astype(F32)
    chosen = ids[...]
    gate_of = jnp.zeros((rows, 128), F32)
    named = jnp.zeros((rows, 128), F32)
    for k in range(ids.shape[1]):
        hit = chosen[:, k : k + 1] == expert
        gate_of = gate_of + jnp.where(hit, gate[:, k : k + 1], 0.0)
        named = named + jnp.where(hit, 1.0, 0.0)
    before = jnp.where(iota((rows, rows), 0) > iota((rows, rows), 1), 1.0, 0.0).astype(BF)
    place = named * (dot(before, named.astype(BF)) + 1.0)
    both = jnp.where(lane < HALF, gate_of, place)
    table[...] = both
    pay[:, :width] = tok[...]
    pay[:, width : 2 * width] = gout[...]
    pay[:, 2 * width :] = both.T.astype(BF)


def pick_kernel(cap, n_z, *refs):
    blocks = refs[: n_z + 1]
    sel, place, origin = refs[n_z + 1 : n_z + 4]
    own, sib = refs[-2:]
    rows, lanes = blocks[0].shape
    width = lanes - 128
    mid = n_z // 2
    block = n_z * cap
    tops = [b for i, b in enumerate(blocks) if i != mid + 1]
    ends = [b for i, b in enumerate(blocks) if i != mid]
    gates = jnp.concatenate([b[:HALF, width:] for b in tops], axis=0)
    places = jnp.concatenate(
        [b[b.shape[0] - HALF :, width:] for b in ends], axis=0
    )
    hits, gate_cols = [], []
    for b in range(4):
        part = slice(b * block, (b + 1) * block)
        hit = dot(sel[part], places) == place[...]
        gate_cols.append(
            jnp.sum(jnp.where(hit, dot(sel[part], gates), 0.0), axis=1, keepdims=True)
        )
        ones = jnp.where(hit, 1.0, 0.0)
        hits.append(
            jnp.concatenate(
                [jnp.where(origin[...] == s, ones, 0.0).astype(BF) for s in range(n_z)], axis=1
            )
        )
    step = min(width, 512)
    for b in range(4):
        out = own if b < 2 else sib
        for c in range(0, width, step):
            data = jnp.concatenate([r[:, c : c + step] for r in blocks], axis=0)
            out[b % 2, :, c : c + step] = dot(hits[b], data).astype(BF)
        out[b % 2, :, width:] = jnp.broadcast_to(gate_cols[b], (block, 128)).astype(BF)


def expert_kernel(cap, spot, w_ref, own, got, perm_l, perm_r, perm_s, lane_of, back, fac_up, fac_down, grads, marks):
    rows_in = (own, got)
    width = w_ref.shape[1]
    block = own.shape[1]
    n_z = block // cap
    half = width // 2
    for e in range(2):
        up, down = w_ref[e], w_ref[2 + e]
        x = jnp.concatenate([r[e, :, :width] for r in rows_in], axis=0)
        g = jnp.concatenate([r[e, :, width : 2 * width] for r in rows_in], axis=0)
        gate = jnp.concatenate([r[e, :, 2 * width :] for r in rows_in], axis=0).astype(F32)[:, :1]
        pre = dot(x, up)
        q = dot(g, down)
        s = jax.nn.sigmoid(pre)
        hidden = pre * s
        score = jnp.sum(hidden.astype(BF).astype(F32) * q, axis=1, keepdims=True)
        grad_a = (gate * q * (s * (1.0 + pre * (1.0 - s)))).astype(BF)
        fac_up[e] = grad_a
        fac_down[e] = (gate * hidden).astype(BF)
        rows = dot(grad_a, up, 1, 1).astype(BF)
        for b in range(2):
            part = slice(b * block, (b + 1) * block)
            to = slice(e * block, (e + 1) * block)
            grads[b, to] = rows[part]
            marks[b, to] = (score[part] * lane_of[to]).astype(BF)
    for b in range(2):
        left = dot(perm_l[...], grads[b, :, :half]) + dot(perm_r[...], grads[b, :, half:])
        first = left[:, :128] + dot(perm_s[...], marks[b])
        at = lax.bitwise_xor(spot[2], b)
        back[:, at, :, :128] = first.astype(BF).reshape(n_z, 2 * SLOTS, 128)
        back[:, at, :, 128:] = left[:, 128:].astype(BF).reshape(n_z, 2 * SLOTS, half - 128)


def weight_kernel(n_y, n_x, spot, *refs):
    rows_in, fac = refs[:4], refs[4:8]
    g_out, parts = refs[8 : 8 + n_x], refs[8 + n_x]
    share, hidden_len = parts.shape[2:]
    width = parts.shape[0] * share
    for e in range(2):
        for m in range(2):
            x = jnp.concatenate([r[e, :, m * width : (m + 1) * width] for r in rows_in], axis=0)
            f = jnp.concatenate((fac[m][e], fac[2 + m][e]), axis=0)
            parts[:, 2 * m + e] = dot(x, f, 0, 0).astype(BF).reshape(-1, share, hidden_len)
    for d in range(n_x):
        for i in range(n_y):
            g_out[d][i] = parts[lax.rem(spot[0] + i, n_y) * n_x + lax.rem(spot[1] + d, n_x)]


def total_kernel(*refs):
    *ends, up, down = refs
    up[...] = sum(r[:2].astype(F32) for r in ends).astype(BF)
    down[...] = sum(r[2:].astype(F32) for r in ends).astype(BF)


def partial_sums(cap, got, at, lane_places, owners, slots, place_l, place_r):
    n_dev, _, half = got.shape
    data = got[...].reshape(n_dev * 2 * SLOTS, half)
    left = dot((at == place_l[...]).astype(F32).astype(BF), data)
    right = dot((at == place_r[...]).astype(F32).astype(BF), data)
    lines = got[:, 32:48, :128].reshape(n_dev * 16, 128)
    by_place = jnp.zeros((slots.shape[1], 128), F32)
    for m in range(2):
        by_place = by_place + dot(dot(slots[m], lines, 1, 1).astype(BF), owners[m])
    scores = jnp.zeros(lane_places.shape, F32)
    for r in range(cap):
        scores = scores + jnp.where(lane_places == r + 1.0, by_place[r : r + 1, :], 0.0)
    return left, right, scores


def partner_kernel(cap, got, pay, sel, owners, slots, place_l, place_r, out):
    width = out.shape[1] - 128
    half = width // 2
    meta = pay[HALF:, 2 * width :]
    at = dot(meta, sel[...], 0, 0)
    lane = iota((HALF, 128), 0) == iota((HALF, 128), 1)
    lane_places = dot(meta, jnp.where(lane, 1.0, 0.0).astype(BF), 0, 0)
    left, right, scores = partial_sums(cap, got, at, lane_places, owners, slots, place_l, place_r)
    out[:, :half] = left.astype(BF)
    out[:, half:width] = right.astype(BF)
    out[:, width:] = scores.astype(BF)


def combine_kernel(cap, got, table, ids, sel, owners, slots, place_l, place_r, other, grad_tok, grad_gate):
    rows, width = grad_tok.shape
    half = width // 2
    both = table[...]
    at = dot(both.astype(BF), sel[...])
    at_lane = iota((128, 128), 0) == iota((128, 128), 1) + HALF
    lane_places = dot(both.astype(BF), jnp.where(at_lane, 1.0, 0.0).astype(BF))
    left, right, scores = partial_sums(cap, got, at, lane_places, owners, slots, place_l, place_r)
    grad_tok[:, :half] = (left + other[:, :half].astype(F32)).astype(BF)
    grad_tok[:, half:] = (right + other[:, half:width].astype(F32)).astype(BF)
    scores = scores + other[:, width:].astype(F32)
    lane = iota((rows, 128), 1)
    column = iota((rows, ids.shape[1]), 1)
    chosen = ids[...]
    total = jnp.zeros((rows, ids.shape[1]), F32)
    for k in range(ids.shape[1]):
        score = jnp.sum(
            jnp.where(lane == chosen[:, k : k + 1], scores, 0.0), axis=1, keepdims=True
        )
        total = total + jnp.where(column == k, score, 0.0)
    grad_gate[...] = total.astype(BF)


def shift(value, axis, by):
    n = lax.axis_size(axis)
    return lax.ppermute(value, axis, [(i, (i + by) % n) for i in range(n)])


def together(values, after=()):
    anywhere = pl.BlockSpec(memory_space=pl.ANY)
    return pl.pallas_call(
        lambda *refs: None,
        out_shape=tuple(jax.ShapeDtypeStruct(v.shape, v.dtype) for v in values),
        in_specs=[anywhere] * (len(values) + len(after)),
        out_specs=(anywhere,) * len(values),
        input_output_aliases={i: i for i in range(len(values))},
    )(*values, *after)


def rings(block):
    steps = lax.axis_size("z") // 2
    rows = block.shape[0] // 2
    chains = [([block], [block]), ([], [])]

    def advance(chain):
        below, above = chain
        if len(below) < steps:
            below.append(shift(below[-1], "z", 1))
            above.append(shift(above[-1], "z", -1))
        elif len(below) == steps:
            below.append(shift(below[-1][:rows], "z", 1))
            above.append(shift(above[-1][rows:], "z", -1))

    def settle():
        ends = [chain[-1] for pair in chains for chain in pair]
        ends[2:] = ends[2:] if ends[2] is not ends[3] else ends[2:3]
        held = together(ends)
        for n, chain in enumerate(chain for pair in chains for chain in pair):
            chain[-1] = held[min(n, len(held) - 1)]

    partner = shift(block, "yh", 1)
    advance(chains[0])
    advance(chains[0])
    for chain in chains[1]:
        chain.append(partner)
    settle()
    partner = chains[1][0][0]
    while len(chains[0][0]) <= steps:
        advance(chains[0])
        advance(chains[1])
        settle()
    while len(chains[1][0]) <= steps:
        advance(chains[1])
    order = [
        below[:steps] + [below[steps], above[steps]] + above[steps - 1 : 0 : -1]
        for below, above in chains
    ]
    return partner, order[0], order[1]


def per_device(tokens, grad_out, gates, expert_ids, w_up, w_down):
    rows, width = tokens.shape
    top = expert_ids.shape[1]
    n_y, n_x, n_z = lax.axis_size("yl"), lax.axis_size("x"), lax.axis_size("z")
    experts = 8 * n_z
    cap = rows * top * 9 // (8 * experts)
    block = n_z * cap
    share, hidden_len = w_up.shape[1:]
    half = width // 2
    yl, x, z, yh, c = [lax.axis_index(a) for a in ("yl", "x", "z", "yh", "c")]
    shape = jax.ShapeDtypeStruct

    pay, table = pl.pallas_call(
        prepare_kernel,
        out_shape=(shape((rows, 2 * width + 128), BF), shape((rows, 128), F32)),
        in_specs=vmem(4),
        out_specs=tuple(vmem(2)),
        cost_estimate=cost(0.1, 2),
        compiler_params=params(8),
    )(tokens, grad_out, gates, expert_ids)
    pay_other, blocks_own, blocks_other = rings(pay)
    w_mine = jnp.concatenate((w_up, jnp.transpose(w_down, (0, 2, 1))), axis=0)
    w_all = lax.all_gather(w_mine, ("yl", "x"), axis=0)
    w_all = jnp.transpose(w_all, (1, 0, 2, 3)).reshape(4, width, hidden_len)

    j = jnp.arange(4 * block)
    b_j, d_j, r_j = j // block, (j % block) // cap, j % cap
    core_j = jnp.where(b_j >= 2, 1 - c, c)
    e_j = ((z * 2 + yh) * 2 + core_j) * 2 + b_j % 2
    sel = ((d_j * HALF + e_j)[:, None] == jnp.arange(n_z * HALF)[None, :]).astype(BF)
    place = jnp.broadcast_to((r_j[:block, None] + 1).astype(F32), (block, 128))
    origin = jnp.broadcast_to(d_j[:block, None].astype(jnp.int32), (block, 128))

    def picked(blocks, after=()):
        own, sib = pl.pallas_call(
            functools.partial(pick_kernel, cap, n_z),
            out_shape=(shape((2, block, 2 * width + 128), BF),) * 2,
            in_specs=vmem(n_z + 4) + [pl.BlockSpec(memory_space=pl.ANY)] * len(after),
            out_specs=tuple(vmem(2)),
            cost_estimate=cost(2.6, 12),
        compiler_params=params(20),
        )(*blocks, sel, place, origin, *after)
        return own, shift(sib, "c", 1)

    i = jnp.arange(2 * block)
    e_i, d_i, r_i = i // block, (i % block) // cap, i % cap
    z_i = (z + n_z - d_i) % n_z
    p = jnp.arange(n_z * 2 * SLOTS)
    z_p, q_p = p // (2 * SLOTS), p % (2 * SLOTS)
    same = z_p[:, None] == z_i[None, :]
    slot_i = (e_i * cap + r_i)[None, :]
    perm_l = (same & (q_p[:, None] == slot_i)).astype(BF)
    perm_r = (same & (q_p[:, None] == slot_i + SLOTS)).astype(BF)
    perm_s = (same & (q_p[:, None] == 2 * cap)).astype(BF)
    lane_of = (slot_i.T == jnp.arange(128)[None, :]).astype(F32)
    spot = jnp.stack([yl, x, c]).astype(jnp.int32)

    def worked(own, got):
        return pl.pallas_call(
            functools.partial(expert_kernel, cap),
            out_shape=(shape((n_z, 2, 2 * SLOTS, half), BF),)
            + (shape((2, 2 * block, hidden_len), BF),) * 2,
            in_specs=[pl.BlockSpec(memory_space=pltpu.SMEM)] + vmem(7),
            out_specs=tuple(vmem(3)),
            scratch_shapes=[
                pltpu.VMEM((2, 2 * block, width), BF),
                pltpu.VMEM((2, 2 * block, 128), BF),
            ],
            cost_estimate=cost(4, 24),
        compiler_params=params(28),
        )(spot, w_all, own, got, perm_l, perm_r, perm_s, lane_of)

    def replies(back):
        return lax.all_to_all(
            back.reshape(2 * n_z, 2 * SLOTS, half), ("z", "c"), 0, 0, tiled=True
        )

    a_own, a_got = picked(blocks_own)
    a_back, a_up, a_down = worked(a_own, a_got)
    (a_back,) = together((a_back,), (blocks_other[n_z // 2 - 1], blocks_other[n_z // 2 + 2]))
    got_own = replies(a_back)
    b_own, b_got = picked(blocks_other, (a_up,))
    b_back, b_up, b_down = worked(b_own, b_got)
    parts = pl.pallas_call(
        functools.partial(weight_kernel, n_y, n_x),
        out_shape=(shape((n_y, 4, share, hidden_len), BF),) * n_x,
        in_specs=[pl.BlockSpec(memory_space=pltpu.SMEM)] + vmem(8),
        out_specs=tuple(vmem(n_x)),
        scratch_shapes=[pltpu.VMEM((n_y * n_x, 4, share, hidden_len), BF)],
        cost_estimate=cost(2, 18),
        compiler_params=params(28),
    )(spot, a_own, a_got, b_own, b_got, a_up, a_down, b_up, b_down)
    (b_back,) = together((b_back,), (got_own, parts[0]))
    got_other = replies(b_back)

    lines = [parts[0]] + [shift(parts[d], "x", d) for d in range(1, n_x)]
    line = sum(v.astype(F32) for v in lines).astype(BF)
    ends = [line[0]] + [shift(line[d], "yl", d) for d in range(1, n_y)]
    grad_up, grad_down = pl.pallas_call(
        total_kernel,
        out_shape=(shape((2, share, hidden_len), BF),) * 2,
        in_specs=vmem(n_y),
        out_specs=tuple(vmem(2)),
        cost_estimate=cost(0, 60),
        compiler_params=params(6),
    )(*ends)
    grad_down = jnp.transpose(grad_down, (0, 2, 1))

    n_dev = 2 * n_z
    p = jnp.arange(n_dev * 2 * SLOTS)
    dev_p, s_p = p // (2 * SLOTS), p % (2 * SLOTS)
    q = s_p % SLOTS
    first_of = ((dev_p // 2 * 2 + yh) * 2 + dev_p % 2) * 2
    e_p = (first_of + (q >= cap))[None, :]
    sel_t = (jnp.arange(128)[:, None] == HALF + e_p).astype(BF)
    sel_p = (jnp.arange(HALF)[:, None] == e_p).astype(BF)
    tgt = jnp.where(q < 2 * cap, q % cap + 1, -1)
    place_l = jnp.where(s_p < SLOTS, tgt, -1).astype(F32)[None, :]
    place_r = jnp.where(s_p >= SLOTS, tgt, -1).astype(F32)[None, :]
    line_o = jnp.arange(n_dev * 16)
    first_o = ((line_o // 32 * 2 + yh) * 2 + line_o // 16 % 2) * 2
    first_o = jnp.where(line_o % 16 == 2 * cap - 32, first_o, -2)
    parity = jnp.arange(2)[:, None, None]
    owners = (first_o[None, :, None] + parity == jnp.arange(128)[None, None, :]).astype(BF)
    at_slot = jnp.arange(24)[None, :, None]
    slots = (
        (at_slot < cap) & (jnp.arange(128)[None, None, :] == at_slot + parity * cap)
    ).astype(BF)
    partner = pl.pallas_call(
        functools.partial(partner_kernel, cap),
        out_shape=shape((rows, width + 128), BF),
        in_specs=vmem(7),
        out_specs=vmem(1)[0],
        cost_estimate=cost(0.4, 4),
        compiler_params=params(12),
    )(got_other, pay_other, sel_p, owners, slots, place_l, place_r)
    other = shift(partner, "yh", 1)
    grad_tokens, grad_gates = pl.pallas_call(
        functools.partial(combine_kernel, cap),
        out_shape=(shape((rows, width), BF), shape((rows, top), BF)),
        in_specs=vmem(9),
        out_specs=tuple(vmem(2)),
        cost_estimate=cost(0.4, 4),
        compiler_params=params(12),
    )(got_own, table, expert_ids, sel_t, owners, slots, place_l, place_r, other)
    return (grad_tokens, grad_gates, grad_up, grad_down)


def build(mesh):
    every, dp, ctx = ("yl", "x", "z", "yh", "c"), ("yl", "x"), ("z", "yh", "c")
    tok, up, down = P(every, None), P(ctx, dp, None), P(ctx, None, dp)
    return jax.shard_map(
        per_device,
        mesh=mesh,
        in_specs=(tok, tok, tok, tok, up, down),
        out_specs=(tok, tok, up, down),
        check_vma=False,
    )


def solution(mesh):
    return build(Mesh(mesh.devices.reshape(4, 4, 8, 2, 2), ("yl", "x", "z", "yh", "c")))
```

time: 274 us -> 338 us (1.23)
  the two profiles are of different devices: /device:TPU:299 before, /device:TPU:23 now
where the time goes in v2:
time: 338 us; the launch traced here: 336 us
  waiting for transfers between devices  145 us (43%)
  starting transfers between devices  102 us (30%)
  local copies, waits for them, and re-layouts  42.2 us (12%)
  Pallas kernels  26.1 us (8%)
  between operations  14.8 us (4%)
  other arithmetic  5.12 us (2%)
    ppermute x26, waiting for transfers between devices, shift(): return lax.ppermute(value, axis, [(i, (i + by) % n) for i in range(n)])  145 us
    ppermute x26, starting transfers between devices, shift(): return lax.ppermute(value, axis, [(i, (i + by) % n) for i in range(n)])  91.2 us
    unnamed x141, local copies, waits for them, and re-layouts  36.8 us
    all_to_all x2, starting transfers between devices, replies(): lax.all_to_all(back.reshape(2 * n_z, 2 * SLOTS, half), ('z', 'c'), 0, 0,...  11.2 us
    pallas_call x2, Pallas kernels, worked(): pl.pallas_call(functools.partial(expert_kernel, cap), out_shape=(shape((n...  10.7 us
    pallas_call x2, Pallas kernels, picked(): pl.pallas_call(functools.partial(pick_kernel, cap, n_z), out_shape=(shape...  6.92 us
  transfers between devices with their start and end apart: 29, of which 15 were waited for; matrix products, arithmetic and copies ran while one was open for 3% of the time, Pallas kernels for 7%

profile of v2, /device:TPU:23, one launch (start us, length us, event | category | flops | bytes accessed | tf_op | source)
XLA Modules:
  0.0 335.7 jit_solution(2545598100586868056)
XLA Ops:
  7.2 1.6 pad_maximum_fusion
  13.5 4.0 %collective-permute-start = (bf16[128,2176]{1,0:T(8,128)(2,1)S(1)}, bf16[128,2176]{1,0:T(8,128)(2,1)S(1)}, u32[]{:S(2)}, u32[]{:S(2)}) collective-permute-start(bf16[128,2176]{1,0:T(8,128)(2,1)S(1)} %get-tuple-element.35.refs_0_), channel_id=1, source_target_pairs={{0,4},{4,8},{8,12},{12,16},{16,20},{20,24},{24,28},{28,0},{1,5},{5... | collective-permute-start | bytes 1671176 | tf_op jit(solution)/shard_map/ppermute | solution.py:201
  17.5 8.6 %collective-permute-start.2 = (bf16[128,2176]{1,0:T(8,128)(2,1)S(1)}, bf16[128,2176]{1,0:T(8,128)(2,1)S(1)}, u32[]{:S(2)}, u32[]{:S(2)}) collective-permute-start(bf16[128,2176]{1,0:T(8,128)(2,1)S(1)} %get-tuple-element.35.refs_0_), channel_id=1, source_target_pairs={{0,28},{4,0},{8,4},{12,8},{16,12},{20,16},{24,20},{28,24},{1,29},{... | collective-permute-start | bytes 1671176 | tf_op jit(solution)/shard_map/ppermute | solution.py:201
  26.1 5.7 %collective-permute-start.4 = (bf16[128,2176]{1,0:T(8,128)(2,1)S(1)}, bf16[128,2176]{1,0:T(8,128)(2,1)S(1)}, u32[]{:S(2)}, u32[]{:S(2)}) collective-permute-start(bf16[128,2176]{1,0:T(8,128)(2,1)S(1)} %get-tuple-element.35.refs_0_), channel_id=1, source_target_pairs={{0,2},{2,0},{1,3},{3,1},{4,6},{6,4},{5,7},{7,5},{8,10},{10,8},{9,1... | collective-permute-start | bytes 1671176 | tf_op jit(solution)/shard_map/ppermute | solution.py:201
  32.5 3.9 %collective-permute-done.refs_1_ = bf16[128,2176]{1,0:T(8,128)(2,1)S(1)} collective-permute-done((bf16[128,2176]{1,0:T(8,128)(2,1)S(1)}, bf16[128,2176]{1,0:T(8,128)(2,1)S(1)}, u32[]{:S(2)}, u32[]{:S(2)}) %collective-permute-start) | collective-permute-done | bytes 557088 | tf_op jit(solution)/shard_map/ppermute | solution.py:201
  36.5 1.9 collective-permute-start.1
  39.2 4.6 %collective-permute-start.3 = (bf16[128,2176]{1,0:T(8,128)(2,1)S(1)}, bf16[128,2176]{1,0:T(8,128)(2,1)S(1)}, u32[]{:S(2)}, u32[]{:S(2)}) collective-permute-start(bf16[128,2176]{1,0:T(8,128)(2,1)S(1)} %collective-permute-done.2.refs_8_), channel_id=1, source_target_pairs={{0,28},{4,0},{8,4},{12,8},{16,12},{20,16},{24,20},{28,24},{1,29},{... | collective-permute-start | bytes 1671176 | tf_op jit(solution)/shard_map/ppermute | solution.py:201
  44.6 25.3 %collective-permute-done.4.refs_2_ = bf16[128,2176]{1,0:T(8,128)(2,1)S(1)} collective-permute-done((bf16[128,2176]{1,0:T(8,128)(2,1)S(1)}, bf16[128,2176]{1,0:T(8,128)(2,1)S(1)}, u32[]{:S(2)}, u32[]{:S(2)}) %collective-permute-start.4) | collective-permute-done | bytes 557088 | tf_op jit(solution)/shard_map/ppermute | solution.py:201
  71.7 1.9 collective-permute-start.7
  73.7 4.6 %collective-permute-start.8 = (bf16[128,2176]{1,0:T(8,128)(2,1)}, bf16[128,2176]{1,0:T(8,128)(2,1)S(1)}, u32[]{:S(2)}, u32[]{:S(2)}) collective-permute-start(bf16[128,2176]{1,0:T(8,128)(2,1)} %get-tuple-element.38.refs_0_.pay), channel_id=1, source_target_pairs={{0,28},{4,0},{8,4},{12,8},{16,12},{20,16},{24,20},{28,24},{1,29},{... | collective-permute-start | bytes 1671176 | tf_op jit(solution)/shard_map/ppermute | solution.py:201
  78.2 1.9 collective-permute-start.5
  80.2 4.6 %collective-permute-start.6 = (bf16[128,2176]{1,0:T(8,128)(2,1)}, bf16[128,2176]{1,0:T(8,128)(2,1)S(1)}, u32[]{:S(2)}, u32[]{:S(2)}) collective-permute-start(bf16[128,2176]{1,0:T(8,128)(2,1)} %get-tuple-element.37.refs_7_), channel_id=1, source_target_pairs={{0,28},{4,0},{8,4},{12,8},{16,12},{20,16},{24,20},{28,24},{1,29},{... | collective-permute-start | bytes 1671176 | tf_op jit(solution)/shard_map/ppermute | solution.py:201
  84.8 3.3 collective-permute-done.7.refs_2_
  89.1 10.9 %collective-permute-done.5.refs_0_ = bf16[128,2176]{1,0:T(8,128)(2,1)S(1)} collective-permute-done((bf16[128,2176]{1,0:T(8,128)(2,1)}, bf16[128,2176]{1,0:T(8,128)(2,1)S(1)}, u32[]{:S(2)}, u32[]{:S(2)}) %collective-permute-start.5) | collective-permute-done | bytes 557088 | tf_op jit(solution)/shard_map/ppermute | solution.py:201
  101.8 1.9 collective-permute-start.11
  103.8 5.3 %collective-permute-start.12 = (bf16[128,2176]{1,0:T(8,128)(2,1)}, bf16[128,2176]{1,0:T(8,128)(2,1)S(1)}, u32[]{:S(2)}, u32[]{:S(2)}) collective-permute-start(bf16[128,2176]{1,0:T(8,128)(2,1)} %get-tuple-element.42.refs_8_), channel_id=1, source_target_pairs={{0,28},{4,0},{8,4},{12,8},{16,12},{20,16},{24,20},{28,24},{1,29},{... | collective-permute-start | bytes 1671176 | tf_op jit(solution)/shard_map/ppermute | solution.py:201
  110.1 3.4 %collective-permute-start.10 = (bf16[64,2176]{1,0:T(8,128)(2,1)S(1)}, bf16[64,2176]{1,0:T(8,128)(2,1)S(1)}, u32[]{:S(2)}, u32[]{:S(2)}) collective-permute-start(bf16[64,2176]{1,0:T(8,128)(2,1)S(1)} %slice.35), channel_id=1, source_target_pairs={{0,28},{4,0},{8,4},{12,8},{16,12},{20,16},{24,20},{28,24},{1,29},{... | collective-permute-start | bytes 835592 | tf_op jit(solution)/shard_map/ppermute | solution.py:201
  114.5 2.1 collective-permute-start.9
  116.7 8.5 %collective-permute-done.10.refs_1_ = bf16[64,2176]{1,0:T(8,128)(2,1)S(1)} collective-permute-done((bf16[64,2176]{1,0:T(8,128)(2,1)S(1)}, bf16[64,2176]{1,0:T(8,128)(2,1)S(1)}, u32[]{:S(2)}, u32[]{:S(2)}) %collective-permute-start.10) | collective-permute-done | bytes 278560 | tf_op jit(solution)/shard_map/ppermute | solution.py:201
  134.0 4.0 %shard_map.97 = (bf16[2,144,2176]{2,1,0:T(8,128)(2,1)S(1)}, bf16[2,144,2176]{2,1,0:T(8,128)(2,1)}) custom-call(bf16[128,2176]{1,0:T(8,128)(2,1)S(1)} %copy-done.56, bf16[128,2176]{1,0:T(8,128)(2,1)S(1)} %copy-done.58, bf16[128,2176]{1,0:T(8,128)(2,1)S(1)} %copy-done.31, bf16[128,2176]{1,0:T(8,128)(2,1)S(1)} %copy-done.15, bf16[64,2176]{1,0:T(8,128)(2,1)S(1)} %copy-done.41, ...), custom_call_target="tpu_custom_call" | custom-call | flops 2600000000 | bytes 12582912 | tf_op jit(solution)/shard_map/pallas_call | solution.py:290
  139.2 4.9 %collective-permute-start.13 = (bf16[2,144,2176]{2,1,0:T(8,128)(2,1)}, bf16[2,144,2176]{2,1,0:T(8,128)(2,1)}, u32[]{:S(2)}, u32[]{:S(2)}) collective-permute-start(bf16[2,144,2176]{2,1,0:T(8,128)(2,1)} %get-tuple-element.46), channel_id=1, source_target_pairs={{0,1},{1,0},{2,3},{3,2},{4,5},{5,4},{6,7},{7,6},{8,9},{9,8},{10,11... | collective-permute-start | bytes 3760136 | tf_op jit(solution)/shard_map/ppermute | solution.py:201
  144.2 2.0 fusion.2
  146.2 3.9 %collective-permute-start.14 = (bf16[128,2176]{1,0:T(8,128)(2,1)S(1)}, bf16[128,2176]{1,0:T(8,128)(2,1)S(1)}, u32[]{:S(2)}, u32[]{:S(2)}) collective-permute-start(bf16[128,2176]{1,0:T(8,128)(2,1)S(1)} %copy-done.25), channel_id=1, source_target_pairs={{0,4},{4,8},{8,12},{12,16},{16,20},{20,24},{24,28},{28,0},{1,5},{5... | collective-permute-start | bytes 1671176 | tf_op jit(solution)/shard_map/ppermute | solution.py:201
  150.0 3.4 collective-permute-start.15
  153.6 2.4 copy.28
  156.1 6.2 %shard_map.98 = (bf16[8,2,80,512]{3,2,1,0:T(8,128)(2,1)S(1)}, bf16[2,288,384]{2,1,0:T(8,128)(2,1)S(1)}, bf16[2,288,384]{2,1,0:T(8,128)(2,1)S(1)}) custom-call(s32[3]{0:T(128)S(1)} %pad_add_fusion.spot, bf16[4,1024,384]{2,1,0:T(8,128)(2,1)S(1)} %bitcast.21, bf16[2,144,2176]{2,1,0:T(8,128)(2,1)S(1)} %copy-done.62, ...), custom_call_target="tpu_custom_call" | custom-call | flops 4000000000 | bytes 25165824 | tf_op jit(solution)/shard_map/pallas_call | solution.py:314
  166.7 6.1 %all-to-all-start = ((bf16[16,80,512]{2,1,0:T(8,128)(2,1)}), bf16[16,80,512]{2,1,0:T(8,128)(2,1)S(1)}, u32[]{:S(2)}, u32[]{:S(2)}) async-start(bf16[16,80,512]{2,1,0:T(8,128)(2,1)} %bitcast.20), calls=%async_computation | async-start | bytes 2621440 | tf_op jit(solution)/shard_map/all_to_all | solution.py:329
  172.9 3.3 collective-permute-start.16
  176.2 3.4 %collective-permute-start.17 = (bf16[64,2176]{1,0:T(8,128)(2,1)S(1)}, bf16[64,2176]{1,0:T(8,128)(2,1)S(1)}, u32[]{:S(2)}, u32[]{:S(2)}) collective-permute-start(bf16[64,2176]{1,0:T(8,128)(2,1)S(1)} %slice.45), channel_id=1, source_target_pairs={{0,28},{4,0},{8,4},{12,8},{16,12},{20,16},{24,20},{28,24},{1,29},{... | collective-permute-start | bytes 835592 | tf_op jit(solution)/shard_map/ppermute | solution.py:201
  179.7 30.8 %collective-permute-done.16.refs_4_ = bf16[64,2176]{1,0:T(8,128)(2,1)S(1)} collective-permute-done((bf16[64,2176]{1,0:T(8,128)(2,1)S(1)}, bf16[64,2176]{1,0:T(8,128)(2,1)S(1)}, u32[]{:S(2)}, u32[]{:S(2)}) %collective-permute-start.16) | collective-permute-done | bytes 278560 | tf_op jit(solution)/shard_map/ppermute | solution.py:201
  218.6 2.9 shard_map.100
  221.5 2.8 collective-permute-start.18
  224.3 2.5 collective-permute-done.18.got.refs_3_
  226.9 4.5 %shard_map.101 = (bf16[8,2,80,512]{3,2,1,0:T(8,128)(2,1)S(1)}, bf16[2,288,384]{2,1,0:T(8,128)(2,1)S(1)}, bf16[2,288,384]{2,1,0:T(8,128)(2,1)S(1)}) custom-call(s32[3]{0:T(128)S(1)} %pad_add_fusion.spot, bf16[4,1024,384]{2,1,0:T(8,128)(2,1)S(1)} %bitcast.22, bf16[2,144,2176]{2,1,0:T(8,128)(2,1)S(1)} %get-tuple-element.52.own.refs_2_, ...), custom_call_target="tpu_custom_call" | custom-call | flops 4000000000 | bytes 25165824 | tf_op jit(solution)/shard_map/pallas_call | solution.py:314
  232.5 4.8 %shard_map.102 = (bf16[4,4,64,384]{3,2,1,0:T(8,128)(2,1)S(1)}, bf16[4,4,64,384]{3,2,1,0:T(8,128)(2,1)S(1)}, bf16[4,4,64,384]{3,2,1,0:T(8,128)(2,1)S(1)}, bf16[4,4,64,384]{3,2,1,0:T(8,128)(2,1)S(1)}) custom-call(s32[3]{0:T(128)S(1)} %pad_add_fusion.spot, bf16[2,144,2176]{2,1,0:T(8,128)(2,1)S(1)} %copy-done.63, ...), custom_call_target="tpu_custom_call" | custom-call | flops 2000000000 | bytes 18874368 | tf_op jit(solution)/shard_map/pallas_call | solution.py:339
  242.0 5.1 %all-to-all-start.1 = ((bf16[16,80,512]{2,1,0:T(8,128)(2,1)}), bf16[16,80,512]{2,1,0:T(8,128)(2,1)S(1)}, u32[]{:S(2)}, u32[]{:S(2)}) async-start(bf16[16,80,512]{2,1,0:T(8,128)(2,1)} %bitcast.19), calls=%async_computation.1 | async-start | bytes 2621440 | tf_op jit(solution)/shard_map/all_to_all | solution.py:329
  247.4 1.9 collective-permute-start.20
  249.3 1.9 collective-permute-start.21
  251.3 3.4 %collective-permute-start.22 = (bf16[4,4,64,384]{3,2,1,0:T(8,128)(2,1)}, bf16[4,4,64,384]{3,2,1,0:T(8,128)(2,1)S(1)}, u32[]{:S(2)}, u32[]{:S(2)}) collective-permute-start(bf16[4,4,64,384]{3,2,1,0:T(8,128)(2,1)} %copy-done.52), channel_id=1, source_target_pairs={{0,96},{32,0},{64,32},{96,64},{1,97},{33,1},{65,33},{97,65},{2,98}... | collective-permute-start | bytes 2359304 | tf_op jit(solution)/shard_map/ppermute | solution.py:201
  254.9 13.8 %collective-permute-done.20 = bf16[4,4,64,384]{3,2,1,0:T(8,128)(2,1)S(1)} collective-permute-done((bf16[4,4,64,384]{3,2,1,0:T(8,128)(2,1)}, bf16[4,4,64,384]{3,2,1,0:T(8,128)(2,1)S(1)}, u32[]{:S(2)}, u32[]{:S(2)}) %collective-permute-start.20) | collective-permute-done | bytes 786464 | tf_op jit(solution)/shard_map/ppermute | solution.py:201
  268.6 3.5 %collective-permute-done.21 = bf16[4,4,64,384]{3,2,1,0:T(8,128)(2,1)S(1)} collective-permute-done((bf16[4,4,64,384]{3,2,1,0:T(8,128)(2,1)}, bf16[4,4,64,384]{3,2,1,0:T(8,128)(2,1)S(1)}, u32[]{:S(2)}, u32[]{:S(2)}) %collective-permute-start.21) | collective-permute-done | bytes 786464 | tf_op jit(solution)/shard_map/ppermute | solution.py:201
  272.1 17.2 %collective-permute-done.22 = bf16[4,4,64,384]{3,2,1,0:T(8,128)(2,1)S(1)} collective-permute-done((bf16[4,4,64,384]{3,2,1,0:T(8,128)(2,1)}, bf16[4,4,64,384]{3,2,1,0:T(8,128)(2,1)S(1)}, u32[]{:S(2)}, u32[]{:S(2)}) %collective-permute-start.22) | collective-permute-done | bytes 786464 | tf_op jit(solution)/shard_map/ppermute | solution.py:201
  290.6 1.9 collective-permute-start.23
  292.5 2.7 collective-permute-start.24
  295.2 2.6 collective-permute-start.25
  298.8 4.9 %collective-permute-start.19 = (bf16[128,1152]{1,0:T(8,128)(2,1)S(1)}, bf16[128,1152]{1,0:T(8,128)(2,1)S(1)}, u32[]{:S(2)}, u32[]{:S(2)}) collective-permute-start(bf16[128,1152]{1,0:T(8,128)(2,1)S(1)} %shard_map.104), channel_id=1, source_target_pairs={{0,2},{2,0},{1,3},{3,1},{4,6},{6,4},{5,7},{7,5},{8,10},{10,8},{9,1... | collective-permute-start | bytes 884744 | tf_op jit(solution)/shard_map/ppermute | solution.py:201
  303.8 10.0 %collective-permute-done.25.refs_3_ = bf16[4,64,384]{2,1,0:T(8,128)(2,1)S(1)} collective-permute-done((bf16[4,64,384]{2,1,0:T(8,128)(2,1)S(1)}, bf16[4,64,384]{2,1,0:T(8,128)(2,1)S(1)}, u32[]{:S(2)}, u32[]{:S(2)}) %collective-permute-start.25) | collective-permute-done | bytes 196640 | tf_op jit(solution)/shard_map/ppermute | solution.py:201
  314.6 12.0 %collective-permute-done.19.other = bf16[128,1152]{1,0:T(8,128)(2,1)S(1)} collective-permute-done((bf16[128,1152]{1,0:T(8,128)(2,1)S(1)}, bf16[128,1152]{1,0:T(8,128)(2,1)S(1)}, u32[]{:S(2)}, u32[]{:S(2)}) %collective-permute-start.19) | collective-permute-done | bytes 294944 | tf_op jit(solution)/shard_map/ppermute | solution.py:201
  (201 shorter events, 48.1 us)
Async XLA Ops:
  7.2 146.4 %all-gather.3.cloned.1.call-start = ((), (), s32[]{:S(2)}) async-start(), calls=%async_computation.2 | async-start | bytes 3342336 | tf_op jit(solution)/shard_map/all_gather | solution.py:278
  13.5 23.0 %collective-permute-start = (bf16[128,2176]{1,0:T(8,128)(2,1)S(1)}, bf16[128,2176]{1,0:T(8,128)(2,1)S(1)}, u32[]{:S(2)}, u32[]{:S(2)}) collective-permute-start(bf16[128,2176]{1,0:T(8,128)(2,1)S(1)} %get-tuple-element.35.refs_0_), channel_id=1, source_target_pairs={{0,4},{4,8},{8,12},{12,16},{16,20},{20,24},{24,28},{28,0},{1,5},{5... | collective-permute-start | bytes 1671176 | tf_op jit(solution)/shard_map/ppermute | solution.py:201
  17.5 21.7 %collective-permute-start.2 = (bf16[128,2176]{1,0:T(8,128)(2,1)S(1)}, bf16[128,2176]{1,0:T(8,128)(2,1)S(1)}, u32[]{:S(2)}, u32[]{:S(2)}) collective-permute-start(bf16[128,2176]{1,0:T(8,128)(2,1)S(1)} %get-tuple-element.35.refs_0_), channel_id=1, source_target_pairs={{0,28},{4,0},{8,4},{12,8},{16,12},{20,16},{24,20},{28,24},{1,29},{... | collective-permute-start | bytes 1671176 | tf_op jit(solution)/shard_map/ppermute | solution.py:201
  26.1 43.8 %collective-permute-start.4 = (bf16[128,2176]{1,0:T(8,128)(2,1)S(1)}, bf16[128,2176]{1,0:T(8,128)(2,1)S(1)}, u32[]{:S(2)}, u32[]{:S(2)}) collective-permute-start(bf16[128,2176]{1,0:T(8,128)(2,1)S(1)} %get-tuple-element.35.refs_0_), channel_id=1, source_target_pairs={{0,2},{2,0},{1,3},{3,1},{4,6},{6,4},{5,7},{7,5},{8,10},{10,8},{9,1... | collective-permute-start | bytes 1671176 | tf_op jit(solution)/shard_map/ppermute | solution.py:201
  36.5 33.4 %collective-permute-start.1 = (bf16[128,2176]{1,0:T(8,128)(2,1)S(1)}, bf16[128,2176]{1,0:T(8,128)(2,1)S(1)}, u32[]{:S(2)}, u32[]{:S(2)}) collective-permute-start(bf16[128,2176]{1,0:T(8,128)(2,1)S(1)} %collective-permute-done.refs_1_), channel_id=1, source_target_pairs={{0,4},{4,8},{8,12},{12,16},{16,20},{20,24},{24,28},{28,0},{1,5},{5... | collective-permute-start | bytes 1671176 | tf_op jit(solution)/shard_map/ppermute | solution.py:201
  39.2 30.7 %collective-permute-start.3 = (bf16[128,2176]{1,0:T(8,128)(2,1)S(1)}, bf16[128,2176]{1,0:T(8,128)(2,1)S(1)}, u32[]{:S(2)}, u32[]{:S(2)}) collective-permute-start(bf16[128,2176]{1,0:T(8,128)(2,1)S(1)} %collective-permute-done.2.refs_8_), channel_id=1, source_target_pairs={{0,28},{4,0},{8,4},{12,8},{16,12},{20,16},{24,20},{28,24},{1,29},{... | collective-permute-start | bytes 1671176 | tf_op jit(solution)/shard_map/ppermute | solution.py:201
  71.7 16.4 %collective-permute-start.7 = (bf16[128,2176]{1,0:T(8,128)(2,1)}, bf16[128,2176]{1,0:T(8,128)(2,1)S(1)}, u32[]{:S(2)}, u32[]{:S(2)}) collective-permute-start(bf16[128,2176]{1,0:T(8,128)(2,1)} %get-tuple-element.38.refs_0_.pay), channel_id=1, source_target_pairs={{0,4},{4,8},{8,12},{12,16},{16,20},{20,24},{24,28},{28,0},{1,5},{5... | collective-permute-start | bytes 1671176 | tf_op jit(solution)/shard_map/ppermute | solution.py:201
  73.7 15.4 %collective-permute-start.8 = (bf16[128,2176]{1,0:T(8,128)(2,1)}, bf16[128,2176]{1,0:T(8,128)(2,1)S(1)}, u32[]{:S(2)}, u32[]{:S(2)}) collective-permute-start(bf16[128,2176]{1,0:T(8,128)(2,1)} %get-tuple-element.38.refs_0_.pay), channel_id=1, source_target_pairs={{0,28},{4,0},{8,4},{12,8},{16,12},{20,16},{24,20},{28,24},{1,29},{... | collective-permute-start | bytes 1671176 | tf_op jit(solution)/shard_map/ppermute | solution.py:201
  78.2 21.8 %collective-permute-start.5 = (bf16[128,2176]{1,0:T(8,128)(2,1)}, bf16[128,2176]{1,0:T(8,128)(2,1)S(1)}, u32[]{:S(2)}, u32[]{:S(2)}) collective-permute-start(bf16[128,2176]{1,0:T(8,128)(2,1)} %get-tuple-element.36.refs_2_), channel_id=1, source_target_pairs={{0,4},{4,8},{8,12},{12,16},{16,20},{20,24},{24,28},{28,0},{1,5},{5... | collective-permute-start | bytes 1671176 | tf_op jit(solution)/shard_map/ppermute | solution.py:201
  80.2 20.9 %collective-permute-start.6 = (bf16[128,2176]{1,0:T(8,128)(2,1)}, bf16[128,2176]{1,0:T(8,128)(2,1)S(1)}, u32[]{:S(2)}, u32[]{:S(2)}) collective-permute-start(bf16[128,2176]{1,0:T(8,128)(2,1)} %get-tuple-element.37.refs_7_), channel_id=1, source_target_pairs={{0,28},{4,0},{8,4},{12,8},{16,12},{20,16},{24,20},{28,24},{1,29},{... | collective-permute-start | bytes 1671176 | tf_op jit(solution)/shard_map/ppermute | solution.py:201
  88.1 12.9 %copy-start.20 = (bf16[128,2176]{1,0:T(8,128)(2,1)}, bf16[128,2176]{1,0:T(8,128)(2,1)S(1)}, u32[]{:S(2)}) copy-start(bf16[128,2176]{1,0:T(8,128)(2,1)S(1)} %collective-permute-done.7.refs_2_) | copy-start | bytes 1671172
  89.1 11.9 %copy-start.22 = (bf16[128,2176]{1,0:T(8,128)(2,1)}, bf16[128,2176]{1,0:T(8,128)(2,1)S(1)}, u32[]{:S(2)}) copy-start(bf16[128,2176]{1,0:T(8,128)(2,1)S(1)} %collective-permute-done.8.refs_3_) | copy-start | bytes 1671172
  101.8 23.4 %collective-permute-start.11 = (bf16[128,2176]{1,0:T(8,128)(2,1)}, bf16[128,2176]{1,0:T(8,128)(2,1)S(1)}, u32[]{:S(2)}, u32[]{:S(2)}) collective-permute-start(bf16[128,2176]{1,0:T(8,128)(2,1)} %get-tuple-element.41.refs_1_), channel_id=1, source_target_pairs={{0,4},{4,8},{8,12},{12,16},{16,20},{20,24},{24,28},{28,0},{1,5},{5... | collective-permute-start | bytes 1671176 | tf_op jit(solution)/shard_map/ppermute | solution.py:201
  103.8 22.3 %collective-permute-start.12 = (bf16[128,2176]{1,0:T(8,128)(2,1)}, bf16[128,2176]{1,0:T(8,128)(2,1)S(1)}, u32[]{:S(2)}, u32[]{:S(2)}) collective-permute-start(bf16[128,2176]{1,0:T(8,128)(2,1)} %get-tuple-element.42.refs_8_), channel_id=1, source_target_pairs={{0,28},{4,0},{8,4},{12,8},{16,12},{20,16},{24,20},{28,24},{1,29},{... | collective-permute-start | bytes 1671176 | tf_op jit(solution)/shard_map/ppermute | solution.py:201
  110.1 15.2 %collective-permute-start.10 = (bf16[64,2176]{1,0:T(8,128)(2,1)S(1)}, bf16[64,2176]{1,0:T(8,128)(2,1)S(1)}, u32[]{:S(2)}, u32[]{:S(2)}) collective-permute-start(bf16[64,2176]{1,0:T(8,128)(2,1)S(1)} %slice.35), channel_id=1, source_target_pairs={{0,28},{4,0},{8,4},{12,8},{16,12},{20,16},{24,20},{28,24},{1,29},{... | collective-permute-start | bytes 835592 | tf_op jit(solution)/shard_map/ppermute | solution.py:201
  114.4 13.4 %copy-start.15 = (bf16[128,2176]{1,0:T(8,128)(2,1)S(1)}, bf16[128,2176]{1,0:T(8,128)(2,1)}, u32[]{:S(2)}) copy-start(bf16[128,2176]{1,0:T(8,128)(2,1)} %get-tuple-element.39.refs_3_) | copy-start | bytes 1671172
  114.4 13.4 %copy-start.17 = (bf16[128,2176]{1,0:T(8,128)(2,1)S(1)}, bf16[128,2176]{1,0:T(8,128)(2,1)}, u32[]{:S(2)}) copy-start(bf16[128,2176]{1,0:T(8,128)(2,1)} %get-tuple-element.40.refs_6_) | copy-start | bytes 1671172
  114.5 13.4 %copy-start.33 = (bf16[128,2176]{1,0:T(8,128)(2,1)S(1)}, bf16[128,2176]{1,0:T(8,128)(2,1)}, u32[]{:S(2)}) copy-start(bf16[128,2176]{1,0:T(8,128)(2,1)} %get-tuple-element.37.refs_7_) | copy-start | bytes 1671172
  114.5 10.8 %collective-permute-start.9 = (bf16[64,2176]{1,0:T(8,128)(2,1)S(1)}, bf16[64,2176]{1,0:T(8,128)(2,1)S(1)}, u32[]{:S(2)}, u32[]{:S(2)}) collective-permute-start(bf16[64,2176]{1,0:T(8,128)(2,1)S(1)} %slice.34), channel_id=1, source_target_pairs={{0,4},{4,8},{8,12},{12,16},{16,20},{20,24},{24,28},{28,0},{1,5},{5... | collective-permute-start | bytes 835592 | tf_op jit(solution)/shard_map/ppermute | solution.py:201
  116.7 21.3 %copy-start.18 = (bf16[576,512]{1,0:T(8,128)(2,1)}, bf16[576,512]{1,0:T(8,128)(2,1)S(1)}, u32[]{:S(2)}) copy-start(bf16[576,512]{1,0:T(8,128)(2,1)S(1)} %fusion.refs_9_) | copy-start | bytes 1769476
  127.8 10.2 %copy-start.46 = (f32[144,128]{1,0:T(8,128)}, f32[144,128]{1,0:T(8,128)S(1)}, u32[]{:S(2)}) copy-start(f32[144,128]{1,0:T(8,128)S(1)} %broadcast_in_dim.24.refs_10_) | copy-start | bytes 221188
  139.2 7.0 %copy-start.25 = (bf16[128,2176]{1,0:T(8,128)(2,1)S(1)}, bf16[128,2176]{1,0:T(8,128)(2,1)}, u32[]{:S(2)}) copy-start(bf16[128,2176]{1,0:T(8,128)(2,1)} %get-tuple-element.48.refs_2_) | copy-start | bytes 1671172
  139.2 10.9 %copy-start.28 = (bf16[128,2176]{1,0:T(8,128)(2,1)S(1)}, bf16[128,2176]{1,0:T(8,128)(2,1)}, u32[]{:S(2)}) copy-start(bf16[128,2176]{1,0:T(8,128)(2,1)} %get-tuple-element.49.refs_7_) | copy-start | bytes 1671172
  139.2 16.9 %collective-permute-start.13 = (bf16[2,144,2176]{2,1,0:T(8,128)(2,1)}, bf16[2,144,2176]{2,1,0:T(8,128)(2,1)}, u32[]{:S(2)}, u32[]{:S(2)}) collective-permute-start(bf16[2,144,2176]{2,1,0:T(8,128)(2,1)} %get-tuple-element.46), channel_id=1, source_target_pairs={{0,1},{1,0},{2,3},{3,2},{4,5},{5,4},{6,7},{7,6},{8,9},{9,8},{10,11... | collective-permute-start | bytes 3760136 | tf_op jit(solution)/shard_map/ppermute | solution.py:201
  146.1 9.9 %copy-start.34 = (bf16[640,288]{1,0:T(8,128)(2,1)}, bf16[640,288]{1,0:T(8,128)(2,1)S(1)}, u32[]{:S(2)}) copy-start(bf16[640,288]{1,0:T(8,128)(2,1)S(1)} %get-tuple-element.79.perm_l) | copy-start | bytes 1105924
  146.2 18.7 %collective-permute-start.14 = (bf16[128,2176]{1,0:T(8,128)(2,1)S(1)}, bf16[128,2176]{1,0:T(8,128)(2,1)S(1)}, u32[]{:S(2)}, u32[]{:S(2)}) collective-permute-start(bf16[128,2176]{1,0:T(8,128)(2,1)S(1)} %copy-done.25), channel_id=1, source_target_pairs={{0,4},{4,8},{8,12},{12,16},{16,20},{20,24},{24,28},{28,0},{1,5},{5... | collective-permute-start | bytes 1671176 | tf_op jit(solution)/shard_map/ppermute | solution.py:201
  150.0 15.8 %collective-permute-start.15 = (bf16[128,2176]{1,0:T(8,128)(2,1)S(1)}, bf16[128,2176]{1,0:T(8,128)(2,1)S(1)}, u32[]{:S(2)}, u32[]{:S(2)}) collective-permute-start(bf16[128,2176]{1,0:T(8,128)(2,1)S(1)} %copy-done.28), channel_id=1, source_target_pairs={{0,28},{4,0},{8,4},{12,8},{16,12},{20,16},{24,20},{28,24},{1,29},{... | collective-permute-start | bytes 1671176 | tf_op jit(solution)/shard_map/ppermute | solution.py:201
  166.7 9.5 %copy-start.13 = (bf16[128,2176]{1,0:T(8,128)(2,1)S(1)}, bf16[128,2176]{1,0:T(8,128)(2,1)}, u32[]{:S(2)}) copy-start(bf16[128,2176]{1,0:T(8,128)(2,1)} %copy-done.12) | copy-start | bytes 1671172
  166.7 43.8 %copy-start.9 = (bf16[128,2176]{1,0:T(8,128)(2,1)S(1)}, bf16[128,2176]{1,0:T(8,128)(2,1)}, u32[]{:S(2)}) copy-start(bf16[128,2176]{1,0:T(8,128)(2,1)} %get-tuple-element.38.refs_0_.pay) | copy-start | bytes 1671172
  166.7 74.2 %all-to-all-start = ((bf16[16,80,512]{2,1,0:T(8,128)(2,1)}), bf16[16,80,512]{2,1,0:T(8,128)(2,1)S(1)}, u32[]{:S(2)}, u32[]{:S(2)}) async-start(bf16[16,80,512]{2,1,0:T(8,128)(2,1)} %bitcast.20), calls=%async_computation | async-start | bytes 2621440 | tf_op jit(solution)/shard_map/all_to_all | solution.py:329
  172.9 37.6 %collective-permute-start.16 = (bf16[64,2176]{1,0:T(8,128)(2,1)S(1)}, bf16[64,2176]{1,0:T(8,128)(2,1)S(1)}, u32[]{:S(2)}, u32[]{:S(2)}) collective-permute-start(bf16[64,2176]{1,0:T(8,128)(2,1)S(1)} %slice.44), channel_id=1, source_target_pairs={{0,4},{4,8},{8,12},{12,16},{16,20},{20,24},{24,28},{28,0},{1,5},{5... | collective-permute-start | bytes 835592 | tf_op jit(solution)/shard_map/ppermute | solution.py:201
  176.2 34.3 %collective-permute-start.17 = (bf16[64,2176]{1,0:T(8,128)(2,1)S(1)}, bf16[64,2176]{1,0:T(8,128)(2,1)S(1)}, u32[]{:S(2)}, u32[]{:S(2)}) collective-permute-start(bf16[64,2176]{1,0:T(8,128)(2,1)S(1)} %slice.45), channel_id=1, source_target_pairs={{0,28},{4,0},{8,4},{12,8},{16,12},{20,16},{24,20},{28,24},{1,29},{... | collective-permute-start | bytes 835592 | tf_op jit(solution)/shard_map/ppermute | solution.py:201
  218.6 8.3 %copy-start.5 = (bf16[16,4,64,384]{3,2,0,1:T(8,128)(2,1)S(1)}, bf16[16,4,64,384]{3,2,0,1:T(8,128)(2,1)}, u32[]{:S(2)}) copy-start(bf16[16,4,64,384]{3,2,0,1:T(8,128)(2,1)} %copy-done.4) | copy-start | bytes 9437188
  218.6 8.3 %copy-start.35 = (bf16[640,288]{1,0:T(8,128)(2,1)S(1)}, bf16[640,288]{1,0:T(8,128)(2,1)}, u32[]{:S(2)}) copy-start(bf16[640,288]{1,0:T(8,128)(2,1)} %copy-done.34) | copy-start | bytes 1105924
  218.6 8.3 %copy-start.37 = (bf16[640,288]{1,0:T(8,128)(2,1)S(1)}, bf16[640,288]{1,0:T(8,128)(2,1)}, u32[]{:S(2)}) copy-start(bf16[640,288]{1,0:T(8,128)(2,1)} %get-tuple-element.80.perm_s) | copy-start | bytes 1105924
  218.6 8.3 %copy-start.45 = (f32[288,128]{1,0:T(8,128)S(1)}, f32[288,128]{1,0:T(8,128)}, u32[]{:S(2)}) copy-start(f32[288,128]{1,0:T(8,128)} %copy-done.44) | copy-start | bytes 442372
  221.5 5.3 %collective-permute-start.18 = (bf16[2,144,2176]{2,1,0:T(8,128)(2,1)S(1)}, bf16[2,144,2176]{2,1,0:T(8,128)(2,1)S(1)}, u32[]{:S(2)}, u32[]{:S(2)}) collective-permute-start(bf16[2,144,2176]{2,1,0:T(8,128)(2,1)S(1)} %get-tuple-element.53), channel_id=1, source_target_pairs={{0,1},{1,0},{2,3},{3,2},{4,5},{5,4},{6,7},{7,6},{8,9},{9,8},{10,11... | collective-permute-start | bytes 3760136 | tf_op jit(solution)/shard_map/ppermute | solution.py:201
  242.0 47.3 %copy-start.7 = (bf16[4,4,64,384]{3,2,1,0:T(8,128)(2,1)S(1)}, bf16[4,4,64,384]{3,2,1,0:T(8,128)(2,1)}, u32[]{:S(2)}) copy-start(bf16[4,4,64,384]{3,2,1,0:T(8,128)(2,1)} %copy-done.6) | copy-start | bytes 2359300
  242.0 55.8 %all-to-all-start.1 = ((bf16[16,80,512]{2,1,0:T(8,128)(2,1)}), bf16[16,80,512]{2,1,0:T(8,128)(2,1)S(1)}, u32[]{:S(2)}, u32[]{:S(2)}) async-start(bf16[16,80,512]{2,1,0:T(8,128)(2,1)} %bitcast.19), calls=%async_computation.1 | async-start | bytes 2621440 | tf_op jit(solution)/shard_map/all_to_all | solution.py:329
  247.4 21.2 %collective-permute-start.20 = (bf16[4,4,64,384]{3,2,1,0:T(8,128)(2,1)}, bf16[4,4,64,384]{3,2,1,0:T(8,128)(2,1)S(1)}, u32[]{:S(2)}, u32[]{:S(2)}) collective-permute-start(bf16[4,4,64,384]{3,2,1,0:T(8,128)(2,1)} %copy-done.54), channel_id=1, source_target_pairs={{0,32},{32,64},{64,96},{96,0},{1,33},{33,65},{65,97},{97,1},{2,34}... | collective-permute-start | bytes 2359304 | tf_op jit(solution)/shard_map/ppermute | solution.py:201
  249.3 22.8 %collective-permute-start.21 = (bf16[4,4,64,384]{3,2,1,0:T(8,128)(2,1)}, bf16[4,4,64,384]{3,2,1,0:T(8,128)(2,1)S(1)}, u32[]{:S(2)}, u32[]{:S(2)}) collective-permute-start(bf16[4,4,64,384]{3,2,1,0:T(8,128)(2,1)} %copy-done.53), channel_id=1, source_target_pairs={{0,64},{32,96},{64,0},{96,32},{1,65},{33,97},{65,1},{97,33},{2,66}... | collective-permute-start | bytes 2359304 | tf_op jit(solution)/shard_map/ppermute | solution.py:201
  251.3 38.0 %collective-permute-start.22 = (bf16[4,4,64,384]{3,2,1,0:T(8,128)(2,1)}, bf16[4,4,64,384]{3,2,1,0:T(8,128)(2,1)S(1)}, u32[]{:S(2)}, u32[]{:S(2)}) collective-permute-start(bf16[4,4,64,384]{3,2,1,0:T(8,128)(2,1)} %copy-done.52), channel_id=1, source_target_pairs={{0,96},{32,0},{64,32},{96,64},{1,97},{33,1},{65,33},{97,65},{2,98}... | collective-permute-start | bytes 2359304 | tf_op jit(solution)/shard_map/ppermute | solution.py:201
  290.6 13.1 %collective-permute-start.23 = (bf16[4,64,384]{2,1,0:T(8,128)(2,1)}, bf16[4,64,384]{2,1,0:T(8,128)(2,1)S(1)}, u32[]{:S(2)}, u32[]{:S(2)}) collective-permute-start(bf16[4,64,384]{2,1,0:T(8,128)(2,1)} %get-tuple-element.76), channel_id=1, source_target_pairs={{0,128},{128,256},{256,384},{384,0},{1,129},{129,257},{257,385},{3... | collective-permute-start | bytes 589832 | tf_op jit(solution)/shard_map/ppermute | solution.py:201
  292.5 11.2 %collective-permute-start.24 = (bf16[4,64,384]{2,1,0:T(8,128)(2,1)S(1)}, bf16[4,64,384]{2,1,0:T(8,128)(2,1)S(1)}, u32[]{:S(2)}, u32[]{:S(2)}) collective-permute-start(bf16[4,64,384]{2,1,0:T(8,128)(2,1)S(1)} %get-tuple-element.75), channel_id=1, source_target_pairs={{0,256},{128,384},{256,0},{384,128},{1,257},{129,385},{257,1},{385... | collective-permute-start | bytes 589832 | tf_op jit(solution)/shard_map/ppermute | solution.py:201
  295.2 18.6 %collective-permute-start.25 = (bf16[4,64,384]{2,1,0:T(8,128)(2,1)S(1)}, bf16[4,64,384]{2,1,0:T(8,128)(2,1)S(1)}, u32[]{:S(2)}, u32[]{:S(2)}) collective-permute-start(bf16[4,64,384]{2,1,0:T(8,128)(2,1)S(1)} %get-tuple-element.74), channel_id=1, source_target_pairs={{0,384},{128,0},{256,128},{384,256},{1,385},{129,1},{257,129},{385... | collective-permute-start | bytes 589832 | tf_op jit(solution)/shard_map/ppermute | solution.py:201
  297.9 28.7 %copy-start.1 = (bf16[16,80,512]{2,1,0:T(8,128)(2,1)S(1)}, bf16[16,80,512]{2,1,0:T(8,128)(2,1)}, u32[]{:S(2)}) copy-start(bf16[16,80,512]{2,1,0:T(8,128)(2,1)} %copy-done) | copy-start | bytes 3932164
  297.9 28.7 %copy-start.51 = (f32[128,128]{1,0:T(8,128)S(1)}, f32[128,128]{1,0:T(8,128)}, u32[]{:S(2)}) copy-start(f32[128,128]{1,0:T(8,128)} %copy-done.50) | copy-start | bytes 196612
  298.8 27.8 %collective-permute-start.19 = (bf16[128,1152]{1,0:T(8,128)(2,1)S(1)}, bf16[128,1152]{1,0:T(8,128)(2,1)S(1)}, u32[]{:S(2)}, u32[]{:S(2)}) collective-permute-start(bf16[128,1152]{1,0:T(8,128)(2,1)S(1)} %shard_map.104), channel_id=1, source_target_pairs={{0,2},{2,0},{1,3},{3,1},{4,6},{6,4},{5,7},{7,5},{8,10},{10,8},{9,1... | collective-permute-start | bytes 884744 | tf_op jit(solution)/shard_map/ppermute | solution.py:201
  (50 other events, 78.8 us)
Sparse Core Ops, SparseCore 0:
  10.7 91.5 all-gather.2

commit v3 on v2

--- a/solution.py
+++ b/solution.py
@@ -56,15 +56,15 @@
 
 
 def pick_kernel(cap, n_z, *refs):
-    blocks = refs[: n_z + 1]
-    sel, place, origin = refs[n_z + 1 : n_z + 4]
-    own, sib = refs[-2:]
-    rows, lanes = blocks[0].shape
-    width = lanes - 128
-    mid = n_z // 2
+    *blocks, sel, place, origin, own, sib = refs
+    if len(blocks) == 1:
+        blocks = tops = ends = [blocks[0].at[i] for i in range(n_z)]
+    else:
+        mid = n_z // 2
+        tops = [b for i, b in enumerate(blocks) if i != mid + 1]
+        ends = [b for i, b in enumerate(blocks) if i != mid]
+    width = own.shape[2] - 128
     block = n_z * cap
-    tops = [b for i, b in enumerate(blocks) if i != mid + 1]
-    ends = [b for i, b in enumerate(blocks) if i != mid]
     gates = jnp.concatenate([b[:HALF, width:] for b in tops], axis=0)
     places = jnp.concatenate(
         [b[b.shape[0] - HALF :, width:] for b in ends], axis=0
@@ -126,23 +126,27 @@
 
 def weight_kernel(n_y, n_x, spot, *refs):
     rows_in, fac = refs[:4], refs[4:8]
-    g_out, parts = refs[8 : 8 + n_x], refs[8 + n_x]
+    g_out, parts = refs[8:-1], refs[-1]
     share, hidden_len = parts.shape[2:]
     width = parts.shape[0] * share
     for e in range(2):
         for m in range(2):
             x = jnp.concatenate([r[e, :, m * width : (m + 1) * width] for r in rows_in], axis=0)
             f = jnp.concatenate((fac[m][e], fac[2 + m][e]), axis=0)
-            parts[:, 2 * m + e] = dot(x, f, 0, 0).astype(BF).reshape(-1, share, hidden_len)
-    for d in range(n_x):
-        for i in range(n_y):
-            g_out[d][i] = parts[lax.rem(spot[0] + i, n_y) * n_x + lax.rem(spot[1] + d, n_x)]
+            parts[:, 2 * e + m] = dot(x, f, 0, 0).astype(BF).reshape(-1, share, hidden_len)
+        for d in range(n_x):
+            for i in range(n_y):
+                group = lax.rem(spot[0] + i, n_y) * n_x + lax.rem(spot[1] + d, n_x)
+                g_out[e * n_x + d][i] = parts[group, 2 * e : 2 * e + 2]
 
 
 def total_kernel(*refs):
     *ends, up, down = refs
-    up[...] = sum(r[:2].astype(F32) for r in ends).astype(BF)
-    down[...] = sum(r[2:].astype(F32) for r in ends).astype(BF)
+    n_y = len(ends) // 2
+    for e in range(2):
+        some = ends[e * n_y : (e + 1) * n_y]
+        up[e] = sum(r[0].astype(F32) for r in some).astype(BF)
+        down[e] = sum(r[1].astype(F32) for r in some).astype(BF)
 
 
 def partial_sums(cap, got, at, lane_places, owners, slots, place_l, place_r):
@@ -201,56 +205,36 @@
     return lax.ppermute(value, axis, [(i, (i + by) % n) for i in range(n)])
 
 
-def together(values, after=()):
-    anywhere = pl.BlockSpec(memory_space=pl.ANY)
-    return pl.pallas_call(
-        lambda *refs: None,
-        out_shape=tuple(jax.ShapeDtypeStruct(v.shape, v.dtype) for v in values),
-        in_specs=[anywhere] * (len(values) + len(after)),
-        out_specs=(anywhere,) * len(values),
-        input_output_aliases={i: i for i in range(len(values))},
-    )(*values, *after)
-
-
-def rings(block):
+def ring(block, beside, then):
     steps = lax.axis_size("z") // 2
     rows = block.shape[0] // 2
-    chains = [([block], [block]), ([], [])]
-
-    def advance(chain):
-        below, above = chain
-        if len(below) < steps:
-            below.append(shift(below[-1], "z", 1))
-            above.append(shift(above[-1], "z", -1))
-        elif len(below) == steps:
-            below.append(shift(below[-1][:rows], "z", 1))
-            above.append(shift(above[-1][rows:], "z", -1))
-
-    def settle():
-        ends = [chain[-1] for pair in chains for chain in pair]
-        ends[2:] = ends[2:] if ends[2] is not ends[3] else ends[2:3]
-        held = together(ends)
-        for n, chain in enumerate(chain for pair in chains for chain in pair):
-            chain[-1] = held[min(n, len(held) - 1)]
-
-    partner = shift(block, "yh", 1)
-    advance(chains[0])
-    advance(chains[0])
-    for chain in chains[1]:
-        chain.append(partner)
-    settle()
-    partner = chains[1][0][0]
-    while len(chains[0][0]) <= steps:
-        advance(chains[0])
-        advance(chains[1])
-        settle()
-    while len(chains[1][0]) <= steps:
-        advance(chains[1])
-    order = [
-        below[:steps] + [below[steps], above[steps]] + above[steps - 1 : 0 : -1]
-        for below, above in chains
-    ]
-    return partner, order[0], order[1]
+    below, above = [block], [block]
+    for k in range(1, steps):
+        below.append(shift(below[-1], "z", 1))
+        above.append(shift(above[-1], "z", -1))
+        if k == 1:
+            below[1], above[1], *beside = held(below[1], above[1], *beside)
+            later = then(beside)
+        if k == steps - 1:
+            below[k], above[k], *later = held(below[k], above[k], *later)
+    low = shift(below[-1][:rows], "z", 1)
+    high = shift(above[-1][rows:], "z", -1)
+    return below + [low, high] + above[:0:-1], later
+
+
+def weights_kernel(n_y, n_x, spot, *refs):
+    *blocks, out = refs
+    share = blocks[0].shape[2]
+    for i in range(n_y):
+        for d in range(n_x):
+            group = lax.rem(spot[0] + n_y - i, n_y) * n_x + lax.rem(spot[1] + n_x - d, n_x)
+            start = pl.multiple_of(group * share, share)
+            for m in range(4):
+                out[m, pl.ds(start, share), :] = blocks[d][i, m]
+
+
+def held(*values):
+    return lax.optimization_barrier(values)
 
 
 def per_device(tokens, grad_out, gates, expert_ids, w_up, w_down):
@@ -273,10 +257,27 @@
         cost_estimate=cost(0.1, 2),
         compiler_params=params(8),
     )(tokens, grad_out, gates, expert_ids)
-    pay_other, blocks_own, blocks_other = rings(pay)
+    spot = jnp.stack([yl, x, c]).astype(jnp.int32)
+    smem = [pl.BlockSpec(memory_space=pltpu.SMEM)]
+    gath = lax.all_gather(pay, "z", axis=0)
+    pay_other = shift(pay, "yh", 1)
     w_mine = jnp.concatenate((w_up, jnp.transpose(w_down, (0, 2, 1))), axis=0)
-    w_all = lax.all_gather(w_mine, ("yl", "x"), axis=0)
-    w_all = jnp.transpose(w_all, (1, 0, 2, 3)).reshape(4, width, hidden_len)
+    pay_other, w_mine = held(pay_other, w_mine)
+
+    def across(parts):
+        line = jnp.stack(parts)
+        return [line] + [shift(line, "x", d) for d in range(1, n_x)]
+
+    w_parts = [w_mine] + [shift(w_mine, "yl", d) for d in range(1, n_y)]
+    blocks_other, w_parts = ring(pay_other, w_parts, across)
+    w_all = pl.pallas_call(
+        functools.partial(weights_kernel, n_y, n_x),
+        out_shape=shape((4, width, hidden_len), BF),
+        in_specs=smem + vmem(n_x),
+        out_specs=vmem(1)[0],
+        cost_estimate=cost(0, 6),
+        compiler_params=params(10),
+    )(spot, *w_parts)
 
     j = jnp.arange(4 * block)
     b_j, d_j, r_j = j // block, (j % block) // cap, j % cap
@@ -286,77 +287,84 @@
     place = jnp.broadcast_to((r_j[:block, None] + 1).astype(F32), (block, 128))
     origin = jnp.broadcast_to(d_j[:block, None].astype(jnp.int32), (block, 128))
 
-    def picked(blocks, after=()):
+    def picked(*blocks):
         own, sib = pl.pallas_call(
             functools.partial(pick_kernel, cap, n_z),
             out_shape=(shape((2, block, 2 * width + 128), BF),) * 2,
-            in_specs=vmem(n_z + 4) + [pl.BlockSpec(memory_space=pl.ANY)] * len(after),
+            in_specs=vmem(len(blocks) + 3),
             out_specs=tuple(vmem(2)),
             cost_estimate=cost(2.6, 12),
-        compiler_params=params(20),
-        )(*blocks, sel, place, origin, *after)
+            compiler_params=params(20),
+        )(*blocks, sel, place, origin)
         return own, shift(sib, "c", 1)
 
     i = jnp.arange(2 * block)
     e_i, d_i, r_i = i // block, (i % block) // cap, i % cap
-    z_i = (z + n_z - d_i) % n_z
     p = jnp.arange(n_z * 2 * SLOTS)
     z_p, q_p = p // (2 * SLOTS), p % (2 * SLOTS)
-    same = z_p[:, None] == z_i[None, :]
     slot_i = (e_i * cap + r_i)[None, :]
-    perm_l = (same & (q_p[:, None] == slot_i)).astype(BF)
-    perm_r = (same & (q_p[:, None] == slot_i + SLOTS)).astype(BF)
-    perm_s = (same & (q_p[:, None] == 2 * cap)).astype(BF)
     lane_of = (slot_i.T == jnp.arange(128)[None, :]).astype(F32)
-    spot = jnp.stack([yl, x, c]).astype(jnp.int32)
-
-    def worked(own, got):
+
+    def worked(own, got, z_i):
+        same = z_p[:, None] == z_i[None, :]
+        perms = [
+            (same & (q_p[:, None] == at)).astype(BF) for at in (slot_i, slot_i + SLOTS, 2 * cap)
+        ]
         return pl.pallas_call(
             functools.partial(expert_kernel, cap),
             out_shape=(shape((n_z, 2, 2 * SLOTS, half), BF),)
             + (shape((2, 2 * block, hidden_len), BF),) * 2,
-            in_specs=[pl.BlockSpec(memory_space=pltpu.SMEM)] + vmem(7),
+            in_specs=smem + vmem(7),
             out_specs=tuple(vmem(3)),
             scratch_shapes=[
                 pltpu.VMEM((2, 2 * block, width), BF),
                 pltpu.VMEM((2, 2 * block, 128), BF),
             ],
             cost_estimate=cost(4, 24),
-        compiler_params=params(28),
-        )(spot, w_all, own, got, perm_l, perm_r, perm_s, lane_of)
+            compiler_params=params(28),
+        )(spot, w_all, own, got, *perms, lane_of)
 
     def replies(back):
         return lax.all_to_all(
             back.reshape(2 * n_z, 2 * SLOTS, half), ("z", "c"), 0, 0, tiled=True
         )
 
-    a_own, a_got = picked(blocks_own)
-    a_back, a_up, a_down = worked(a_own, a_got)
-    (a_back,) = together((a_back,), (blocks_other[n_z // 2 - 1], blocks_other[n_z // 2 + 2]))
-    got_own = replies(a_back)
-    b_own, b_got = picked(blocks_other, (a_up,))
-    b_back, b_up, b_down = worked(b_own, b_got)
+    second = (2, len(blocks_other) - 2) if n_z > 4 else (0, 1)
+    gath, *some = held(gath, *[blocks_other[i] for i in second])
+    for i, value in zip(second, some):
+        blocks_other[i] = value
+    a_own, a_got = picked(gath)
+    a_back, a_up, a_down = worked(a_own, a_got, d_i)
+    b_own, b_got = picked(*blocks_other)
+    a_up, b_got = held(a_up, b_got)
+    b_back, b_up, b_down = worked(b_own, b_got, (z + n_z - d_i) % n_z)
+    got_other = replies(b_back)
     parts = pl.pallas_call(
         functools.partial(weight_kernel, n_y, n_x),
-        out_shape=(shape((n_y, 4, share, hidden_len), BF),) * n_x,
-        in_specs=[pl.BlockSpec(memory_space=pltpu.SMEM)] + vmem(8),
-        out_specs=tuple(vmem(n_x)),
+        out_shape=(shape((n_y, 2, share, hidden_len), BF),) * (2 * n_x),
+        in_specs=smem + vmem(8),
+        out_specs=tuple(vmem(2 * n_x)),
         scratch_shapes=[pltpu.VMEM((n_y * n_x, 4, share, hidden_len), BF)],
         cost_estimate=cost(2, 18),
         compiler_params=params(28),
     )(spot, a_own, a_got, b_own, b_got, a_up, a_down, b_up, b_down)
-    (b_back,) = together((b_back,), (got_own, parts[0]))
-    got_other = replies(b_back)
-
-    lines = [parts[0]] + [shift(parts[d], "x", d) for d in range(1, n_x)]
-    line = sum(v.astype(F32) for v in lines).astype(BF)
-    ends = [line[0]] + [shift(line[d], "yl", d) for d in range(1, n_y)]
+
+    lines, ends = [], []
+    for e in range(2):
+        some = parts[e * n_x : (e + 1) * n_x]
+        some = [some[0]] + [shift(some[d], "x", d) for d in range(1, n_x)]
+        lines.append(sum(v.astype(F32) for v in some).astype(BF))
+    a_back, got_other, lines[0] = held(a_back, got_other, lines[0])
+    got_own = replies(a_back)
+    for e in range(2):
+        ends += [lines[e][0]] + [shift(lines[e][d], "yl", d) for d in range(1, n_y)]
+        lines[1], *ends = held(lines[1], *ends)
     grad_up, grad_down = pl.pallas_call(
         total_kernel,
         out_shape=(shape((2, share, hidden_len), BF),) * 2,
-        in_specs=vmem(n_y),
+        in_specs=vmem(2 * n_y),
         out_specs=tuple(vmem(2)),
-        cost_estimate=cost(0, 60),
+        cost_estimate=cost(0, 2),
         compiler_params=params(6),
     )(*ends)
     grad_down = jnp.transpose(grad_down, (0, 2, 1))

time: 338 us -> 297 us (0.88)
  the two profiles are of different devices: /device:TPU:23 before, /device:TPU:11 now
where the time goes in v3:
time: 297 us; the launch traced here: 295 us
  starting transfers between devices  121 us (41%)
  waiting for transfers between devices  95.1 us (32%)
  Pallas kernels  32.7 us (11%)
  local copies, waits for them, and re-layouts  27.3 us (9%)
  between operations  14.7 us (5%)
  other arithmetic  4.16 us (1%)
    ppermute x30, starting transfers between devices, shift(): return lax.ppermute(value, axis, [(i, (i + by) % n) for i in range(n)])  109 us
    ppermute x30, waiting for transfers between devices, shift(): return lax.ppermute(value, axis, [(i, (i + by) % n) for i in range(n)])  95.1 us
    unnamed x61, local copies, waits for them, and re-layouts  24.5 us
    all_to_all x2, starting transfers between devices, replies(): lax.all_to_all(back.reshape(2 * n_z, 2 * SLOTS, half), ('z', 'c'), 0, 0,...  12.4 us
    pallas_call x2, Pallas kernels, worked(): pl.pallas_call(functools.partial(expert_kernel, cap), out_shape=(shape((n...  11.6 us
    pallas_call x2, Pallas kernels, picked(): pl.pallas_call(functools.partial(pick_kernel, cap, n_z), out_shape=(shape...  9.67 us
    pallas_call x1, Pallas kernels, per_device(): pl.pallas_call(functools.partial(weight_kernel, n_y, n_x), out_shape=(sha...  5.96 us
  transfers between devices with their start and end apart: 33, of which 12 were waited for; matrix products, arithmetic and copies ran while one was open for 2% of the time, Pallas kernels for 8%

profile of v3, /device:TPU:11, one launch (start us, length us, event | category | flops | bytes accessed | tf_op | source)
XLA Modules:
  0.0 295.4 jit_solution(5009484268565594380)
XLA Ops:
  12.0 6.6 %collective-permute-start = (bf16[128,2176]{1,0:T(8,128)(2,1)}, bf16[128,2176]{1,0:T(8,128)(2,1)S(1)}, u32[]{:S(2)}, u32[]{:S(2)}) collective-permute-start(bf16[128,2176]{1,0:T(8,128)(2,1)} %get-tuple-element.63), channel_id=1, source_target_pairs={{0,2},{2,0},{1,3},{3,1},{4,6},{6,4},{5,7},{7,5},{8,10},{10,8},{9,1... | collective-permute-start | bytes 1671176 | tf_op jit(solution)/shard_map/ppermute | solution.py:205
  18.7 23.2 %collective-permute-done.refs_0_.pay = bf16[128,2176]{1,0:T(8,128)(2,1)S(1)} collective-permute-done((bf16[128,2176]{1,0:T(8,128)(2,1)}, bf16[128,2176]{1,0:T(8,128)(2,1)S(1)}, u32[]{:S(2)}, u32[]{:S(2)}) %collective-permute-start) | collective-permute-done | bytes 557088 | tf_op jit(solution)/shard_map/ppermute | solution.py:205
  41.9 4.0 %collective-permute-start.1 = (bf16[128,2176]{1,0:T(8,128)(2,1)S(1)}, bf16[128,2176]{1,0:T(8,128)(2,1)}, u32[]{:S(2)}, u32[]{:S(2)}) collective-permute-start(bf16[128,2176]{1,0:T(8,128)(2,1)S(1)} %collective-permute-done.refs_0_.pay), channel_id=1, source_target_pairs={{0,4},{4,8},{8,12},{12,16},{16,20},{20,24},{24,28},{28,0},{1,5},{5... | collective-permute-start | bytes 1671176 | tf_op jit(solution)/shard_map/ppermute | solution.py:205
  45.9 8.6 %collective-permute-start.2 = (bf16[128,2176]{1,0:T(8,128)(2,1)S(1)}, bf16[128,2176]{1,0:T(8,128)(2,1)}, u32[]{:S(2)}, u32[]{:S(2)}) collective-permute-start(bf16[128,2176]{1,0:T(8,128)(2,1)S(1)} %collective-permute-done.refs_0_.pay), channel_id=1, source_target_pairs={{0,28},{4,0},{8,4},{12,8},{16,12},{20,16},{24,20},{28,24},{1,29},{... | collective-permute-start | bytes 1671176 | tf_op jit(solution)/shard_map/ppermute | solution.py:205
  55.3 5.8 %collective-permute-start.3 = (bf16[4,64,384]{2,1,0:T(8,128)(2,1)S(1)}, bf16[4,64,384]{2,1,0:T(8,128)(2,1)S(1)}, u32[]{:S(2)}, u32[]{:S(2)}) collective-permute-start(bf16[4,64,384]{2,1,0:T(8,128)(2,1)S(1)} %pad_maximum_fusion.1), channel_id=1, source_target_pairs={{0,128},{128,256},{256,384},{384,0},{1,129},{129,257},{257,385},{3... | collective-permute-start | bytes 589832 | tf_op jit(solution)/shard_map/ppermute | solution.py:205
  61.2 1.9 collective-permute-start.4
  63.1 3.1 %collective-permute-start.5 = (bf16[4,64,384]{2,1,0:T(8,128)(2,1)S(1)}, bf16[4,64,384]{2,1,0:T(8,128)(2,1)S(1)}, u32[]{:S(2)}, u32[]{:S(2)}) collective-permute-start(bf16[4,64,384]{2,1,0:T(8,128)(2,1)S(1)} %pad_maximum_fusion.1), channel_id=1, source_target_pairs={{0,384},{128,0},{256,128},{384,256},{1,385},{129,1},{257,129},{385... | collective-permute-start | bytes 589832 | tf_op jit(solution)/shard_map/ppermute | solution.py:205
  66.2 10.8 %collective-permute-done.4 = bf16[4,64,384]{2,1,0:T(8,128)(2,1)S(1)} collective-permute-done((bf16[4,64,384]{2,1,0:T(8,128)(2,1)S(1)}, bf16[4,64,384]{2,1,0:T(8,128)(2,1)S(1)}, u32[]{:S(2)}, u32[]{:S(2)}) %collective-permute-start.4) | collective-permute-done | bytes 196640 | tf_op jit(solution)/shard_map/ppermute | solution.py:205
  78.7 1.9 collective-permute-start.6
  80.6 4.6 %collective-permute-start.8 = (bf16[128,2176]{1,0:T(8,128)(2,1)}, bf16[128,2176]{1,0:T(8,128)(2,1)}, u32[]{:S(2)}, u32[]{:S(2)}) collective-permute-start(bf16[128,2176]{1,0:T(8,128)(2,1)} %collective-permute-done.2.refs_8_), channel_id=1, source_target_pairs={{0,28},{4,0},{8,4},{12,8},{16,12},{20,16},{24,20},{28,24},{1,29},{... | collective-permute-start | bytes 1671176 | tf_op jit(solution)/shard_map/ppermute | solution.py:205
  85.4 3.1 %collective-permute-start.10 = (bf16[4,4,64,384]{3,2,1,0:T(8,128)(2,1)S(1)}, bf16[4,4,64,384]{3,2,1,0:T(8,128)(2,1)S(1)}, u32[]{:S(2)}, u32[]{:S(2)}) collective-permute-start(bf16[4,4,64,384]{3,2,1,0:T(8,128)(2,1)S(1)} %pad_maximum_fusion.refs_0_), channel_id=1, source_target_pairs={{0,32},{32,64},{64,96},{96,0},{1,33},{33,65},{65,97},{97,1},{2,34}... | collective-permute-start | bytes 2359304 | tf_op jit(solution)/shard_map/ppermute | solution.py:205
  88.5 2.7 collective-permute-start.11
  91.3 3.8 %collective-permute-start.12 = (bf16[4,4,64,384]{3,2,1,0:T(8,128)(2,1)S(1)}, bf16[4,4,64,384]{3,2,1,0:T(8,128)(2,1)S(1)}, u32[]{:S(2)}, u32[]{:S(2)}) collective-permute-start(bf16[4,4,64,384]{3,2,1,0:T(8,128)(2,1)S(1)} %pad_maximum_fusion.refs_0_), channel_id=1, source_target_pairs={{0,96},{32,0},{64,32},{96,64},{1,97},{33,1},{65,33},{97,65},{2,98}... | collective-permute-start | bytes 2359304 | tf_op jit(solution)/shard_map/ppermute | solution.py:205
  95.1 4.9 %collective-permute-done.6.refs_2_ = bf16[128,2176]{1,0:T(8,128)(2,1)} collective-permute-done((bf16[128,2176]{1,0:T(8,128)(2,1)}, bf16[128,2176]{1,0:T(8,128)(2,1)}, u32[]{:S(2)}, u32[]{:S(2)}) %collective-permute-start.6) | collective-permute-done | bytes 557088 | tf_op jit(solution)/shard_map/ppermute | solution.py:205
  100.0 1.9 collective-permute-start.7
  101.9 4.6 %collective-permute-start.9 = (bf16[128,2176]{1,0:T(8,128)(2,1)}, bf16[128,2176]{1,0:T(8,128)(2,1)S(1)}, u32[]{:S(2)}, u32[]{:S(2)}) collective-permute-start(bf16[128,2176]{1,0:T(8,128)(2,1)} %collective-permute-done.8.refs_7_), channel_id=1, source_target_pairs={{0,28},{4,0},{8,4},{12,8},{16,12},{20,16},{24,20},{28,24},{1,29},{... | collective-permute-start | bytes 1671176 | tf_op jit(solution)/shard_map/ppermute | solution.py:205
  107.5 20.7 %collective-permute-done.12.refs_3_ = bf16[4,4,64,384]{3,2,1,0:T(8,128)(2,1)S(1)} collective-permute-done((bf16[4,4,64,384]{3,2,1,0:T(8,128)(2,1)S(1)}, bf16[4,4,64,384]{3,2,1,0:T(8,128)(2,1)S(1)}, u32[]{:S(2)}, u32[]{:S(2)}) %collective-permute-start.12) | collective-permute-done | bytes 786464 | tf_op jit(solution)/shard_map/ppermute | solution.py:205
  129.8 1.9 collective-permute-start.14
  132.5 4.6 %collective-permute-start.15 = (bf16[64,2176]{1,0:T(8,128)(2,1)}, bf16[64,2176]{1,0:T(8,128)(2,1)}, u32[]{:S(2)}, u32[]{:S(2)}) collective-permute-start(bf16[64,2176]{1,0:T(8,128)(2,1)} %slice.43), channel_id=1, source_target_pairs={{0,28},{4,0},{8,4},{12,8},{16,12},{20,16},{24,20},{28,24},{1,29},{... | collective-permute-start | bytes 835592 | tf_op jit(solution)/shard_map/ppermute | solution.py:205
  138.3 2.3 copy-done.14
  140.6 4.0 %shard_map.95 = (bf16[2,144,2176]{2,1,0:T(8,128)(2,1)S(1)}, bf16[2,144,2176]{2,1,0:T(8,128)(2,1)}) custom-call(bf16[8,128,2176]{2,1,0:T(8,128)(2,1)S(1)} %bitcast.29, bf16[576,512]{1,0:T(8,128)(2,1)S(1)} %copy-done.1, f32[144,128]{1,0:T(8,128)S(1)} %broadcast_in_dim.24.refs_2_.refs_10_, s32[144,128]{1,0:T(8,128)S(1)} %broadcast_in_dim.25.refs_3_.refs_11_), custom_call_target="tpu_custom_call" | custom-call | flops 2600000000 | bytes 12582912 | tf_op jit(solution)/shard_map/pallas_call | solution.py:291
  145.6 3.0 collective-permute-start.13
  152.9 5.7 %shard_map.97 = (bf16[2,144,2176]{2,1,0:T(8,128)(2,1)S(1)}, bf16[2,144,2176]{2,1,0:T(8,128)(2,1)}) custom-call(bf16[128,2176]{1,0:T(8,128)(2,1)S(1)} %copy-done.4, bf16[128,2176]{1,0:T(8,128)(2,1)} %collective-permute-done.1.refs_1_, bf16[128,2176]{1,0:T(8,128)(2,1)} %collective-permute-done.6.refs_2_, bf16[128,2176]{1,0:T(8,128)(2,1)S(1)} %copy-done.11, ...), custom_call_target="tpu_custom_call" | custom-call | flops 2600000000 | bytes 12582912 | tf_op jit(solution)/shard_map/pallas_call | solution.py:291
  159.7 2.1 collective-permute-start.16
  164.4 5.3 %shard_map.96 = (bf16[8,2,80,512]{3,2,1,0:T(8,128)(2,1)S(1)}, bf16[2,288,384]{2,1,0:T(8,128)(2,1)S(1)}, bf16[2,288,384]{2,1,0:T(8,128)(2,1)S(1)}) custom-call(s32[3]{0:T(128)S(1)} %pad_add_fusion.spot, bf16[4,1024,384]{2,1,0:T(8,128)(2,1)S(1)} %shard_map.94.w_ref, bf16[2,144,2176]{2,1,0:T(8,128)(2,1)S(1)} %copy-done.16, ...), custom_call_target="tpu_custom_call" | custom-call | flops 4000000000 | bytes 25165824 | tf_op jit(solution)/shard_map/pallas_call | solution.py:313
  171.5 6.3 %shard_map.98 = (bf16[8,2,80,512]{3,2,1,0:T(8,128)(2,1)}, bf16[2,288,384]{2,1,0:T(8,128)(2,1)S(1)}, bf16[2,288,384]{2,1,0:T(8,128)(2,1)S(1)}) custom-call(s32[3]{0:T(128)S(1)} %pad_add_fusion.spot, bf16[4,1024,384]{2,1,0:T(8,128)(2,1)S(1)} %shard_map.94.w_ref, bf16[2,144,2176]{2,1,0:T(8,128)(2,1)S(1)} %copy-done.19, ...), custom_call_target="tpu_custom_call" | custom-call | flops 4000000000 | bytes 25165824 | tf_op jit(solution)/shard_map/pallas_call | solution.py:313
  179.4 5.1 %all-to-all-start = ((bf16[16,80,512]{2,1,0:T(8,128)(2,1)}), bf16[16,80,512]{2,1,0:T(8,128)(2,1)S(1)}, u32[]{:S(2)}, u32[]{:S(2)}) async-start(bf16[16,80,512]{2,1,0:T(8,128)(2,1)} %bitcast.9), calls=%async_computation | async-start | bytes 2621440 | tf_op jit(solution)/shard_map/all_to_all | solution.py:328
  188.9 6.0 %shard_map.99 = (bf16[4,2,64,384]{3,2,1,0:T(8,128)(2,1)S(1)}, bf16[4,2,64,384]{3,2,1,0:T(8,128)(2,1)S(1)}, bf16[4,2,64,384]{3,2,1,0:T(8,128)(2,1)S(1)}, bf16[4,2...) custom-call(s32[3]{0:T(128)S(1)} %pad_add_fusion.spot, ...), custom_call_target="tpu_custom_call" | custom-call | flops 2000000000 | bytes 18874368 | tf_op jit(solution)/shard_map/pallas_call | solution.py:342
  195.7 2.2 collective-permute-start.17
  197.9 2.7 collective-permute-start.18
  200.7 3.7 %collective-permute-start.19 = (bf16[4,2,64,384]{3,2,1,0:T(8,128)(2,1)S(1)}, bf16[4,2,64,384]{3,2,1,0:T(8,128)(2,1)S(1)}, u32[]{:S(2)}, u32[]{:S(2)}) collective-permute-start(bf16[4,2,64,384]{3,2,1,0:T(8,128)(2,1)S(1)} %get-tuple-element.96), channel_id=1, source_target_pairs={{0,96},{32,0},{64,32},{96,64},{1,97},{33,1},{65,33},{97,65},{2,98}... | collective-permute-start | bytes 1179656 | tf_op jit(solution)/shard_map/ppermute | solution.py:205
  204.4 3.8 %collective-permute-done.17 = bf16[4,2,64,384]{3,2,1,0:T(8,128)(2,1)S(1)} collective-permute-done((bf16[4,2,64,384]{3,2,1,0:T(8,128)(2,1)S(1)}, bf16[4,2,64,384]{3,2,1,0:T(8,128)(2,1)S(1)}, u32[]{:S(2)}, u32[]{:S(2)}) %collective-permute-start.17) | collective-permute-done | bytes 393248 | tf_op jit(solution)/shard_map/ppermute | solution.py:205
  208.2 3.5 %collective-permute-done.18 = bf16[4,2,64,384]{3,2,1,0:T(8,128)(2,1)S(1)} collective-permute-done((bf16[4,2,64,384]{3,2,1,0:T(8,128)(2,1)S(1)}, bf16[4,2,64,384]{3,2,1,0:T(8,128)(2,1)S(1)}, u32[]{:S(2)}, u32[]{:S(2)}) %collective-permute-start.18) | collective-permute-done | bytes 393248 | tf_op jit(solution)/shard_map/ppermute | solution.py:205
  211.7 9.1 %collective-permute-done.19 = bf16[4,2,64,384]{3,2,1,0:T(8,128)(2,1)S(1)} collective-permute-done((bf16[4,2,64,384]{3,2,1,0:T(8,128)(2,1)S(1)}, bf16[4,2,64,384]{3,2,1,0:T(8,128)(2,1)S(1)}, u32[]{:S(2)}, u32[]{:S(2)}) %collective-permute-start.19) | collective-permute-done | bytes 393248 | tf_op jit(solution)/shard_map/ppermute | solution.py:205
  221.7 7.3 %all-to-all-start.1 = ((bf16[16,80,512]{2,1,0:T(8,128)(2,1)}), bf16[16,80,512]{2,1,0:T(8,128)(2,1)S(1)}, u32[]{:S(2)}, u32[]{:S(2)}) async-start(bf16[16,80,512]{2,1,0:T(8,128)(2,1)} %bitcast.28), calls=%async_computation.1 | async-start | bytes 2621440 | tf_op jit(solution)/shard_map/all_to_all | solution.py:328
  229.3 2.3 collective-permute-start.21
  231.6 2.7 collective-permute-start.22
  234.3 3.7 %collective-permute-start.23 = (bf16[4,2,64,384]{3,2,1,0:T(8,128)(2,1)}, bf16[4,2,64,384]{3,2,1,0:T(8,128)(2,1)S(1)}, u32[]{:S(2)}, u32[]{:S(2)}) collective-permute-start(bf16[4,2,64,384]{3,2,1,0:T(8,128)(2,1)} %get-tuple-element.105), channel_id=1, source_target_pairs={{0,96},{32,0},{64,32},{96,64},{1,97},{33,1},{65,33},{97,65},{2,98}... | collective-permute-start | bytes 1179656 | tf_op jit(solution)/shard_map/ppermute | solution.py:205
  239.3 6.1 %collective-permute-start.24 = (bf16[2,64,384]{2,1,0:T(8,128)(2,1)S(1)}, bf16[2,64,384]{2,1,0:T(8,128)(2,1)S(1)}, u32[]{:S(2)}, u32[]{:S(2)}) collective-permute-start(bf16[2,64,384]{2,1,0:T(8,128)(2,1)S(1)} %get-tuple-element.136), channel_id=1, source_target_pairs={{0,128},{128,256},{256,384},{384,0},{1,129},{129,257},{257,385},{3... | collective-permute-start | bytes 294920 | tf_op jit(solution)/shard_map/ppermute | solution.py:205
  245.3 1.9 collective-permute-start.25
  247.3 3.1 %collective-permute-start.26 = (bf16[2,64,384]{2,1,0:T(8,128)(2,1)S(1)}, bf16[2,64,384]{2,1,0:T(8,128)(2,1)S(1)}, u32[]{:S(2)}, u32[]{:S(2)}) collective-permute-start(bf16[2,64,384]{2,1,0:T(8,128)(2,1)S(1)} %get-tuple-element.134), channel_id=1, source_target_pairs={{0,384},{128,0},{256,128},{384,256},{1,385},{129,1},{257,129},{385... | collective-permute-start | bytes 294920 | tf_op jit(solution)/shard_map/ppermute | solution.py:205
  250.4 4.3 %collective-permute-done.23 = bf16[4,2,64,384]{3,2,1,0:T(8,128)(2,1)S(1)} collective-permute-done((bf16[4,2,64,384]{3,2,1,0:T(8,128)(2,1)}, bf16[4,2,64,384]{3,2,1,0:T(8,128)(2,1)S(1)}, u32[]{:S(2)}, u32[]{:S(2)}) %collective-permute-start.23) | collective-permute-done | bytes 393248 | tf_op jit(solution)/shard_map/ppermute | solution.py:205
  255.8 6.7 %collective-permute-start.20 = (bf16[128,1152]{1,0:T(8,128)(2,1)S(1)}, bf16[128,1152]{1,0:T(8,128)(2,1)S(1)}, u32[]{:S(2)}, u32[]{:S(2)}) collective-permute-start(bf16[128,1152]{1,0:T(8,128)(2,1)S(1)} %shard_map.100), channel_id=1, source_target_pairs={{0,2},{2,0},{1,3},{3,1},{4,6},{6,4},{5,7},{7,5},{8,10},{10,8},{9,1... | collective-permute-start | bytes 884744 | tf_op jit(solution)/shard_map/ppermute | solution.py:205
  262.5 3.5 %collective-permute-start.27 = (bf16[2,64,384]{2,1,0:T(8,128)(2,1)S(1)}, bf16[2,64,384]{2,1,0:T(8,128)(2,1)S(1)}, u32[]{:S(2)}, u32[]{:S(2)}) collective-permute-start(bf16[2,64,384]{2,1,0:T(8,128)(2,1)S(1)} %get-tuple-element.132), channel_id=1, source_target_pairs={{0,128},{128,256},{256,384},{384,0},{1,129},{129,257},{257,385},{3... | collective-permute-start | bytes 294920 | tf_op jit(solution)/shard_map/ppermute | solution.py:205
  266.1 2.9 collective-permute-start.28
  269.0 3.4 %collective-permute-start.29 = (bf16[2,64,384]{2,1,0:T(8,128)(2,1)S(1)}, bf16[2,64,384]{2,1,0:T(8,128)(2,1)S(1)}, u32[]{:S(2)}, u32[]{:S(2)}) collective-permute-start(bf16[2,64,384]{2,1,0:T(8,128)(2,1)S(1)} %get-tuple-element.130), channel_id=1, source_target_pairs={{0,384},{128,0},{256,128},{384,256},{1,385},{129,1},{257,129},{385... | collective-permute-start | bytes 294920 | tf_op jit(solution)/shard_map/ppermute | solution.py:205
  274.3 6.3 %collective-permute-done.28.refs_6_ = bf16[2,64,384]{2,1,0:T(8,128)(2,1)S(1)} collective-permute-done((bf16[2,64,384]{2,1,0:T(8,128)(2,1)S(1)}, bf16[2,64,384]{2,1,0:T(8,128)(2,1)S(1)}, u32[]{:S(2)}, u32[]{:S(2)}) %collective-permute-start.28) | collective-permute-done | bytes 98336 | tf_op jit(solution)/shard_map/ppermute | solution.py:205
  280.6 4.9 %collective-permute-done.29.refs_7_ = bf16[2,64,384]{2,1,0:T(8,128)(2,1)S(1)} collective-permute-done((bf16[2,64,384]{2,1,0:T(8,128)(2,1)S(1)}, bf16[2,64,384]{2,1,0:T(8,128)(2,1)S(1)}, u32[]{:S(2)}, u32[]{:S(2)}) %collective-permute-start.29) | collective-permute-done | bytes 98336 | tf_op jit(solution)/shard_map/ppermute | solution.py:205
  (126 shorter events, 38.2 us)
Async XLA Ops:
  7.2 11.4 %copy-start.27 = (bf16[2,384,64]{1,2,0:T(8,128)(2,1)S(1)}, bf16[2,384,64]{1,2,0:T(8,128)(2,1)}, u32[]{:S(2)}) copy-start(bf16[2,384,64]{1,2,0:T(8,128)(2,1)} %param.11) | copy-start | bytes 294916
  7.2 129.9 %all-gather.3.cloned.1.call-start = ((), (), s32[]{:S(2)}) async-start(), calls=%async_computation.2 | async-start | bytes 5013504 | tf_op jit(solution)/shard_map/all_gather | solution.py:262
  10.7 7.9 %copy-start.28 = (bf16[2,64,384]{2,1,0:T(8,128)(2,1)S(1)}, bf16[2,64,384]{2,1,0:T(8,128)(2,1)}, u32[]{:S(2)}) copy-start(bf16[2,64,384]{2,1,0:T(8,128)(2,1)} %param.10) | copy-start | bytes 294916
  12.0 29.9 %collective-permute-start = (bf16[128,2176]{1,0:T(8,128)(2,1)}, bf16[128,2176]{1,0:T(8,128)(2,1)S(1)}, u32[]{:S(2)}, u32[]{:S(2)}) collective-permute-start(bf16[128,2176]{1,0:T(8,128)(2,1)} %get-tuple-element.63), channel_id=1, source_target_pairs={{0,2},{2,0},{1,3},{3,1},{4,6},{6,4},{5,7},{7,5},{8,10},{10,8},{9,1... | collective-permute-start | bytes 1671176 | tf_op jit(solution)/shard_map/ppermute | solution.py:205
  41.9 36.8 %collective-permute-start.1 = (bf16[128,2176]{1,0:T(8,128)(2,1)S(1)}, bf16[128,2176]{1,0:T(8,128)(2,1)}, u32[]{:S(2)}, u32[]{:S(2)}) collective-permute-start(bf16[128,2176]{1,0:T(8,128)(2,1)S(1)} %collective-permute-done.refs_0_.pay), channel_id=1, source_target_pairs={{0,4},{4,8},{8,12},{12,16},{16,20},{20,24},{24,28},{28,0},{1,5},{5... | collective-permute-start | bytes 1671176 | tf_op jit(solution)/shard_map/ppermute | solution.py:205
  45.9 32.8 %collective-permute-start.2 = (bf16[128,2176]{1,0:T(8,128)(2,1)S(1)}, bf16[128,2176]{1,0:T(8,128)(2,1)}, u32[]{:S(2)}, u32[]{:S(2)}) collective-permute-start(bf16[128,2176]{1,0:T(8,128)(2,1)S(1)} %collective-permute-done.refs_0_.pay), channel_id=1, source_target_pairs={{0,28},{4,0},{8,4},{12,8},{16,12},{20,16},{24,20},{28,24},{1,29},{... | collective-permute-start | bytes 1671176 | tf_op jit(solution)/shard_map/ppermute | solution.py:205
  55.3 10.9 %collective-permute-start.3 = (bf16[4,64,384]{2,1,0:T(8,128)(2,1)S(1)}, bf16[4,64,384]{2,1,0:T(8,128)(2,1)S(1)}, u32[]{:S(2)}, u32[]{:S(2)}) collective-permute-start(bf16[4,64,384]{2,1,0:T(8,128)(2,1)S(1)} %pad_maximum_fusion.1), channel_id=1, source_target_pairs={{0,128},{128,256},{256,384},{384,0},{1,129},{129,257},{257,385},{3... | collective-permute-start | bytes 589832 | tf_op jit(solution)/shard_map/ppermute | solution.py:205
  61.2 15.9 %collective-permute-start.4 = (bf16[4,64,384]{2,1,0:T(8,128)(2,1)S(1)}, bf16[4,64,384]{2,1,0:T(8,128)(2,1)S(1)}, u32[]{:S(2)}, u32[]{:S(2)}) collective-permute-start(bf16[4,64,384]{2,1,0:T(8,128)(2,1)S(1)} %pad_maximum_fusion.1), channel_id=1, source_target_pairs={{0,256},{128,384},{256,0},{384,128},{1,257},{129,385},{257,1},{385... | collective-permute-start | bytes 589832 | tf_op jit(solution)/shard_map/ppermute | solution.py:205
  63.1 15.6 %collective-permute-start.5 = (bf16[4,64,384]{2,1,0:T(8,128)(2,1)S(1)}, bf16[4,64,384]{2,1,0:T(8,128)(2,1)S(1)}, u32[]{:S(2)}, u32[]{:S(2)}) collective-permute-start(bf16[4,64,384]{2,1,0:T(8,128)(2,1)S(1)} %pad_maximum_fusion.1), channel_id=1, source_target_pairs={{0,384},{128,0},{256,128},{384,256},{1,385},{129,1},{257,129},{385... | collective-permute-start | bytes 589832 | tf_op jit(solution)/shard_map/ppermute | solution.py:205
  78.7 21.3 %collective-permute-start.6 = (bf16[128,2176]{1,0:T(8,128)(2,1)}, bf16[128,2176]{1,0:T(8,128)(2,1)}, u32[]{:S(2)}, u32[]{:S(2)}) collective-permute-start(bf16[128,2176]{1,0:T(8,128)(2,1)} %collective-permute-done.1.refs_1_), channel_id=1, source_target_pairs={{0,4},{4,8},{8,12},{12,16},{16,20},{20,24},{24,28},{28,0},{1,5},{5... | collective-permute-start | bytes 1671176 | tf_op jit(solution)/shard_map/ppermute | solution.py:205
  80.6 21.3 %collective-permute-start.8 = (bf16[128,2176]{1,0:T(8,128)(2,1)}, bf16[128,2176]{1,0:T(8,128)(2,1)}, u32[]{:S(2)}, u32[]{:S(2)}) collective-permute-start(bf16[128,2176]{1,0:T(8,128)(2,1)} %collective-permute-done.2.refs_8_), channel_id=1, source_target_pairs={{0,28},{4,0},{8,4},{12,8},{16,12},{20,16},{24,20},{28,24},{1,29},{... | collective-permute-start | bytes 1671176 | tf_op jit(solution)/shard_map/ppermute | solution.py:205
  85.4 22.1 %collective-permute-start.10 = (bf16[4,4,64,384]{3,2,1,0:T(8,128)(2,1)S(1)}, bf16[4,4,64,384]{3,2,1,0:T(8,128)(2,1)S(1)}, u32[]{:S(2)}, u32[]{:S(2)}) collective-permute-start(bf16[4,4,64,384]{3,2,1,0:T(8,128)(2,1)S(1)} %pad_maximum_fusion.refs_0_), channel_id=1, source_target_pairs={{0,32},{32,64},{64,96},{96,0},{1,33},{33,65},{65,97},{97,1},{2,34}... | collective-permute-start | bytes 2359304 | tf_op jit(solution)/shard_map/ppermute | solution.py:205
  88.5 19.0 %collective-permute-start.11 = (bf16[4,4,64,384]{3,2,1,0:T(8,128)(2,1)S(1)}, bf16[4,4,64,384]{3,2,1,0:T(8,128)(2,1)S(1)}, u32[]{:S(2)}, u32[]{:S(2)}) collective-permute-start(bf16[4,4,64,384]{3,2,1,0:T(8,128)(2,1)S(1)} %pad_maximum_fusion.refs_0_), channel_id=1, source_target_pairs={{0,64},{32,96},{64,0},{96,32},{1,65},{33,97},{65,1},{97,33},{2,66}... | collective-permute-start | bytes 2359304 | tf_op jit(solution)/shard_map/ppermute | solution.py:205
  91.3 37.0 %collective-permute-start.12 = (bf16[4,4,64,384]{3,2,1,0:T(8,128)(2,1)S(1)}, bf16[4,4,64,384]{3,2,1,0:T(8,128)(2,1)S(1)}, u32[]{:S(2)}, u32[]{:S(2)}) collective-permute-start(bf16[4,4,64,384]{3,2,1,0:T(8,128)(2,1)S(1)} %pad_maximum_fusion.refs_0_), channel_id=1, source_target_pairs={{0,96},{32,0},{64,32},{96,64},{1,97},{33,1},{65,33},{97,65},{2,98}... | collective-permute-start | bytes 2359304 | tf_op jit(solution)/shard_map/ppermute | solution.py:205
  100.0 28.3 %collective-permute-start.7 = (bf16[128,2176]{1,0:T(8,128)(2,1)}, bf16[128,2176]{1,0:T(8,128)(2,1)S(1)}, u32[]{:S(2)}, u32[]{:S(2)}) collective-permute-start(bf16[128,2176]{1,0:T(8,128)(2,1)} %collective-permute-done.6.refs_2_), channel_id=1, source_target_pairs={{0,4},{4,8},{8,12},{12,16},{16,20},{20,24},{24,28},{28,0},{1,5},{5... | collective-permute-start | bytes 1671176 | tf_op jit(solution)/shard_map/ppermute | solution.py:205
  101.9 26.3 %collective-permute-start.9 = (bf16[128,2176]{1,0:T(8,128)(2,1)}, bf16[128,2176]{1,0:T(8,128)(2,1)S(1)}, u32[]{:S(2)}, u32[]{:S(2)}) collective-permute-start(bf16[128,2176]{1,0:T(8,128)(2,1)} %collective-permute-done.8.refs_7_), channel_id=1, source_target_pairs={{0,28},{4,0},{8,4},{12,8},{16,12},{20,16},{24,20},{28,24},{1,29},{... | collective-permute-start | bytes 1671176 | tf_op jit(solution)/shard_map/ppermute | solution.py:205
  128.2 3.5 %copy-start.12 = (bf16[128,2176]{1,0:T(8,128)(2,1)}, bf16[128,2176]{1,0:T(8,128)(2,1)S(1)}, u32[]{:S(2)}) copy-start(bf16[128,2176]{1,0:T(8,128)(2,1)S(1)} %collective-permute-done.9.refs_6_) | copy-start | bytes 1671172
  129.8 18.8 %collective-permute-start.14 = (bf16[64,2176]{1,0:T(8,128)(2,1)}, bf16[64,2176]{1,0:T(8,128)(2,1)}, u32[]{:S(2)}, u32[]{:S(2)}) collective-permute-start(bf16[64,2176]{1,0:T(8,128)(2,1)} %slice.42), channel_id=1, source_target_pairs={{0,4},{4,8},{8,12},{12,16},{16,20},{20,24},{24,28},{28,0},{1,5},{5... | collective-permute-start | bytes 835592 | tf_op jit(solution)/shard_map/ppermute | solution.py:205
  132.5 16.1 %collective-permute-start.15 = (bf16[64,2176]{1,0:T(8,128)(2,1)}, bf16[64,2176]{1,0:T(8,128)(2,1)}, u32[]{:S(2)}, u32[]{:S(2)}) collective-permute-start(bf16[64,2176]{1,0:T(8,128)(2,1)} %slice.43), channel_id=1, source_target_pairs={{0,28},{4,0},{8,4},{12,8},{16,12},{20,16},{24,20},{28,24},{1,29},{... | collective-permute-start | bytes 835592 | tf_op jit(solution)/shard_map/ppermute | solution.py:205
  137.2 1.1 copy-start.1
  138.3 2.3 copy-start.14
  144.6 1.1 copy-start.15
  145.6 18.3 %collective-permute-start.13 = (bf16[2,144,2176]{2,1,0:T(8,128)(2,1)}, bf16[2,144,2176]{2,1,0:T(8,128)(2,1)}, u32[]{:S(2)}, u32[]{:S(2)}) collective-permute-start(bf16[2,144,2176]{2,1,0:T(8,128)(2,1)} %get-tuple-element.78), channel_id=1, source_target_pairs={{0,1},{1,0},{2,3},{3,2},{4,5},{5,4},{6,7},{7,6},{8,9},{9,8},{10,11... | collective-permute-start | bytes 3760136 | tf_op jit(solution)/shard_map/ppermute | solution.py:205
  148.6 1.1 copy-start.2
  158.6 1.1 copy-start.18
  159.7 11.8 %collective-permute-start.16 = (bf16[2,144,2176]{2,1,0:T(8,128)(2,1)}, bf16[2,144,2176]{2,1,0:T(8,128)(2,1)}, u32[]{:S(2)}, u32[]{:S(2)}) collective-permute-start(bf16[2,144,2176]{2,1,0:T(8,128)(2,1)} %get-tuple-element.86), channel_id=1, source_target_pairs={{0,1},{1,0},{2,3},{3,2},{4,5},{5,4},{6,7},{7,6},{8,9},{9,8},{10,11... | collective-permute-start | bytes 3760136 | tf_op jit(solution)/shard_map/ppermute | solution.py:205
  163.1 1.3 copy-start.16
  164.4 7.2 %copy-start.19 = (bf16[2,144,2176]{2,1,0:T(8,128)(2,1)S(1)}, bf16[2,144,2176]{2,1,0:T(8,128)(2,1)}, u32[]{:S(2)}) copy-start(bf16[2,144,2176]{2,1,0:T(8,128)(2,1)} %copy-done.18) | copy-start | bytes 3760132
  169.7 1.1 copy-start
  179.4 5.2 %copy-start.17 = (bf16[2,144,2176]{2,1,0:T(8,128)(2,1)S(1)}, bf16[2,144,2176]{2,1,0:T(8,128)(2,1)}, u32[]{:S(2)}) copy-start(bf16[2,144,2176]{2,1,0:T(8,128)(2,1)} %copy-done.15) | copy-start | bytes 3760132
  179.4 42.3 %all-to-all-start = ((bf16[16,80,512]{2,1,0:T(8,128)(2,1)}), bf16[16,80,512]{2,1,0:T(8,128)(2,1)S(1)}, u32[]{:S(2)}, u32[]{:S(2)}) async-start(bf16[16,80,512]{2,1,0:T(8,128)(2,1)} %bitcast.9), calls=%async_computation | async-start | bytes 2621440 | tf_op jit(solution)/shard_map/all_to_all | solution.py:328
  184.6 1.3 copy-start.20
  195.7 12.6 %collective-permute-start.17 = (bf16[4,2,64,384]{3,2,1,0:T(8,128)(2,1)S(1)}, bf16[4,2,64,384]{3,2,1,0:T(8,128)(2,1)S(1)}, u32[]{:S(2)}, u32[]{:S(2)}) collective-permute-start(bf16[4,2,64,384]{3,2,1,0:T(8,128)(2,1)S(1)} %get-tuple-element.94), channel_id=1, source_target_pairs={{0,32},{32,64},{64,96},{96,0},{1,33},{33,65},{65,97},{97,1},{2,34}... | collective-permute-start | bytes 1179656 | tf_op jit(solution)/shard_map/ppermute | solution.py:205
  197.9 13.8 %collective-permute-start.18 = (bf16[4,2,64,384]{3,2,1,0:T(8,128)(2,1)S(1)}, bf16[4,2,64,384]{3,2,1,0:T(8,128)(2,1)S(1)}, u32[]{:S(2)}, u32[]{:S(2)}) collective-permute-start(bf16[4,2,64,384]{3,2,1,0:T(8,128)(2,1)S(1)} %get-tuple-element.95), channel_id=1, source_target_pairs={{0,64},{32,96},{64,0},{96,32},{1,65},{33,97},{65,1},{97,33},{2,66}... | collective-permute-start | bytes 1179656 | tf_op jit(solution)/shard_map/ppermute | solution.py:205
  200.7 20.1 %collective-permute-start.19 = (bf16[4,2,64,384]{3,2,1,0:T(8,128)(2,1)S(1)}, bf16[4,2,64,384]{3,2,1,0:T(8,128)(2,1)S(1)}, u32[]{:S(2)}, u32[]{:S(2)}) collective-permute-start(bf16[4,2,64,384]{3,2,1,0:T(8,128)(2,1)S(1)} %get-tuple-element.96), channel_id=1, source_target_pairs={{0,96},{32,0},{64,32},{96,64},{1,97},{33,1},{65,33},{97,65},{2,98}... | collective-permute-start | bytes 1179656 | tf_op jit(solution)/shard_map/ppermute | solution.py:205
  221.7 64.5 %all-to-all-start.1 = ((bf16[16,80,512]{2,1,0:T(8,128)(2,1)}), bf16[16,80,512]{2,1,0:T(8,128)(2,1)S(1)}, u32[]{:S(2)}, u32[]{:S(2)}) async-start(bf16[16,80,512]{2,1,0:T(8,128)(2,1)} %bitcast.28), calls=%async_computation.1 | async-start | bytes 2621440 | tf_op jit(solution)/shard_map/all_to_all | solution.py:328
  229.1 25.6 %copy-start.7 = (bf16[4,2,64,384]{3,2,1,0:T(8,128)(2,1)S(1)}, bf16[4,2,64,384]{3,2,1,0:T(8,128)(2,1)}, u32[]{:S(2)}) copy-start(bf16[4,2,64,384]{3,2,1,0:T(8,128)(2,1)} %copy-done.6) | copy-start | bytes 1179652
  229.3 18.0 %collective-permute-start.21 = (bf16[4,2,64,384]{3,2,1,0:T(8,128)(2,1)}, bf16[4,2,64,384]{3,2,1,0:T(8,128)(2,1)S(1)}, u32[]{:S(2)}, u32[]{:S(2)}) collective-permute-start(bf16[4,2,64,384]{3,2,1,0:T(8,128)(2,1)} %get-tuple-element.103), channel_id=1, source_target_pairs={{0,32},{32,64},{64,96},{96,0},{1,33},{33,65},{65,97},{97,1},{2,34}... | collective-permute-start | bytes 1179656 | tf_op jit(solution)/shard_map/ppermute | solution.py:205
  231.6 18.8 %collective-permute-start.22 = (bf16[4,2,64,384]{3,2,1,0:T(8,128)(2,1)}, bf16[4,2,64,384]{3,2,1,0:T(8,128)(2,1)S(1)}, u32[]{:S(2)}, u32[]{:S(2)}) collective-permute-start(bf16[4,2,64,384]{3,2,1,0:T(8,128)(2,1)} %get-tuple-element.104), channel_id=1, source_target_pairs={{0,64},{32,96},{64,0},{96,32},{1,65},{33,97},{65,1},{97,33},{2,66}... | collective-permute-start | bytes 1179656 | tf_op jit(solution)/shard_map/ppermute | solution.py:205
  234.3 20.3 %collective-permute-start.23 = (bf16[4,2,64,384]{3,2,1,0:T(8,128)(2,1)}, bf16[4,2,64,384]{3,2,1,0:T(8,128)(2,1)S(1)}, u32[]{:S(2)}, u32[]{:S(2)}) collective-permute-start(bf16[4,2,64,384]{3,2,1,0:T(8,128)(2,1)} %get-tuple-element.105), channel_id=1, source_target_pairs={{0,96},{32,0},{64,32},{96,64},{1,97},{33,1},{65,33},{97,65},{2,98}... | collective-permute-start | bytes 1179656 | tf_op jit(solution)/shard_map/ppermute | solution.py:205
  238.1 16.8 %copy-start.5 = (bf16[128,2176]{1,0:T(8,128)(2,1)S(1)}, bf16[128,2176]{1,0:T(8,128)(2,1)}, u32[]{:S(2)}) copy-start(bf16[128,2176]{1,0:T(8,128)(2,1)} %copy-done.3) | copy-start | bytes 1671172
  239.3 23.2 %collective-permute-start.24 = (bf16[2,64,384]{2,1,0:T(8,128)(2,1)S(1)}, bf16[2,64,384]{2,1,0:T(8,128)(2,1)S(1)}, u32[]{:S(2)}, u32[]{:S(2)}) collective-permute-start(bf16[2,64,384]{2,1,0:T(8,128)(2,1)S(1)} %get-tuple-element.136), channel_id=1, source_target_pairs={{0,128},{128,256},{256,384},{384,0},{1,129},{129,257},{257,385},{3... | collective-permute-start | bytes 294920 | tf_op jit(solution)/shard_map/ppermute | solution.py:205
  245.3 17.1 %collective-permute-start.25 = (bf16[2,64,384]{2,1,0:T(8,128)(2,1)S(1)}, bf16[2,64,384]{2,1,0:T(8,128)(2,1)S(1)}, u32[]{:S(2)}, u32[]{:S(2)}) collective-permute-start(bf16[2,64,384]{2,1,0:T(8,128)(2,1)S(1)} %get-tuple-element.135), channel_id=1, source_target_pairs={{0,256},{128,384},{256,0},{384,128},{1,257},{129,385},{257,1},{385... | collective-permute-start | bytes 294920 | tf_op jit(solution)/shard_map/ppermute | solution.py:205
  247.3 15.2 %collective-permute-start.26 = (bf16[2,64,384]{2,1,0:T(8,128)(2,1)S(1)}, bf16[2,64,384]{2,1,0:T(8,128)(2,1)S(1)}, u32[]{:S(2)}, u32[]{:S(2)}) collective-permute-start(bf16[2,64,384]{2,1,0:T(8,128)(2,1)S(1)} %get-tuple-element.134), channel_id=1, source_target_pairs={{0,384},{128,0},{256,128},{384,256},{1,385},{129,1},{257,129},{385... | collective-permute-start | bytes 294920 | tf_op jit(solution)/shard_map/ppermute | solution.py:205
  255.8 30.5 %collective-permute-start.20 = (bf16[128,1152]{1,0:T(8,128)(2,1)S(1)}, bf16[128,1152]{1,0:T(8,128)(2,1)S(1)}, u32[]{:S(2)}, u32[]{:S(2)}) collective-permute-start(bf16[128,1152]{1,0:T(8,128)(2,1)S(1)} %shard_map.100), channel_id=1, source_target_pairs={{0,2},{2,0},{1,3},{3,1},{4,6},{6,4},{5,7},{7,5},{8,10},{10,8},{9,1... | collective-permute-start | bytes 884744 | tf_op jit(solution)/shard_map/ppermute | solution.py:205
  262.5 11.8 %collective-permute-start.27 = (bf16[2,64,384]{2,1,0:T(8,128)(2,1)S(1)}, bf16[2,64,384]{2,1,0:T(8,128)(2,1)S(1)}, u32[]{:S(2)}, u32[]{:S(2)}) collective-permute-start(bf16[2,64,384]{2,1,0:T(8,128)(2,1)S(1)} %get-tuple-element.132), channel_id=1, source_target_pairs={{0,128},{128,256},{256,384},{384,0},{1,129},{129,257},{257,385},{3... | collective-permute-start | bytes 294920 | tf_op jit(solution)/shard_map/ppermute | solution.py:205
  266.1 14.6 %collective-permute-start.28 = (bf16[2,64,384]{2,1,0:T(8,128)(2,1)S(1)}, bf16[2,64,384]{2,1,0:T(8,128)(2,1)S(1)}, u32[]{:S(2)}, u32[]{:S(2)}) collective-permute-start(bf16[2,64,384]{2,1,0:T(8,128)(2,1)S(1)} %get-tuple-element.131), channel_id=1, source_target_pairs={{0,256},{128,384},{256,0},{384,128},{1,257},{129,385},{257,1},{385... | collective-permute-start | bytes 294920 | tf_op jit(solution)/shard_map/ppermute | solution.py:205
  269.0 16.5 %collective-permute-start.29 = (bf16[2,64,384]{2,1,0:T(8,128)(2,1)S(1)}, bf16[2,64,384]{2,1,0:T(8,128)(2,1)S(1)}, u32[]{:S(2)}, u32[]{:S(2)}) collective-permute-start(bf16[2,64,384]{2,1,0:T(8,128)(2,1)S(1)} %get-tuple-element.130), channel_id=1, source_target_pairs={{0,384},{128,0},{256,128},{384,256},{1,385},{129,1},{257,129},{385... | collective-permute-start | bytes 294920 | tf_op jit(solution)/shard_map/ppermute | solution.py:205
  (14 other events, 12.8 us)
Sparse Core Ops, SparseCore 0:
  12.2 80.1 all-gather.2

commit v4 on v3

v4 whole, which is shorter than its diff:
```python
import functools

import jax
import jax.numpy as jnp
from jax import lax
from jax.experimental import pallas as pl
from jax.experimental.pallas import tpu as pltpu
from jax.sharding import Mesh, PartitionSpec as P

BF, F32 = jnp.bfloat16, jnp.float32
HALF = 64
SLOTS = 40


def params(mebibytes):
    return pltpu.CompilerParams(vmem_limit_bytes=mebibytes * 1024 * 1024)


def cost(gflop, mebibytes):
    return pl.CostEstimate(
        flops=int(gflop * 1e9), bytes_accessed=int(mebibytes * 2**20), transcendentals=0
    )


def vmem(count):
    return [pl.BlockSpec(memory_space=pltpu.VMEM)] * count


def dot(a, b, ca=1, cb=0):
    return lax.dot_general(a, b, (((ca,), (cb,)), ((), ())), preferred_element_type=F32)


def iota(shape, dim):
    return lax.broadcasted_iota(jnp.int32, shape, dim)


def prepare_kernel(tok, gout, gates, ids, pay, table):
    rows, width = tok.shape
    lane = iota((rows, 128), 1)
    expert = jnp.where(lane < HALF, lane, lane - HALF)
    gate = gates[...].astype(F32)
    chosen = ids[...]
    gate_of = jnp.zeros((rows, 128), F32)
    named = jnp.zeros((rows, 128), F32)
    for k in range(ids.shape[1]):
        hit = chosen[:, k : k + 1] == expert
        gate_of = gate_of + jnp.where(hit, gate[:, k : k + 1], 0.0)
        named = named + jnp.where(hit, 1.0, 0.0)
    before = jnp.where(iota((rows, rows), 0) > iota((rows, rows), 1), 1.0, 0.0).astype(BF)
    place = named * (dot(before, named.astype(BF)) + 1.0)
    both = jnp.where(lane < HALF, gate_of, place)
    table[...] = both
    pay[:, :width] = tok[...]
    pay[:, width : 2 * width] = gout[...]
    pay[:, 2 * width :] = both.T.astype(BF)


def pick_kernel(cap, gath, sel, place, origin, own, sib):
    n_z, rows, lanes = gath.shape
    width = lanes - 128
    block = n_z * cap
    gates = gath[:, :HALF, width:].reshape(n_z * HALF, 128)
    places = gath[:, HALF:, width:].reshape(n_z * HALF, 128)
    hits, gate_cols = [], []
    for b in range(4):
        part = slice(b * block, (b + 1) * block)
        hit = dot(sel[part], places) == place[...]
        gate_cols.append(
            jnp.sum(jnp.where(hit, dot(sel[part], gates), 0.0), axis=1, keepdims=True)
        )
        ones = jnp.where(hit, 1.0, 0.0)
        hits.append(
            jnp.concatenate(
                [jnp.where(origin[...] == s, ones, 0.0).astype(BF) for s in range(n_z)], axis=1
            )
        )
    step = min(width, 512)
    for b in range(4):
        out = own if b < 2 else sib
        for c in range(0, width, step):
            data = gath[:, :, c : c + step].reshape(n_z * rows, step)
            out[b % 2, :, c : c + step] = dot(hits[b], data).astype(BF)
        out[b % 2, :, width:] = jnp.broadcast_to(gate_cols[b], (block, 128)).astype(BF)


def experts(w_ref, x_of, g_of, gate_of, perms, lane_of, facs, grads, marks, reply):
    perm_l, perm_r, perm_s = perms
    width = w_ref.shape[1]
    block = grads.shape[1] // 2
    half = width // 2
    for e in range(2):
        up, down = w_ref[e], w_ref[2 + e]
        gate = gate_of(e)
        pre = dot(x_of(e), up)
        q = dot(g_of(e), down)
        s = jax.nn.sigmoid(pre)
        hidden = pre * s
        score = jnp.sum(hidden.astype(BF).astype(F32) * q, axis=1, keepdims=True)
        grad_a = (gate * q * (s * (1.0 + pre * (1.0 - s)))).astype(BF)
        facs[0][e] = grad_a
        facs[1][e] = (gate * hidden).astype(BF)
        rows = dot(grad_a, up, 1, 1).astype(BF)
        for b in range(2):
            part = slice(b * block, (b + 1) * block)
            to = slice(e * block, (e + 1) * block)
            grads[b, to] = rows[part]
            marks[b, to] = (score[part] * lane_of[to]).astype(BF)
    for b in range(2):
        left = dot(perm_l[...], grads[b, :, :half]) + dot(perm_r[...], grads[b, :, half:])
        first = left[:, :128] + dot(perm_s[...], marks[b])
        reply(b, slice(0, 128), first.astype(BF).reshape(-1, 2 * SLOTS, 128))
        reply(b, slice(128, half), left[:, 128:].astype(BF).reshape(-1, 2 * SLOTS, half - 128))


def own_kernel(spot, w_ref, own, got, pl_, pr_, ps_, lane_of, back, fac_up, fac_down, grads, marks):
    width = w_ref.shape[1]

    def rows_of(e, first, last):
        return jnp.concatenate([r[e, :, first:last] for r in (own, got)], axis=0)

    def reply(b, lanes, value):
        back[:, lax.bitwise_xor(spot[2], b), :, lanes] = value

    experts(
        w_ref,
        lambda e: rows_of(e, 0, width),
        lambda e: rows_of(e, width, 2 * width),
        lambda e: rows_of(e, 2 * width, 2 * width + 128).astype(F32)[:, :1],
        (pl_, pr_, ps_), lane_of, (fac_up, fac_down), grads, marks, reply,
    )


def other_kernel(
    w_ref, got, sort, sort_gate, pl_, pr_, ps_, lane_of, back_own, back, rows, fac_up, fac_down, grads, marks
):
    n_z, _, many, width = got.shape
    block = rows.shape[2] // 2
    gates = []
    for b in range(2):
        data = got[:, b].reshape(n_z * many, width)
        sorted_rows = dot(sort[...], data).astype(BF)
        for e in range(2):
            rows[0, e, b * block : (b + 1) * block] = sorted_rows[e * block : (e + 1) * block]
            rows[1, e, b * block : (b + 1) * block] = sorted_rows[(2 + e) * block : (3 + e) * block]
        line = dot(sort_gate[...], data[:, :128]) * lane_of[...]
        gates.append(jnp.sum(line, axis=1, keepdims=True))
    back[:, :, 0] = back_own[...]

    def reply(b, lanes, value):
        back[:, b, 1, :, lanes] = value

    experts(
        w_ref,
        lambda e: rows[0, e],
        lambda e: rows[1, e],
        lambda e: jnp.concatenate([g[e * block : (e + 1) * block] for g in gates], axis=0),
        (pl_, pr_, ps_), lane_of, (fac_up, fac_down), grads, marks, reply,
    )


def send_kernel(cap, pay, sel, place, out):
    n_dev, many, width = out.shape
    half = many // 2
    meta = pay[:, 2 * width :]
    hit = dot(sel[...], meta[HALF:]) == place[...]
    gate = jnp.sum(jnp.where(hit, dot(sel[...], meta[:HALF]), 0.0), axis=1, keepdims=True)
    row = lax.rem(iota(hit.shape, 0), many)
    ones = jnp.where(hit, 1.0, 0.0)
    pick_x = jnp.where(row < half, ones, 0.0).astype(BF)
    pick_g = jnp.where(row < half, 0.0, ones).astype(BF)
    line = jnp.where(row == iota(hit.shape, 1), gate, 0.0).reshape(n_dev, many, 128)
    line = jnp.sum(line, axis=1, keepdims=True)
    line = jnp.where(iota((n_dev, many, 128), 1) == 2 * cap, line, 0.0).reshape(n_dev * many, 128)
    step = min(width, 512)
    for c in range(0, width, step):
        lanes, g_lanes = slice(c, c + step), slice(width + c, width + c + step)
        value = dot(pick_x, pay[:, lanes]) + dot(pick_g, pay[:, g_lanes])
        if c == 0:
            value = jnp.concatenate((value[:, :128] + line, value[:, 128:]), axis=1)
        out[:, :, lanes] = value.astype(BF).reshape(n_dev, many, step)


def weight_kernel(n_y, n_x, spot, a_own, a_got, b_rows, *refs):
    fac, g_out, parts = refs[:4], refs[4:-1], refs[-1]
    share, hidden_len = parts.shape[2:]
    width = parts.shape[0] * share
    for e in range(2):
        for m in range(2):
            own = [r[e, :, m * width : (m + 1) * width] for r in (a_own, a_got)]
            x = jnp.concatenate(own + [b_rows[m, e]], axis=0)
            f = jnp.concatenate((fac[m][e], fac[2 + m][e]), axis=0)
            parts[:, 2 * m + e] = dot(x, f, 0, 0).astype(BF).reshape(-1, share, hidden_len)
    for d in range(n_x):
        for i in range(n_y):
            g_out[d][i] = parts[lax.rem(spot[0] + i, n_y) * n_x + lax.rem(spot[1] + d, n_x)]


def total_kernel(*refs):
    *ends, up, down = refs
    up[...] = sum(r[:2].astype(F32) for r in ends).astype(BF)
    down[...] = sum(r[2:].astype(F32) for r in ends).astype(BF)


def partial_sums(cap, got, which, at, lane_places, owners, slots, place_l, place_r):
    n_dev, _, _, half = got.shape
    data = got[:, which].reshape(n_dev * 2 * SLOTS, half)
    left = dot((at == place_l[...]).astype(F32).astype(BF), data)
    right = dot((at == place_r[...]).astype(F32).astype(BF), data)
    lines = got[:, which, 32:48, :128].reshape(n_dev * 16, 128)
    by_place = jnp.zeros((slots.shape[1], 128), F32)
    for m in range(2):
        by_place = by_place + dot(dot(slots[m], lines, 1, 1).astype(BF), owners[m])
    scores = jnp.zeros(lane_places.shape, F32)
    for r in range(cap):
        scores = scores + jnp.where(lane_places == r + 1.0, by_place[r : r + 1, :], 0.0)
    return left, right, scores


def partner_kernel(cap, got, pay, sel, owners, slots, place_l, place_r, out):
    width = out.shape[1] - 128
    half = width // 2
    meta = pay[HALF:, 2 * width :]
    at = dot(meta, sel[...], 0, 0)
    lane = iota((HALF, 128), 0) == iota((HALF, 128), 1)
    lane_places = dot(meta, jnp.where(lane, 1.0, 0.0).astype(BF), 0, 0)
    left, right, scores = partial_sums(cap, got, 1, at, lane_places, owners, slots, place_l, place_r)
    out[:, :half] = left.astype(BF)
    out[:, half:width] = right.astype(BF)
    out[:, width:] = scores.astype(BF)


def combine_kernel(cap, got, table, ids, sel, owners, slots, place_l, place_r, other, grad_tok, grad_gate):
    rows, width = grad_tok.shape
    half = width // 2
    both = table[...]
    at = dot(both.astype(BF), sel[...])
    at_lane = iota((128, 128), 0) == iota((128, 128), 1) + HALF
    lane_places = dot(both.astype(BF), jnp.where(at_lane, 1.0, 0.0).astype(BF))
    left, right, scores = partial_sums(cap, got, 0, at, lane_places, owners, slots, place_l, place_r)
    grad_tok[:, :half] = (left + other[:, :half].astype(F32)).astype(BF)
    grad_tok[:, half:] = (right + other[:, half:width].astype(F32)).astype(BF)
    scores = scores + other[:, width:].astype(F32)
    lane = iota((rows, 128), 1)
    column = iota((rows, ids.shape[1]), 1)
    chosen = ids[...]
    total = jnp.zeros((rows, ids.shape[1]), F32)
    for k in range(ids.shape[1]):
        score = jnp.sum(
            jnp.where(lane == chosen[:, k : k + 1], scores, 0.0), axis=1, keepdims=True
        )
        total = total + jnp.where(column == k, score, 0.0)
    grad_gate[...] = total.astype(BF)


def shift(value, axis, by):
    n = lax.axis_size(axis)
    return lax.ppermute(value, axis, [(i, (i + by) % n) for i in range(n)])


def weights_kernel(n_y, n_x, spot, *refs):
    *blocks, out = refs
    share = blocks[0].shape[2]
    for i in range(n_y):
        for d in range(n_x):
            group = lax.rem(spot[0] + n_y - i, n_y) * n_x + lax.rem(spot[1] + n_x - d, n_x)
            start = pl.multiple_of(group * share, share)
            for m in range(4):
                out[m, pl.ds(start, share), :] = blocks[d][i, m]


def held(*values):
    return lax.optimization_barrier(values)


def per_device(tokens, grad_out, gates, expert_ids, w_up, w_down):
    rows, width = tokens.shape
    top = expert_ids.shape[1]
    n_y, n_x, n_z = lax.axis_size("yl"), lax.axis_size("x"), lax.axis_size("z")
    experts = 8 * n_z
    cap = rows * top * 9 // (8 * experts)
    block = n_z * cap
    share, hidden_len = w_up.shape[1:]
    half = width // 2
    yl, x, z, yh, c = [lax.axis_index(a) for a in ("yl", "x", "z", "yh", "c")]
    shape = jax.ShapeDtypeStruct

    pay, table = pl.pallas_call(
        prepare_kernel,
        out_shape=(shape((rows, 2 * width + 128), BF), shape((rows, 128), F32)),
        in_specs=vmem(4),
        out_specs=tuple(vmem(2)),
        cost_estimate=cost(0.1, 2),
        compiler_params=params(8),
    )(tokens, grad_out, gates, expert_ids)
    spot = jnp.stack([yl, x, c]).astype(jnp.int32)
    smem = [pl.BlockSpec(memory_space=pltpu.SMEM)]
    gath = lax.all_gather(pay, "z", axis=0)
    pay_other = shift(pay, "yh", 1)
    n_dev = 2 * n_z
    many = 2 * SLOTS

    p = jnp.arange(n_dev * many)
    dev_p, s_p = p // many, p % many
    q = s_p % SLOTS
    first_of = ((dev_p // 2 * 2 + yh) * 2 + dev_p % 2) * 2
    e_p = first_of + (q >= cap)
    tgt = jnp.where(q < 2 * cap, q % cap + 1, -1)
    sel_s = (e_p[:, None] == jnp.arange(HALF)[None, :]).astype(BF)
    place_s = jnp.broadcast_to(tgt.astype(F32)[:, None], (n_dev * many, 128))
    sent = pl.pallas_call(
        functools.partial(send_kernel, cap),
        out_shape=shape((n_dev, many, width), BF),
        in_specs=vmem(3),
        out_specs=vmem(1)[0],
        cost_estimate=cost(1, 6),
        compiler_params=params(20),
    )(pay_other, sel_s, place_s)
    got_rows = lax.all_to_all(sent, ("z", "c"), 0, 0, tiled=True)

    w_mine = jnp.concatenate((w_up, jnp.transpose(w_down, (0, 2, 1))), axis=0)
    w_mine, _ = held(w_mine, sent)
    w_line = jnp.stack([w_mine] + [shift(w_mine, "yl", d) for d in range(1, n_y)])
    w_parts = [w_line] + [shift(w_line, "x", d) for d in range(1, n_x)]
    gath, *w_parts = held(gath, *w_parts)
    w_all = pl.pallas_call(
        functools.partial(weights_kernel, n_y, n_x),
        out_shape=shape((4, width, hidden_len), BF),
        in_specs=smem + vmem(n_x),
        out_specs=vmem(1)[0],
        cost_estimate=cost(0, 6),
        compiler_params=params(10),
    )(spot, *w_parts)

    j = jnp.arange(4 * block)
    b_j, d_j, r_j = j // block, (j % block) // cap, j % cap
    core_j = jnp.where(b_j >= 2, 1 - c, c)
    e_j = ((z * 2 + yh) * 2 + core_j) * 2 + b_j % 2
    sel = ((d_j * HALF + e_j)[:, None] == jnp.arange(n_z * HALF)[None, :]).astype(BF)
    place = jnp.broadcast_to((r_j[:block, None] + 1).astype(F32), (block, 128))
    origin = jnp.broadcast_to(d_j[:block, None].astype(jnp.int32), (block, 128))

    a_own, a_sib = pl.pallas_call(
        functools.partial(pick_kernel, cap),
        out_shape=(shape((2, block, 2 * width + 128), BF),) * 2,
        in_specs=vmem(4),
        out_specs=tuple(vmem(2)),
        cost_estimate=cost(2.6, 12),
        compiler_params=params(20),
    )(gath, sel, place, origin)
    a_got = shift(a_sib, "c", 1)

    i = jnp.arange(2 * block)
    e_i, z_i, r_i = i // block, (i % block) // cap, i % cap
    v = jnp.arange(n_z * many)
    z_v, q_v = v // many, v % many
    same = z_v[:, None] == z_i[None, :]
    slot_i = (e_i * cap + r_i)[None, :]
    in_x, in_g, in_s = [same & (q_v[:, None] == at) for at in (slot_i, slot_i + SLOTS, 2 * cap)]
    perms = [m.astype(BF) for m in (in_x, in_g, in_s)]
    sort = jnp.concatenate((in_x, in_g), axis=1).T.astype(BF)
    sort_gate = in_s.T.astype(BF)
    lane_of = (slot_i.T == jnp.arange(128)[None, :]).astype(F32)
    scratch = [pltpu.VMEM((2, 2 * block, width), BF), pltpu.VMEM((2, 2 * block, 128), BF)]
    facs = (shape((2, 2 * block, hidden_len), BF),) * 2
    a_back, a_up, a_down = pl.pallas_call(
        own_kernel,
        out_shape=(shape((n_z, 2, many, half), BF), *facs),
        in_specs=smem + vmem(7),
        out_specs=tuple(vmem(3)),
        scratch_shapes=scratch,
        cost_estimate=cost(4, 24),
        compiler_params=params(28),
    )(spot, w_all, a_own, a_got, *perms, lane_of)
    got_rows, a_up = held(got_rows, a_up)
    back, b_rows, b_up, b_down = pl.pallas_call(
        other_kernel,
        out_shape=(
            shape((n_z, 2, 2, many, half), BF),
            shape((2, 2, 2 * block, width), BF),
            *facs,
        ),
        in_specs=vmem(9),
        out_specs=tuple(vmem(4)),
        scratch_shapes=scratch,
        cost_estimate=cost(5, 24),
        compiler_params=params(32),
    )(w_all, got_rows.reshape(n_z, 2, many, width), sort, sort_gate, *perms, lane_of, a_back)
    got = lax.all_to_all(back.reshape(n_dev, 2, many, half), ("z", "c"), 0, 0, tiled=True)
    parts = pl.pallas_call(
        functools.partial(weight_kernel, n_y, n_x),
        out_shape=(shape((n_y, 4, share, hidden_len), BF),) * n_x,
        in_specs=smem + vmem(7),
        out_specs=tuple(vmem(n_x)),
        scratch_shapes=[pltpu.VMEM((n_y * n_x, 4, share, hidden_len), BF)],
        cost_estimate=cost(2, 18),
        compiler_params=params(28),
    )(spot, a_own, a_got, b_rows, a_up, a_down, b_up, b_down)

    lines = [parts[0]] + [shift(parts[d], "x", d) for d in range(1, n_x)]
    line = sum(u.astype(F32) for u in lines).astype(BF)
    ends = [line[0]] + [shift(line[d], "yl", d) for d in range(1, n_y)]
    grad_up, grad_down = pl.pallas_call(
        total_kernel,
        out_shape=(shape((2, share, hidden_len), BF),) * 2,
        in_specs=vmem(n_y),
        out_specs=tuple(vmem(2)),
        cost_estimate=cost(0, 2),
        compiler_params=params(6),
    )(*ends)
    grad_down = jnp.transpose(grad_down, (0, 2, 1))

    sel_t = (jnp.arange(128)[:, None] == HALF + e_p[None, :]).astype(BF)
    sel_p = (jnp.arange(HALF)[:, None] == e_p[None, :]).astype(BF)
    place_l = jnp.where(s_p < SLOTS, tgt, -1).astype(F32)[None, :]
    place_r = jnp.where(s_p >= SLOTS, tgt, -1).astype(F32)[None, :]
    line_o = jnp.arange(n_dev * 16)
    first_o = ((line_o // 32 * 2 + yh) * 2 + line_o // 16 % 2) * 2
    first_o = jnp.where(line_o % 16 == 2 * cap - 32, first_o, -2)
    parity = jnp.arange(2)[:, None, None]
    owners = (first_o[None, :, None] + parity == jnp.arange(128)[None, None, :]).astype(BF)
    at_slot = jnp.arange(24)[None, :, None]
    slots = (
        (at_slot < cap) & (jnp.arange(128)[None, None, :] == at_slot + parity * cap)
    ).astype(BF)
    partner = pl.pallas_call(
        functools.partial(partner_kernel, cap),
        out_shape=shape((rows, width + 128), BF),
        in_specs=vmem(7),
        out_specs=vmem(1)[0],
        cost_estimate=cost(0.4, 4),
        compiler_params=params(12),
    )(got, pay_other, sel_p, owners, slots, place_l, place_r)
    other = shift(partner, "yh", 1)
    grad_tokens, grad_gates = pl.pallas_call(
        functools.partial(combine_kernel, cap),
        out_shape=(shape((rows, width), BF), shape((rows, top), BF)),
        in_specs=vmem(9),
        out_specs=tuple(vmem(2)),
        cost_estimate=cost(0.4, 4),
        compiler_params=params(12),
    )(got, table, expert_ids, sel_t, owners, slots, place_l, place_r, other)
    return (grad_tokens, grad_gates, grad_up, grad_down)


def build(mesh):
    every, dp, ctx = ("yl", "x", "z", "yh", "c"), ("yl", "x"), ("z", "yh", "c")
    tok, up, down = P(every, None), P(ctx, dp, None), P(ctx, None, dp)
    return jax.shard_map(
        per_device,
        mesh=mesh,
        in_specs=(tok, tok, tok, tok, up, down),
        out_specs=(tok, tok, up, down),
        check_vma=False,
    )


def solution(mesh):
    return build(Mesh(mesh.devices.reshape(4, 4, 8, 2, 2), ("yl", "x", "z", "yh", "c")))
```

time: 297 us -> 288 us (0.970)
  the two profiles are of different devices: /device:TPU:11 before, /device:TPU:58 now
where the time goes in v4:
time: 288 us; the launch traced here: 286 us
  waiting for transfers between devices  121 us (42%)
  starting transfers between devices  66.8 us (23%)
  local copies, waits for them, and re-layouts  44.3 us (15%)
  Pallas kernels  29.9 us (10%)
  between operations  14.6 us (5%)
  other arithmetic  9.89 us (3%)
    ppermute x15, waiting for transfers between devices, shift(): return lax.ppermute(value, axis, [(i, (i + by) % n) for i in range(n)])  121 us
    ppermute x15, starting transfers between devices, shift(): return lax.ppermute(value, axis, [(i, (i + by) % n) for i in range(n)])  49.4 us
    unnamed x117, local copies, waits for them, and re-layouts  40.8 us
    all_to_all x1, starting transfers between devices, per_device(): got_rows = lax.all_to_all(sent, ('z', 'c'), 0, 0, tiled=True)  10.6 us
    all_to_all x1, starting transfers between devices, per_device(): lax.all_to_all(back.reshape(n_dev, 2, many, half), ('z', 'c'), 0, 0, tile...  6.81 us
    pallas_call x1, Pallas kernels, per_device(): pl.pallas_call(other_kernel, out_shape=(shape((n_z, 2, 2, many, half), BF...  5.96 us
  transfers between devices with their start and end apart: 18, of which 9 were waited for; matrix products, arithmetic and copies ran while one was open for 5% of the time, Pallas kernels for 7%

profile of v4, /device:TPU:58, one launch (start us, length us, event | category | flops | bytes accessed | tf_op | source)
XLA Modules:
  0.0 286.1 jit_solution(15738368504596612332)
XLA Ops:
  10.7 1.3 shard_map.93
  12.7 4.7 %collective-permute-start = (bf16[128,2176]{1,0:T(8,128)(2,1)}, bf16[128,2176]{1,0:T(8,128)(2,1)S(1)}, u32[]{:S(2)}, u32[]{:S(2)}) collective-permute-start(bf16[128,2176]{1,0:T(8,128)(2,1)} %get-tuple-element.31), channel_id=1, source_target_pairs={{0,2},{2,0},{1,3},{3,1},{4,6},{6,4},{5,7},{7,5},{8,10},{10,8},{9,1... | collective-permute-start | bytes 1671176 | tf_op jit(solution)/shard_map/ppermute | solution.py:257
  17.7 27.0 %collective-permute-done.pay = bf16[128,2176]{1,0:T(8,128)(2,1)S(1)} collective-permute-done((bf16[128,2176]{1,0:T(8,128)(2,1)}, bf16[128,2176]{1,0:T(8,128)(2,1)S(1)}, u32[]{:S(2)}, u32[]{:S(2)}) %collective-permute-start) | collective-permute-done | bytes 557088 | tf_op jit(solution)/shard_map/ppermute | solution.py:257
  44.9 3.3 %shard_map.94 = bf16[16,80,1024]{2,1,0:T(8,128)(2,1)} custom-call(bf16[128,2176]{1,0:T(8,128)(2,1)S(1)} %collective-permute-done.pay, bf16[1280,64]{1,0:T(8,128)(2,1)S(1)} %fusion.3.sel, f32[1280,128]{1,0:T(8,128)S(1)} %broadcast_in_dim.21.place), custom_call_target="tpu_custom_call" | custom-call | flops 1000000000 | bytes 6291456 | tf_op jit(solution)/shard_map/pallas_call | solution.py:310
  48.2 10.6 %all-to-all-start = ((bf16[16,80,1024]{2,1,0:T(8,128)(2,1)}), bf16[16,80,1024]{2,1,0:T(8,128)(2,1)S(1)}, u32[]{:S(2)}, u32[]{:S(2)}) async-start(bf16[16,80,1024]{2,1,0:T(8,128)(2,1)} %shard_map.94), calls=%async_computation | async-start | bytes 5242880 | tf_op jit(solution)/shard_map/all_to_all | solution.py:318
  58.8 5.3 %collective-permute-start.1 = (bf16[4,64,384]{2,1,0:T(8,128)(2,1)S(1)}, bf16[4,64,384]{2,1,0:T(8,128)(2,1)S(1)}, u32[]{:S(2)}, u32[]{:S(2)}) collective-permute-start(bf16[4,64,384]{2,1,0:T(8,128)(2,1)S(1)} %pad_maximum_fusion.1), channel_id=1, source_target_pairs={{0,128},{128,256},{256,384},{384,0},{1,129},{129,257},{257,385},{3... | collective-permute-start | bytes 589832 | tf_op jit(solution)/shard_map/ppermute | solution.py:257
  64.1 1.9 collective-permute-start.2
  66.0 3.0 %collective-permute-start.3 = (bf16[4,64,384]{2,1,0:T(8,128)(2,1)S(1)}, bf16[4,64,384]{2,1,0:T(8,128)(2,1)S(1)}, u32[]{:S(2)}, u32[]{:S(2)}) collective-permute-start(bf16[4,64,384]{2,1,0:T(8,128)(2,1)S(1)} %pad_maximum_fusion.1), channel_id=1, source_target_pairs={{0,384},{128,0},{256,128},{384,256},{1,385},{129,1},{257,129},{385... | collective-permute-start | bytes 589832 | tf_op jit(solution)/shard_map/ppermute | solution.py:257
  69.3 12.8 %collective-permute-done.2 = bf16[4,64,384]{2,1,0:T(8,128)(2,1)S(1)} collective-permute-done((bf16[4,64,384]{2,1,0:T(8,128)(2,1)S(1)}, bf16[4,64,384]{2,1,0:T(8,128)(2,1)S(1)}, u32[]{:S(2)}, u32[]{:S(2)}) %collective-permute-start.2) | collective-permute-done | bytes 196640 | tf_op jit(solution)/shard_map/ppermute | solution.py:257
  82.9 1.3 pad_maximum_fusion.refs_0_
  84.2 3.4 %collective-permute-start.4 = (bf16[4,4,64,384]{3,2,1,0:T(8,128)(2,1)S(1)}, bf16[4,4,64,384]{3,2,1,0:T(8,128)(2,1)S(1)}, u32[]{:S(2)}, u32[]{:S(2)}) collective-permute-start(bf16[4,4,64,384]{3,2,1,0:T(8,128)(2,1)S(1)} %pad_maximum_fusion.refs_0_), channel_id=1, source_target_pairs={{0,32},{32,64},{64,96},{96,0},{1,33},{33,65},{65,97},{97,1},{2,34}... | collective-permute-start | bytes 2359304 | tf_op jit(solution)/shard_map/ppermute | solution.py:257
  87.6 3.0 %collective-permute-start.5 = (bf16[4,4,64,384]{3,2,1,0:T(8,128)(2,1)S(1)}, bf16[4,4,64,384]{3,2,1,0:T(8,128)(2,1)S(1)}, u32[]{:S(2)}, u32[]{:S(2)}) collective-permute-start(bf16[4,4,64,384]{3,2,1,0:T(8,128)(2,1)S(1)} %pad_maximum_fusion.refs_0_), channel_id=1, source_target_pairs={{0,64},{32,96},{64,0},{96,32},{1,65},{33,97},{65,1},{97,33},{2,66}... | collective-permute-start | bytes 2359304 | tf_op jit(solution)/shard_map/ppermute | solution.py:257
  90.7 4.1 %collective-permute-start.6 = (bf16[4,4,64,384]{3,2,1,0:T(8,128)(2,1)S(1)}, bf16[4,4,64,384]{3,2,1,0:T(8,128)(2,1)S(1)}, u32[]{:S(2)}, u32[]{:S(2)}) collective-permute-start(bf16[4,4,64,384]{3,2,1,0:T(8,128)(2,1)S(1)} %pad_maximum_fusion.refs_0_), channel_id=1, source_target_pairs={{0,96},{32,0},{64,32},{96,64},{1,97},{33,1},{65,33},{97,65},{2,98}... | collective-permute-start | bytes 2359304 | tf_op jit(solution)/shard_map/ppermute | solution.py:257
  95.8 10.7 %collective-permute-done.4.refs_1_ = bf16[4,4,64,384]{3,2,1,0:T(8,128)(2,1)S(1)} collective-permute-done((bf16[4,4,64,384]{3,2,1,0:T(8,128)(2,1)S(1)}, bf16[4,4,64,384]{3,2,1,0:T(8,128)(2,1)S(1)}, u32[]{:S(2)}, u32[]{:S(2)}) %collective-permute-start.4) | collective-permute-done | bytes 786464 | tf_op jit(solution)/shard_map/ppermute | solution.py:257
  107.4 4.1 %collective-permute-done.5.refs_2_ = bf16[4,4,64,384]{3,2,1,0:T(8,128)(2,1)S(1)} collective-permute-done((bf16[4,4,64,384]{3,2,1,0:T(8,128)(2,1)S(1)}, bf16[4,4,64,384]{3,2,1,0:T(8,128)(2,1)S(1)}, u32[]{:S(2)}, u32[]{:S(2)}) %collective-permute-start.5) | collective-permute-done | bytes 786464 | tf_op jit(solution)/shard_map/ppermute | solution.py:257
  112.5 14.3 %collective-permute-done.6.refs_3_ = bf16[4,4,64,384]{3,2,1,0:T(8,128)(2,1)S(1)} collective-permute-done((bf16[4,4,64,384]{3,2,1,0:T(8,128)(2,1)S(1)}, bf16[4,4,64,384]{3,2,1,0:T(8,128)(2,1)S(1)}, u32[]{:S(2)}, u32[]{:S(2)}) %collective-permute-start.6) | collective-permute-done | bytes 786464 | tf_op jit(solution)/shard_map/ppermute | solution.py:257
  129.1 2.3 copy-done.29
  131.3 3.9 %shard_map.96 = (bf16[2,144,2176]{2,1,0:T(8,128)(2,1)S(1)}, bf16[2,144,2176]{2,1,0:T(8,128)(2,1)}) custom-call(bf16[8,128,2176]{2,1,0:T(8,128)(2,1)S(1)} %bitcast.24, bf16[576,512]{1,0:T(8,128)(2,1)S(1)} %copy-done.13, f32[144,128]{1,0:T(8,128)S(1)} %broadcast_in_dim.24.place, s32[144,128]{1,0:T(8,128)S(1)} %broadcast_in_dim.25.origin), custom_call_target="tpu_custom_call" | custom-call | flops 2600000000 | bytes 12582912 | tf_op jit(solution)/shard_map/pallas_call | solution.py:342
  136.4 2.1 collective-permute-start.7
  139.1 1.7 compare_and_fusion.2
  140.8 1.2 fusion.2
  142.0 2.3 copy.12.sort
  145.2 1.7 and_convert_fusion.sort_gate
  146.9 1.1 copy-done.6
  152.0 5.4 %shard_map.97 = (bf16[8,2,80,512]{3,2,1,0:T(8,128)(2,1)S(1)}, bf16[2,288,384]{2,1,0:T(8,128)(2,1)S(1)}, bf16[2,288,384]{2,1,0:T(8,128)(2,1)S(1)}) custom-call(s32[3]{0:T(128)S(1)} %pad_add_fusion.spot, bf16[4,1024,384]{2,1,0:T(8,128)(2,1)S(1)} %shard_map.95.w_ref, bf16[2,144,2176]{2,1,0:T(8,128)(2,1)S(1)} %copy-done.33, ...), custom_call_target="tpu_custom_call" | custom-call | flops 4000000000 | bytes 25165824 | tf_op jit(solution)/shard_map/pallas_call | solution.py:365
  157.5 1.6 copy-done
  160.7 1.2 copy-done.43
  161.9 1.9 copy-done.1
  167.8 1.3 copy-done.44
  169.1 6.0 %shard_map.98 = (bf16[8,2,2,80,512]{4,3,2,1,0:T(8,128)(2,1)S(1)}, bf16[2,2,288,1024]{3,2,1,0:T(8,128)(2,1)S(1)}, bf16[2,288,384]{2,1,0:T(8,128)(2,1)S(1)}, bf16[2,288,384]{2,1,0:T(8,128)(2,1)S(1)}) custom-call(bf16[4,1024,384]{2,1,0:T(8,128)(2,1)S(1)} %copy-done.1, bf16[8,2,80,1024]{3,2,1,0:T(8,128)(2,1)S(1)} %bitcast.22, bf16[576,640]{1,0:T(8,128)(2,1)S(1)} %copy-done.11, ...), custom_call_target="tpu_custom_call" | custom-call | flops 5000000000 | bytes 25165824 | tf_op jit(solution)/shard_map/pallas_call | solution.py:375
  175.1 1.5 copy-done.2
  176.6 1.5 copy-done.30
  179.7 6.8 %all-to-all-start.1 = ((bf16[16,2,80,512]{3,2,1,0:T(8,128)(2,1)}), bf16[16,2,80,512]{3,2,1,0:T(8,128)(2,1)S(1)}, u32[]{:S(2)}, u32[]{:S(2)}) async-start(bf16[16,2,80,512]{3,2,1,0:T(8,128)(2,1)} %bitcast.23), calls=%async_computation.1 | async-start | bytes 5242880 | tf_op jit(solution)/shard_map/all_to_all | solution.py:388
  186.8 1.7 copy-done.31
  188.5 1.3 copy-done.34
  192.8 4.8 %shard_map.101 = (bf16[4,4,64,384]{3,2,1,0:T(8,128)(2,1)S(1)}, bf16[4,4,64,384]{3,2,1,0:T(8,128)(2,1)S(1)}, bf16[4,4,64,384]{3,2,1,0:T(8,128)(2,1)S(1)}, bf16[4,4,64,384]{3,2,1,0:T(8,128)(2,1)S(1)}) custom-call(s32[3]{0:T(128)S(1)} %copy-done.28, bf16[2,144,2176]{2,1,0:T(8,128)(2,1)S(1)} %copy-done.34, ...), custom_call_target="tpu_custom_call" | custom-call | flops 2000000000 | bytes 18874368 | tf_op jit(solution)/shard_map/pallas_call | solution.py:389
  197.6 3.0 %collective-permute-start.10 = (bf16[4,4,64,384]{3,2,1,0:T(8,128)(2,1)S(1)}, bf16[4,4,64,384]{3,2,1,0:T(8,128)(2,1)S(1)}, u32[]{:S(2)}, u32[]{:S(2)}) collective-permute-start(bf16[4,4,64,384]{3,2,1,0:T(8,128)(2,1)S(1)} %get-tuple-element.54), channel_id=1, source_target_pairs={{0,64},{32,96},{64,0},{96,32},{1,65},{33,97},{65,1},{97,33},{2,66}... | collective-permute-start | bytes 2359304 | tf_op jit(solution)/shard_map/ppermute | solution.py:257
  200.7 3.5 %collective-permute-start.11 = (bf16[4,4,64,384]{3,2,1,0:T(8,128)(2,1)S(1)}, bf16[4,4,64,384]{3,2,1,0:T(8,128)(2,1)S(1)}, u32[]{:S(2)}, u32[]{:S(2)}) collective-permute-start(bf16[4,4,64,384]{3,2,1,0:T(8,128)(2,1)S(1)} %get-tuple-element.55), channel_id=1, source_target_pairs={{0,96},{32,0},{64,32},{96,64},{1,97},{33,1},{65,33},{97,65},{2,98}... | collective-permute-start | bytes 2359304 | tf_op jit(solution)/shard_map/ppermute | solution.py:257
  204.2 2.4 collective-permute-start.9
  207.4 14.0 %collective-permute-done.10 = bf16[4,4,64,384]{3,2,1,0:T(8,128)(2,1)S(1)} collective-permute-done((bf16[4,4,64,384]{3,2,1,0:T(8,128)(2,1)S(1)}, bf16[4,4,64,384]{3,2,1,0:T(8,128)(2,1)S(1)}, u32[]{:S(2)}, u32[]{:S(2)}) %collective-permute-start.10) | collective-permute-done | bytes 786464 | tf_op jit(solution)/shard_map/ppermute | solution.py:257
  221.4 16.3 %collective-permute-done.11 = bf16[4,4,64,384]{3,2,1,0:T(8,128)(2,1)S(1)} collective-permute-done((bf16[4,4,64,384]{3,2,1,0:T(8,128)(2,1)S(1)}, bf16[4,4,64,384]{3,2,1,0:T(8,128)(2,1)S(1)}, u32[]{:S(2)}, u32[]{:S(2)}) %collective-permute-start.11) | collective-permute-done | bytes 786464 | tf_op jit(solution)/shard_map/ppermute | solution.py:257
  239.1 2.0 collective-permute-start.12
  241.1 5.2 %collective-permute-start.13 = (bf16[4,64,384]{2,1,0:T(8,128)(2,1)}, bf16[4,64,384]{2,1,0:T(8,128)(2,1)}, u32[]{:S(2)}, u32[]{:S(2)}) collective-permute-start(bf16[4,64,384]{2,1,0:T(8,128)(2,1)} %get-tuple-element.63), channel_id=1, source_target_pairs={{0,256},{128,384},{256,0},{384,128},{1,257},{129,385},{257,1},{385... | collective-permute-start | bytes 589832 | tf_op jit(solution)/shard_map/ppermute | solution.py:257
  246.3 3.9 %collective-permute-start.14 = (bf16[4,64,384]{2,1,0:T(8,128)(2,1)}, bf16[4,64,384]{2,1,0:T(8,128)(2,1)}, u32[]{:S(2)}, u32[]{:S(2)}) collective-permute-start(bf16[4,64,384]{2,1,0:T(8,128)(2,1)} %get-tuple-element.62), channel_id=1, source_target_pairs={{0,384},{128,0},{256,128},{384,256},{1,385},{129,1},{257,129},{385... | collective-permute-start | bytes 589832 | tf_op jit(solution)/shard_map/ppermute | solution.py:257
  252.1 1.9 collective-permute-start.8
  254.1 21.0 %collective-permute-done.13.refs_2_ = bf16[4,64,384]{2,1,0:T(8,128)(2,1)} collective-permute-done((bf16[4,64,384]{2,1,0:T(8,128)(2,1)}, bf16[4,64,384]{2,1,0:T(8,128)(2,1)}, u32[]{:S(2)}, u32[]{:S(2)}) %collective-permute-start.13) | collective-permute-done | bytes 196640 | tf_op jit(solution)/shard_map/ppermute | solution.py:257
  275.1 1.9 shard_map.102
  277.0 1.6 shard_map.100
  (154 shorter events, 32.6 us)
Async XLA Ops:
  7.2 120.7 %all-gather.3.cloned.1.call-start = ((), (), s32[]{:S(2)}) async-start(), calls=%async_computation.2 | async-start | bytes 5013504 | tf_op jit(solution)/shard_map/all_gather | solution.py:297
  8.0 4.7 %copy-start.14 = (s32[128,8]{1,0:T(8,128)}, s32[128,8]{1,0:T(8,128)S(1)}, u32[]{:S(2)}) copy-start(s32[128,8]{1,0:T(8,128)S(1)} %copy.11.ids) | copy-start | bytes 12292
  12.7 32.0 %collective-permute-start = (bf16[128,2176]{1,0:T(8,128)(2,1)}, bf16[128,2176]{1,0:T(8,128)(2,1)S(1)}, u32[]{:S(2)}, u32[]{:S(2)}) collective-permute-start(bf16[128,2176]{1,0:T(8,128)(2,1)} %get-tuple-element.31), channel_id=1, source_target_pairs={{0,2},{2,0},{1,3},{3,1},{4,6},{6,4},{5,7},{7,5},{8,10},{10,8},{9,1... | collective-permute-start | bytes 1671176 | tf_op jit(solution)/shard_map/ppermute | solution.py:257
  17.5 27.2 %copy-start.51 = (s32[1280]{0:T(1024)}, s32[1280]{0:T(1024)S(1)}, u32[]{:S(2)}) copy-start(s32[1280]{0:T(1024)S(1)} %fusion.21) | copy-start | bytes 15364
  44.7 3.5 %copy-start.3 = (bf16[128,2176]{1,0:T(8,128)(2,1)}, bf16[128,2176]{1,0:T(8,128)(2,1)S(1)}, u32[]{:S(2)}) copy-start(bf16[128,2176]{1,0:T(8,128)(2,1)S(1)} %collective-permute-done.pay) | copy-start | bytes 1671172
  48.2 10.6 %copy-start.49 = (bf16[2,384,64]{1,2,0:T(8,128)(2,1)S(1)}, bf16[2,384,64]{1,2,0:T(8,128)(2,1)}, u32[]{:S(2)}) copy-start(bf16[2,384,64]{1,2,0:T(8,128)(2,1)} %param.11) | copy-start | bytes 294916
  48.2 10.6 %copy-start.50 = (bf16[2,64,384]{2,1,0:T(8,128)(2,1)S(1)}, bf16[2,64,384]{2,1,0:T(8,128)(2,1)}, u32[]{:S(2)}) copy-start(bf16[2,64,384]{2,1,0:T(8,128)(2,1)} %param.10) | copy-start | bytes 294916
  48.2 113.7 %all-to-all-start = ((bf16[16,80,1024]{2,1,0:T(8,128)(2,1)}), bf16[16,80,1024]{2,1,0:T(8,128)(2,1)S(1)}, u32[]{:S(2)}, u32[]{:S(2)}) async-start(bf16[16,80,1024]{2,1,0:T(8,128)(2,1)} %shard_map.94), calls=%async_computation | async-start | bytes 5242880 | tf_op jit(solution)/shard_map/all_to_all | solution.py:318
  58.8 23.3 %copy-start.45 = (bf16[4,64,384]{2,1,0:T(8,128)(2,1)}, bf16[4,64,384]{2,1,0:T(8,128)(2,1)S(1)}, u32[]{:S(2)}) copy-start(bf16[4,64,384]{2,1,0:T(8,128)(2,1)S(1)} %pad_maximum_fusion.1) | copy-start | bytes 589828
  58.8 10.5 %collective-permute-start.1 = (bf16[4,64,384]{2,1,0:T(8,128)(2,1)S(1)}, bf16[4,64,384]{2,1,0:T(8,128)(2,1)S(1)}, u32[]{:S(2)}, u32[]{:S(2)}) collective-permute-start(bf16[4,64,384]{2,1,0:T(8,128)(2,1)S(1)} %pad_maximum_fusion.1), channel_id=1, source_target_pairs={{0,128},{128,256},{256,384},{384,0},{1,129},{129,257},{257,385},{3... | collective-permute-start | bytes 589832 | tf_op jit(solution)/shard_map/ppermute | solution.py:257
  64.1 18.0 %collective-permute-start.2 = (bf16[4,64,384]{2,1,0:T(8,128)(2,1)S(1)}, bf16[4,64,384]{2,1,0:T(8,128)(2,1)S(1)}, u32[]{:S(2)}, u32[]{:S(2)}) collective-permute-start(bf16[4,64,384]{2,1,0:T(8,128)(2,1)S(1)} %pad_maximum_fusion.1), channel_id=1, source_target_pairs={{0,256},{128,384},{256,0},{384,128},{1,257},{129,385},{257,1},{385... | collective-permute-start | bytes 589832 | tf_op jit(solution)/shard_map/ppermute | solution.py:257
  66.0 16.1 %collective-permute-start.3 = (bf16[4,64,384]{2,1,0:T(8,128)(2,1)S(1)}, bf16[4,64,384]{2,1,0:T(8,128)(2,1)S(1)}, u32[]{:S(2)}, u32[]{:S(2)}) collective-permute-start(bf16[4,64,384]{2,1,0:T(8,128)(2,1)S(1)} %pad_maximum_fusion.1), channel_id=1, source_target_pairs={{0,384},{128,0},{256,128},{384,256},{1,385},{129,1},{257,129},{385... | collective-permute-start | bytes 589832 | tf_op jit(solution)/shard_map/ppermute | solution.py:257
  69.3 12.8 %copy-start.46 = (bf16[4,64,384]{2,1,0:T(8,128)(2,1)}, bf16[4,64,384]{2,1,0:T(8,128)(2,1)S(1)}, u32[]{:S(2)}) copy-start(bf16[4,64,384]{2,1,0:T(8,128)(2,1)S(1)} %collective-permute-done.1) | copy-start | bytes 589828
  84.2 22.3 %collective-permute-start.4 = (bf16[4,4,64,384]{3,2,1,0:T(8,128)(2,1)S(1)}, bf16[4,4,64,384]{3,2,1,0:T(8,128)(2,1)S(1)}, u32[]{:S(2)}, u32[]{:S(2)}) collective-permute-start(bf16[4,4,64,384]{3,2,1,0:T(8,128)(2,1)S(1)} %pad_maximum_fusion.refs_0_), channel_id=1, source_target_pairs={{0,32},{32,64},{64,96},{96,0},{1,33},{33,65},{65,97},{97,1},{2,34}... | collective-permute-start | bytes 2359304 | tf_op jit(solution)/shard_map/ppermute | solution.py:257
  87.6 23.9 %collective-permute-start.5 = (bf16[4,4,64,384]{3,2,1,0:T(8,128)(2,1)S(1)}, bf16[4,4,64,384]{3,2,1,0:T(8,128)(2,1)S(1)}, u32[]{:S(2)}, u32[]{:S(2)}) collective-permute-start(bf16[4,4,64,384]{3,2,1,0:T(8,128)(2,1)S(1)} %pad_maximum_fusion.refs_0_), channel_id=1, source_target_pairs={{0,64},{32,96},{64,0},{96,32},{1,65},{33,97},{65,1},{97,33},{2,66}... | collective-permute-start | bytes 2359304 | tf_op jit(solution)/shard_map/ppermute | solution.py:257
  90.7 36.2 %collective-permute-start.6 = (bf16[4,4,64,384]{3,2,1,0:T(8,128)(2,1)S(1)}, bf16[4,4,64,384]{3,2,1,0:T(8,128)(2,1)S(1)}, u32[]{:S(2)}, u32[]{:S(2)}) collective-permute-start(bf16[4,4,64,384]{3,2,1,0:T(8,128)(2,1)S(1)} %pad_maximum_fusion.refs_0_), channel_id=1, source_target_pairs={{0,96},{32,0},{64,32},{96,64},{1,97},{33,1},{65,33},{97,65},{2,98}... | collective-permute-start | bytes 2359304 | tf_op jit(solution)/shard_map/ppermute | solution.py:257
  94.8 43.8 %copy-start.54 = (s32[288]{0:T(512)}, s32[288]{0:T(512)S(1)}, u32[]{:S(2)}) copy-start(s32[288]{0:T(512)S(1)} %get-tuple-element.73) | copy-start | bytes 3460
  94.8 43.8 %copy-start.55 = (s32[288]{0:T(512)}, s32[288]{0:T(512)S(1)}, u32[]{:S(2)}) copy-start(s32[288]{0:T(512)S(1)} %get-tuple-element.74) | copy-start | bytes 3460
  129.1 2.3 copy-start.29
  136.4 14.8 %collective-permute-start.7 = (bf16[2,144,2176]{2,1,0:T(8,128)(2,1)}, bf16[2,144,2176]{2,1,0:T(8,128)(2,1)}, u32[]{:S(2)}, u32[]{:S(2)}) collective-permute-start(bf16[2,144,2176]{2,1,0:T(8,128)(2,1)} %get-tuple-element.39), channel_id=1, source_target_pairs={{0,1},{1,0},{2,3},{3,2},{4,5},{5,4},{6,7},{7,6},{8,9},{9,8},{10,11... | collective-permute-start | bytes 3760136 | tf_op jit(solution)/shard_map/ppermute | solution.py:257
  138.5 3.6 %copy-start.56 = (pred[640]{0:T(1024)(128)(4,1)}, pred[640]{0:T(1024)(128)(4,1)S(1)}, u32[]{:S(2)}) copy-start(pred[640]{0:T(1024)(128)(4,1)S(1)} %broadcast_compare_fusion) | copy-start | bytes 1924
  144.4 6.7 %copy-start.27 = (s32[3]{0:T(128)}, s32[3]{0:T(128)S(1)}, u32[]{:S(2)}) copy-start(s32[3]{0:T(128)S(1)} %pad_add_fusion.spot) | copy-start | bytes 40
  150.3 1.2 copy-start.18
  150.3 1.3 copy-start.20
  150.3 1.7 copy-start.33
  152.0 9.8 %copy-start.11 = (bf16[576,640]{1,0:T(8,128)(2,1)S(1)}, bf16[576,640]{1,0:T(8,128)(2,1)}, u32[]{:S(2)}) copy-start(bf16[576,640]{1,0:T(8,128)(2,1)} %copy.12.sort) | copy-start | bytes 2211844
  157.5 1.6 copy-start
  160.7 1.2 copy-start.43
  161.9 1.9 copy-start.1
  167.8 1.3 copy-start.44
  175.1 1.5 copy-start.2
  176.6 1.5 copy-start.30
  179.7 7.1 %copy-start.28 = (s32[3]{0:T(128)S(1)}, s32[3]{0:T(128)}, u32[]{:S(2)}) copy-start(s32[3]{0:T(128)} %copy-done.27) | copy-start | bytes 40
  179.7 7.1 %copy-start.36 = (bf16[2,288,384]{2,1,0:T(8,128)(2,1)S(1)}, bf16[2,288,384]{2,1,0:T(8,128)(2,1)}, u32[]{:S(2)}) copy-start(bf16[2,288,384]{2,1,0:T(8,128)(2,1)} %copy-done.35) | copy-start | bytes 1327108
  179.7 70.5 %all-to-all-start.1 = ((bf16[16,2,80,512]{3,2,1,0:T(8,128)(2,1)}), bf16[16,2,80,512]{3,2,1,0:T(8,128)(2,1)S(1)}, u32[]{:S(2)}, u32[]{:S(2)}) async-start(bf16[16,2,80,512]{3,2,1,0:T(8,128)(2,1)} %bitcast.23), calls=%async_computation.1 | async-start | bytes 5242880 | tf_op jit(solution)/shard_map/all_to_all | solution.py:388
  186.8 1.7 copy-start.31
  188.5 1.3 copy-start.34
  192.8 13.9 %copy-start.52 = (s32[1280]{0:T(1024)S(1)}, s32[1280]{0:T(1024)}, u32[]{:S(2)}) copy-start(s32[1280]{0:T(1024)} %copy-done.51) | copy-start | bytes 15364
  197.6 23.8 %collective-permute-start.10 = (bf16[4,4,64,384]{3,2,1,0:T(8,128)(2,1)S(1)}, bf16[4,4,64,384]{3,2,1,0:T(8,128)(2,1)S(1)}, u32[]{:S(2)}, u32[]{:S(2)}) collective-permute-start(bf16[4,4,64,384]{3,2,1,0:T(8,128)(2,1)S(1)} %get-tuple-element.54), channel_id=1, source_target_pairs={{0,64},{32,96},{64,0},{96,32},{1,65},{33,97},{65,1},{97,33},{2,66}... | collective-permute-start | bytes 2359304 | tf_op jit(solution)/shard_map/ppermute | solution.py:257
  200.7 37.1 %collective-permute-start.11 = (bf16[4,4,64,384]{3,2,1,0:T(8,128)(2,1)S(1)}, bf16[4,4,64,384]{3,2,1,0:T(8,128)(2,1)S(1)}, u32[]{:S(2)}, u32[]{:S(2)}) collective-permute-start(bf16[4,4,64,384]{3,2,1,0:T(8,128)(2,1)S(1)} %get-tuple-element.55), channel_id=1, source_target_pairs={{0,96},{32,0},{64,32},{96,64},{1,97},{33,1},{65,33},{97,65},{2,98}... | collective-permute-start | bytes 2359304 | tf_op jit(solution)/shard_map/ppermute | solution.py:257
  204.2 33.6 %collective-permute-start.9 = (bf16[4,4,64,384]{3,2,1,0:T(8,128)(2,1)S(1)}, bf16[4,4,64,384]{3,2,1,0:T(8,128)(2,1)S(1)}, u32[]{:S(2)}, u32[]{:S(2)}) collective-permute-start(bf16[4,4,64,384]{3,2,1,0:T(8,128)(2,1)S(1)} %get-tuple-element.53), channel_id=1, source_target_pairs={{0,32},{32,64},{64,96},{96,0},{1,33},{33,65},{65,97},{97,1},{2,34}... | collective-permute-start | bytes 2359304 | tf_op jit(solution)/shard_map/ppermute | solution.py:257
  238.3 12.0 %copy-start.4 = (bf16[128,2176]{1,0:T(8,128)(2,1)S(1)}, bf16[128,2176]{1,0:T(8,128)(2,1)}, u32[]{:S(2)}) copy-start(bf16[128,2176]{1,0:T(8,128)(2,1)} %copy-done.3) | copy-start | bytes 1671172
  239.1 15.0 %collective-permute-start.12 = (bf16[4,64,384]{2,1,0:T(8,128)(2,1)}, bf16[4,64,384]{2,1,0:T(8,128)(2,1)}, u32[]{:S(2)}, u32[]{:S(2)}) collective-permute-start(bf16[4,64,384]{2,1,0:T(8,128)(2,1)} %get-tuple-element.64), channel_id=1, source_target_pairs={{0,128},{128,256},{256,384},{384,0},{1,129},{129,257},{257,385},{3... | collective-permute-start | bytes 589832 | tf_op jit(solution)/shard_map/ppermute | solution.py:257
  241.1 34.0 %collective-permute-start.13 = (bf16[4,64,384]{2,1,0:T(8,128)(2,1)}, bf16[4,64,384]{2,1,0:T(8,128)(2,1)}, u32[]{:S(2)}, u32[]{:S(2)}) collective-permute-start(bf16[4,64,384]{2,1,0:T(8,128)(2,1)} %get-tuple-element.63), channel_id=1, source_target_pairs={{0,256},{128,384},{256,0},{384,128},{1,257},{129,385},{257,1},{385... | collective-permute-start | bytes 589832 | tf_op jit(solution)/shard_map/ppermute | solution.py:257
  246.3 28.8 %collective-permute-start.14 = (bf16[4,64,384]{2,1,0:T(8,128)(2,1)}, bf16[4,64,384]{2,1,0:T(8,128)(2,1)}, u32[]{:S(2)}, u32[]{:S(2)}) collective-permute-start(bf16[4,64,384]{2,1,0:T(8,128)(2,1)} %get-tuple-element.62), channel_id=1, source_target_pairs={{0,384},{128,0},{256,128},{384,256},{1,385},{129,1},{257,129},{385... | collective-permute-start | bytes 589832 | tf_op jit(solution)/shard_map/ppermute | solution.py:257
  251.2 25.8 %copy-start.15 = (s32[128,8]{1,0:T(8,128)S(1)}, s32[128,8]{1,0:T(8,128)}, u32[]{:S(2)}) copy-start(s32[128,8]{1,0:T(8,128)} %copy-done.14) | copy-start | bytes 12292
  251.2 25.8 %copy-start.26 = (f32[128,128]{1,0:T(8,128)S(1)}, f32[128,128]{1,0:T(8,128)}, u32[]{:S(2)}) copy-start(f32[128,128]{1,0:T(8,128)} %copy-done.25) | copy-start | bytes 196612
  252.1 24.9 %collective-permute-start.8 = (bf16[128,1152]{1,0:T(8,128)(2,1)S(1)}, bf16[128,1152]{1,0:T(8,128)(2,1)S(1)}, u32[]{:S(2)}, u32[]{:S(2)}) collective-permute-start(bf16[128,1152]{1,0:T(8,128)(2,1)S(1)} %shard_map.99), channel_id=1, source_target_pairs={{0,2},{2,0},{1,3},{3,1},{4,6},{6,4},{5,7},{7,5},{8,10},{10,8},{9,1... | collective-permute-start | bytes 884744 | tf_op jit(solution)/shard_map/ppermute | solution.py:257
  (27 other events, 25.1 us)
Sparse Core Ops, SparseCore 0:
  12.8 104.1 all-gather.2

commit v5 on v4

v5 whole, which is shorter than its diff:
```python
import functools

import jax
import jax.numpy as jnp
from jax import lax
from jax.experimental import pallas as pl
from jax.experimental.pallas import tpu as pltpu
from jax.sharding import Mesh, PartitionSpec as P

BF, F32 = jnp.bfloat16, jnp.float32
HALF = 64
SLOTS = 40


def params(mebibytes):
    return pltpu.CompilerParams(vmem_limit_bytes=mebibytes * 1024 * 1024)


def cost(gflop, mebibytes):
    return pl.CostEstimate(
        flops=int(gflop * 1e9), bytes_accessed=int(mebibytes * 2**20), transcendentals=0
    )


def vmem(count):
    return [pl.BlockSpec(memory_space=pltpu.VMEM)] * count


def dot(a, b, ca=1, cb=0):
    return lax.dot_general(a, b, (((ca,), (cb,)), ((), ())), preferred_element_type=F32)


def iota(shape, dim):
    return lax.broadcasted_iota(jnp.int32, shape, dim)


def prepare_kernel(tok, gout, gates, ids, pay, table):
    rows, width = tok.shape
    line = iota((2 * HALF, rows), 0)
    expert = jnp.where(line < HALF, line, line - HALF)
    gate = gates[...].astype(F32)
    chosen = ids[...]
    gate_of = jnp.zeros((2 * HALF, rows), F32)
    named = jnp.zeros((2 * HALF, rows), F32)
    for k in range(ids.shape[0]):
        hit = chosen[k : k + 1] == expert
        gate_of = gate_of + jnp.where(hit, gate[k : k + 1], 0.0)
        named = named + jnp.where(hit, 1.0, 0.0)
    before = jnp.where(iota((rows, rows), 0) < iota((rows, rows), 1), 1.0, 0.0).astype(BF)
    place = named * (dot(named.astype(BF), before) + 1.0)
    table[...] = place[HALF:].astype(BF)
    pay[:, :width] = tok[...]
    pay[:, width : 2 * width] = gout[...]
    pay[:, 2 * width :] = jnp.where(line < HALF, gate_of, place).astype(BF)


def pick_kernel(cap, spot, gath, own, sib):
    n_z, rows, lanes = gath.shape
    width = lanes - 128
    block = n_z * cap
    gates = gath[:, :HALF, width:].reshape(n_z * HALF, 128)
    places = gath[:, HALF:, width:].reshape(n_z * HALF, 128)
    line = iota((block, n_z * HALF), 0)
    expert = lax.div(line, cap) * HALF + spot[3]
    column = iota((block, n_z * HALF), 1)
    place = (lax.rem(iota((block, 128), 0), cap) + 1).astype(F32)
    origin = lax.div(iota((block, 128), 0), cap)
    step = min(width, 512)
    for b in range(4):
        out = own if b < 2 else sib
        core = spot[2] if b < 2 else 1 - spot[2]
        sel = jnp.where(column == expert + (2 * core + b % 2), 1.0, 0.0).astype(BF)
        hit = dot(sel, places) == place
        gate = jnp.sum(jnp.where(hit, dot(sel, gates), 0.0), axis=1, keepdims=True)
        ones = jnp.where(hit, 1.0, 0.0)
        pick = jnp.concatenate(
            [jnp.where(origin == s, ones, 0.0).astype(BF) for s in range(n_z)], axis=1
        )
        for c in range(0, width, step):
            data = gath[:, :, c : c + step].reshape(n_z * rows, step)
            out[b % 2, :, c : c + step] = dot(pick, data).astype(BF)
        out[b % 2, :, width:] = jnp.broadcast_to(gate, (block, 128)).astype(BF)


def expert_kernel(n_y, n_x, cap, spot, *refs):
    w_in, (own, got, sent) = refs[:n_x], refs[n_x : n_x + 3]
    g_out, back = refs[n_x + 3 : 2 * n_x + 3], refs[2 * n_x + 3]
    weights, parts, rows, grads, marks, masks = refs[2 * n_x + 4 :]
    share = w_in[0].shape[2]
    width, hidden_len = weights.shape[1:]
    n_z, _, many, _ = sent.shape
    block = n_z * cap
    half = width // 2

    for i in range(n_y):
        for d in range(n_x):
            group = lax.rem(spot[0] + n_y - i, n_y) * n_x + lax.rem(spot[1] + n_x - d, n_x)
            start = pl.multiple_of(group * share, share)
            for m in range(4):
                weights[m, pl.ds(start, share), :] = w_in[d][i, m]

    column = iota((1, 2 * block), 1)
    slot = jnp.where(column < block, 0, cap) + lax.rem(column, cap)
    device = lax.div(jnp.where(column < block, column, column - block), cap) * many
    line = iota((n_z * many, 2 * block), 0)
    for m, at in enumerate((device + slot, device + slot + SLOTS, device + 2 * cap)):
        masks[m] = jnp.where(line == at, 1.0, 0.0).astype(BF)
    down_line = iota((2 * block, 128), 0)
    slot = jnp.where(down_line < block, 0, cap) + lax.rem(down_line, cap)
    lane_of = jnp.where(slot == iota((2 * block, 128), 1), 1.0, 0.0)

    gates = []
    step = min(width, 512)
    for b in range(2):
        data = sent[:, b].reshape(n_z * many, width)
        for m in range(2):
            for c in range(0, width, step):
                value = dot(masks[m], data[:, c : c + step], 0, 0).astype(BF)
                for e in range(2):
                    to = slice(b * block, (b + 1) * block)
                    rows[m, e, to, c : c + step] = value[e * block : (e + 1) * block]
        line = dot(masks[2], data[:, :128], 0, 0) * lane_of
        gates.append(jnp.sum(line, axis=1, keepdims=True))

    for e in range(2):
        up, down = weights[2 * e], weights[2 * e + 1]
        x = jnp.concatenate([own[e, :, :width], got[e, :, :width], rows[0, e]], axis=0)
        g = jnp.concatenate(
            [own[e, :, width : 2 * width], got[e, :, width : 2 * width], rows[1, e]], axis=0
        )
        gate = jnp.concatenate(
            [r[e, :, 2 * width :].astype(F32)[:, :1] for r in (own, got)]
            + [v[e * block : (e + 1) * block] for v in gates],
            axis=0,
        )
        pre = dot(x, up)
        q = dot(g, down)
        s = jax.nn.sigmoid(pre)
        hidden = pre * s
        score = jnp.sum(hidden.astype(BF).astype(F32) * q, axis=1, keepdims=True)
        grad_a = (gate * q * (s * (1.0 + pre * (1.0 - s)))).astype(BF)
        parts[:, 2 * e] = dot(x, grad_a, 0, 0).astype(BF).reshape(-1, share, hidden_len)
        parts[:, 2 * e + 1] = (
            dot(g, (gate * hidden).astype(BF), 0, 0).astype(BF).reshape(-1, share, hidden_len)
        )
        out = dot(grad_a, up, 1, 1).astype(BF)
        for b in range(4):
            part = slice(b * block, (b + 1) * block)
            to = slice(e * block, (e + 1) * block)
            grads[b, to] = out[part]
            marks[b, to] = (score[part] * lane_of[to]).astype(BF)
    for b in range(4):
        at = lax.bitwise_xor(spot[2], b) if b < 2 else b - 2
        left = dot(masks[0], grads[b, :, :half]) + dot(masks[1], grads[b, :, half:])
        first = left[:, :128] + dot(masks[2], marks[b])
        back[:, at, b // 2, :, :128] = first.astype(BF).reshape(n_z, many, 128)
        back[:, at, b // 2, :, 128:] = left[:, 128:].astype(BF).reshape(n_z, many, half - 128)
    for d in range(n_x):
        for i in range(n_y):
            g_out[d][i] = parts[lax.rem(spot[0] + i, n_y) * n_x + lax.rem(spot[1] + d, n_x)]


def send_kernel(cap, pay, sel, place, out):
    n_dev, many, width = out.shape
    half = many // 2
    meta = pay[:, 2 * width :]
    hit = dot(sel[...], meta[HALF:]) == place[...]
    gate = jnp.sum(jnp.where(hit, dot(sel[...], meta[:HALF]), 0.0), axis=1, keepdims=True)
    row = lax.rem(iota(hit.shape, 0), many)
    ones = jnp.where(hit, 1.0, 0.0)
    pick_x = jnp.where(row < half, ones, 0.0).astype(BF)
    pick_g = jnp.where(row < half, 0.0, ones).astype(BF)
    line = jnp.where(row == iota(hit.shape, 1), gate, 0.0).reshape(n_dev, many, 128)
    line = jnp.sum(line, axis=1, keepdims=True)
    line = jnp.where(iota((n_dev, many, 128), 1) == 2 * cap, line, 0.0).reshape(n_dev * many, 128)
    step = min(width, 512)
    for c in range(0, width, step):
        lanes, g_lanes = slice(c, c + step), slice(width + c, width + c + step)
        value = dot(pick_x, pay[:, lanes]) + dot(pick_g, pay[:, g_lanes])
        if c == 0:
            value = jnp.concatenate((value[:, :128] + line, value[:, 128:]), axis=1)
        out[:, :, lanes] = value.astype(BF).reshape(n_dev, many, step)


def total_kernel(*refs):
    *ends, up, down = refs
    for e in range(2):
        up[e] = sum(r[2 * e].astype(F32) for r in ends).astype(BF)
        down[e] = sum(r[2 * e + 1].astype(F32) for r in ends).astype(BF)


def partial_sums(cap, got, which, at, lane_places, owners, slots, place_l, place_r):
    n_dev, _, _, half = got.shape
    data = got[:, which].reshape(n_dev * 2 * SLOTS, half)
    left = dot((at == place_l[...]).astype(F32).astype(BF), data)
    right = dot((at == place_r[...]).astype(F32).astype(BF), data)
    lines = got[:, which, 32:48, :128].reshape(n_dev * 16, 128)
    by_place = jnp.zeros((slots.shape[1], 128), F32)
    for m in range(2):
        by_place = by_place + dot(dot(slots[m], lines, 1, 1).astype(BF), owners[m])
    scores = jnp.zeros(lane_places.shape, F32)
    for r in range(cap):
        scores = scores + jnp.where(lane_places == r + 1.0, by_place[r : r + 1, :], 0.0)
    return left, right, scores


def places_of(table, sel):
    same = jnp.where(iota((HALF, 128), 0) == iota((HALF, 128), 1), 1.0, 0.0).astype(BF)
    return dot(table, sel[...], 0, 0), dot(table, same, 0, 0)


def partner_kernel(cap, got, pay, sel, owners, slots, place_l, place_r, out):
    width = out.shape[1] - 128
    half = width // 2
    at, by_expert = places_of(pay[HALF:, 2 * width :], sel)
    left, right, scores = partial_sums(cap, got, 1, at, by_expert, owners, slots, place_l, place_r)
    out[:, :half] = left.astype(BF)
    out[:, half:width] = right.astype(BF)
    out[:, width:] = scores.astype(BF)


def combine_kernel(cap, got, table, ids, sel, owners, slots, place_l, place_r, other, grad_tok, grad_gate):
    rows, width = grad_tok.shape
    half = width // 2
    at, by_expert = places_of(table[...], sel)
    left, right, scores = partial_sums(cap, got, 0, at, by_expert, owners, slots, place_l, place_r)
    grad_tok[:, :half] = (left + other[:, :half].astype(F32)).astype(BF)
    grad_tok[:, half:] = (right + other[:, half:width].astype(F32)).astype(BF)
    scores = (scores + other[:, width:].astype(F32)).T
    expert = iota((128, rows), 0)
    line = iota(ids.shape, 0)
    chosen = ids[...]
    total = jnp.zeros(ids.shape, F32)
    for k in range(ids.shape[0]):
        score = jnp.where(chosen[k : k + 1] == expert, scores, 0.0)
        total = total + jnp.where(line == k, jnp.sum(score, axis=0, keepdims=True), 0.0)
    grad_gate[...] = total.astype(BF)


def shift(value, axis, by):
    n = lax.axis_size(axis)
    return lax.ppermute(value, axis, [(i, (i + by) % n) for i in range(n)])


def held(*values):
    return lax.optimization_barrier(values)


def per_device(tokens, grad_out, gates, expert_ids, w_up, w_down):
    rows, width = tokens.shape
    top = expert_ids.shape[1]
    n_y, n_x, n_z = lax.axis_size("yl"), lax.axis_size("x"), lax.axis_size("z")
    experts = 8 * n_z
    cap = rows * top * 9 // (8 * experts)
    block = n_z * cap
    share, hidden_len = w_up.shape[1:]
    half = width // 2
    yl, x, z, yh, c = [lax.axis_index(a) for a in ("yl", "x", "z", "yh", "c")]
    shape = jax.ShapeDtypeStruct

    pay, table = pl.pallas_call(
        prepare_kernel,
        out_shape=(shape((rows, 2 * width + 128), BF), shape((HALF, rows), BF)),
        in_specs=vmem(4),
        out_specs=tuple(vmem(2)),
        cost_estimate=cost(0.1, 2),
        compiler_params=params(8),
    )(tokens, grad_out, gates.T, expert_ids.T)
    spot = jnp.stack([yl, x, c, (z * 2 + yh) * 4]).astype(jnp.int32)
    smem = [pl.BlockSpec(memory_space=pltpu.SMEM)]
    gath = lax.all_gather(pay, "z", axis=0)
    pay_other = shift(pay, "yh", 1)
    n_dev = 2 * n_z
    many = 2 * SLOTS

    p = jnp.arange(n_dev * many)
    dev_p, s_p = p // many, p % many
    q = s_p % SLOTS
    first_of = ((dev_p // 2 * 2 + yh) * 2 + dev_p % 2) * 2
    e_p = first_of + (q >= cap)
    tgt = jnp.where(q < 2 * cap, q % cap + 1, -1)
    sel_s = (e_p[:, None] == jnp.arange(HALF)[None, :]).astype(BF)
    place_s = jnp.broadcast_to(tgt.astype(F32)[:, None], (n_dev * many, 128))
    sent = pl.pallas_call(
        functools.partial(send_kernel, cap),
        out_shape=shape((n_dev, many, width), BF),
        in_specs=vmem(3),
        out_specs=vmem(1)[0],
        cost_estimate=cost(1, 6),
        compiler_params=params(20),
    )(pay_other, sel_s, place_s)
    got_rows = lax.all_to_all(sent, ("z", "c"), 0, 0, tiled=True)

    w_mine = jnp.stack((w_up, jnp.transpose(w_down, (0, 2, 1))), axis=1)
    w_mine = w_mine.reshape(4, share, hidden_len)
    w_mine, _ = held(w_mine, sent)
    w_line = jnp.stack([w_mine] + [shift(w_mine, "yl", d) for d in range(1, n_y)])
    w_parts = [w_line] + [shift(w_line, "x", d) for d in range(1, n_x)]
    gath, *w_parts = held(gath, *w_parts)

    a_own, a_sib = pl.pallas_call(
        functools.partial(pick_kernel, cap),
        out_shape=(shape((2, block, 2 * width + 128), BF),) * 2,
        in_specs=smem + vmem(1),
        out_specs=tuple(vmem(2)),
        cost_estimate=cost(2.6, 12),
        compiler_params=params(20),
    )(spot, gath)
    a_got = shift(a_sib, "c", 1)
    *parts, back = pl.pallas_call(
        functools.partial(expert_kernel, n_y, n_x, cap),
        out_shape=(shape((n_y, 4, share, hidden_len), BF),) * n_x
        + (shape((n_z, 2, 2, many, half), BF),),
        in_specs=smem + vmem(n_x + 3),
        out_specs=tuple(vmem(n_x + 1)),
        scratch_shapes=[
            pltpu.VMEM((4, width, hidden_len), BF),
            pltpu.VMEM((n_y * n_x, 4, share, hidden_len), BF),
            pltpu.VMEM((2, 2, 2 * block, width), BF),
            pltpu.VMEM((4, 2 * block, width), BF),
            pltpu.VMEM((4, 2 * block, 128), BF),
            pltpu.VMEM((3, n_z * many, 2 * block), BF),
        ],
        cost_estimate=cost(9, 24),
        compiler_params=params(44),
    )(spot, *w_parts, a_own, a_got, got_rows.reshape(n_z, 2, many, width))
    got = lax.all_to_all(back.reshape(n_dev, 2, many, half), ("z", "c"), 0, 0, tiled=True)

    lines = [parts[0]] + [shift(parts[d], "x", d) for d in range(1, n_x)]
    line = sum(u.astype(F32) for u in lines).astype(BF)
    ends = [line[0]] + [shift(line[d], "yl", d) for d in range(1, n_y)]
    grad_up, grad_down = pl.pallas_call(
        total_kernel,
        out_shape=(shape((2, share, hidden_len), BF),) * 2,
        in_specs=vmem(n_y),
        out_specs=tuple(vmem(2)),
        cost_estimate=cost(0, 2),
        compiler_params=params(6),
    )(*ends)
    grad_down = jnp.transpose(grad_down, (0, 2, 1))

    sel_p = (jnp.arange(HALF)[:, None] == e_p[None, :]).astype(BF)
    place_l = jnp.where(s_p < SLOTS, tgt, -1).astype(F32)[None, :]
    place_r = jnp.where(s_p >= SLOTS, tgt, -1).astype(F32)[None, :]
    line_o = jnp.arange(n_dev * 16)
    first_o = ((line_o // 32 * 2 + yh) * 2 + line_o // 16 % 2) * 2
    first_o = jnp.where(line_o % 16 == 2 * cap - 32, first_o, -2)
    parity = jnp.arange(2)[:, None, None]
    owners = (first_o[None, :, None] + parity == jnp.arange(128)[None, None, :]).astype(BF)
    at_slot = jnp.arange(24)[None, :, None]
    slots = (
        (at_slot < cap) & (jnp.arange(128)[None, None, :] == at_slot + parity * cap)
    ).astype(BF)
    partner = pl.pallas_call(
        functools.partial(partner_kernel, cap),
        out_shape=shape((rows, width + 128), BF),
        in_specs=vmem(7),
        out_specs=vmem(1)[0],
        cost_estimate=cost(0.4, 4),
        compiler_params=params(12),
    )(got, pay_other, sel_p, owners, slots, place_l, place_r)
    other = shift(partner, "yh", 1)
    grad_tokens, grad_gates = pl.pallas_call(
        functools.partial(combine_kernel, cap),
        out_shape=(shape((rows, width), BF), shape((top, rows), BF)),
        in_specs=vmem(9),
        out_specs=tuple(vmem(2)),
        cost_estimate=cost(0.4, 4),
        compiler_params=params(12),
    )(got, table, expert_ids.T, sel_p, owners, slots, place_l, place_r, other)
    return (grad_tokens, grad_gates.T, grad_up, grad_down)


def build(mesh):
    every, dp, ctx = ("yl", "x", "z", "yh", "c"), ("yl", "x"), ("z", "yh", "c")
    tok, up, down = P(every, None), P(ctx, dp, None), P(ctx, None, dp)
    return jax.shard_map(
        per_device,
        mesh=mesh,
        in_specs=(tok, tok, tok, tok, up, down),
        out_specs=(tok, tok, up, down),
        check_vma=False,
    )


def solution(mesh):
    return build(Mesh(mesh.devices.reshape(4, 4, 8, 2, 2), ("yl", "x", "z", "yh", "c")))
```

time: 288 us -> 275 us (0.955)
  the two profiles are of different devices: /device:TPU:58 before, /device:TPU:11 now
where the time goes in v5:
time: 275 us; the launch traced here: 274 us
  waiting for transfers between devices  143 us (52%)
  starting transfers between devices  71.4 us (26%)
  Pallas kernels  28.8 us (10%)
  between operations  14.3 us (5%)
  local copies, waits for them, and re-layouts  12.3 us (4%)
  other arithmetic  3.46 us (1%)
    ppermute x15, waiting for transfers between devices, shift(): return lax.ppermute(value, axis, [(i, (i + by) % n) for i in range(n)])  126 us
    ppermute x15, starting transfers between devices, shift(): return lax.ppermute(value, axis, [(i, (i + by) % n) for i in range(n)])  50.6 us
    all_to_all x1, waiting for transfers between devices, per_device(): lax.all_to_all(back.reshape(n_dev, 2, many, half), ('z', 'c'), 0, 0, tile...  17 us
    pallas_call x1, Pallas kernels, per_device(): pl.pallas_call(functools.partial(expert_kernel, n_y, n_x, cap), out_shape...  16.5 us
    all_to_all x1, starting transfers between devices, per_device(): got_rows = lax.all_to_all(sent, ('z', 'c'), 0, 0, tiled=True)  13.6 us
    unnamed x34, local copies, waits for them, and re-layouts  12 us
    all_to_all x1, starting transfers between devices, per_device(): lax.all_to_all(back.reshape(n_dev, 2, many, half), ('z', 'c'), 0, 0, tile...  7.22 us
  transfers between devices with their start and end apart: 18, of which 13 were waited for; matrix products, arithmetic and copies ran while one was open for 1% of the time, Pallas kernels for 3%

profile of v5, /device:TPU:11, one launch (start us, length us, event | category | flops | bytes accessed | tf_op | source)
XLA Modules:
  0.0 273.8 jit_solution(903697752915166543)
XLA Ops:
  7.2 0.9 copy-done.1
  8.2 0.9 copy-done.2
  9.1 0.7 copy-done.3
  10.5 1.0 shard_map.93
  11.5 6.6 %collective-permute-start = (bf16[128,2176]{1,0:T(8,128)(2,1)}, bf16[128,2176]{1,0:T(8,128)(2,1)S(1)}, u32[]{:S(2)}, u32[]{:S(2)}) collective-permute-start(bf16[128,2176]{1,0:T(8,128)(2,1)} %get-tuple-element.23), channel_id=1, source_target_pairs={{0,2},{2,0},{1,3},{3,1},{4,6},{6,4},{5,7},{7,5},{8,10},{10,8},{9,1... | collective-permute-start | bytes 1671176 | tf_op jit(solution)/shard_map/ppermute | solution.py:242
  18.4 23.0 %collective-permute-done.pay = bf16[128,2176]{1,0:T(8,128)(2,1)S(1)} collective-permute-done((bf16[128,2176]{1,0:T(8,128)(2,1)}, bf16[128,2176]{1,0:T(8,128)(2,1)S(1)}, u32[]{:S(2)}, u32[]{:S(2)}) %collective-permute-start) | collective-permute-done | bytes 557088 | tf_op jit(solution)/shard_map/ppermute | solution.py:242
  41.6 3.3 %shard_map.94 = bf16[16,80,1024]{2,1,0:T(8,128)(2,1)} custom-call(bf16[128,2176]{1,0:T(8,128)(2,1)S(1)} %collective-permute-done.pay, bf16[1280,64]{1,0:T(8,128)(2,1)S(1)} %fusion.sel, f32[1280,128]{1,0:T(8,128)S(1)} %broadcast_in_dim.9.place), custom_call_target="tpu_custom_call" | custom-call | flops 1000000000 | bytes 6291456 | tf_op jit(solution)/shard_map/pallas_call | solution.py:284
  44.9 13.6 %all-to-all-start = ((bf16[16,80,1024]{2,1,0:T(8,128)(2,1)}), bf16[16,80,1024]{2,1,0:T(8,128)(2,1)}, u32[]{:S(2)}, u32[]{:S(2)}) async-start(bf16[16,80,1024]{2,1,0:T(8,128)(2,1)} %shard_map.94), calls=%async_computation | async-start | bytes 5242880 | tf_op jit(solution)/shard_map/all_to_all | solution.py:292
  58.6 3.4 %collective-permute-start.1 = (bf16[4,64,384]{2,1,0:T(8,128)(2,1)S(1)}, bf16[4,64,384]{2,1,0:T(8,128)(2,1)S(1)}, u32[]{:S(2)}, u32[]{:S(2)}) collective-permute-start(bf16[4,64,384]{2,1,0:T(8,128)(2,1)S(1)} %bitcast.33), channel_id=1, source_target_pairs={{0,128},{128,256},{256,384},{384,0},{1,129},{129,257},{257,385},{3... | collective-permute-start | bytes 589832 | tf_op jit(solution)/shard_map/ppermute | solution.py:242
  61.9 2.3 collective-permute-start.2
  64.3 2.7 collective-permute-start.3
  67.0 11.7 %collective-permute-done.2 = bf16[4,64,384]{2,1,0:T(8,128)(2,1)S(1)} collective-permute-done((bf16[4,64,384]{2,1,0:T(8,128)(2,1)S(1)}, bf16[4,64,384]{2,1,0:T(8,128)(2,1)S(1)}, u32[]{:S(2)}, u32[]{:S(2)}) %collective-permute-start.2) | collective-permute-done | bytes 196640 | tf_op jit(solution)/shard_map/ppermute | solution.py:242
  78.7 1.8 collective-permute-done.3
  80.6 3.1 %collective-permute-start.4 = (bf16[4,4,64,384]{3,2,1,0:T(8,128)(2,1)S(1)}, bf16[4,4,64,384]{3,2,1,0:T(8,128)(2,1)S(1)}, u32[]{:S(2)}, u32[]{:S(2)}) collective-permute-start(bf16[4,4,64,384]{3,2,1,0:T(8,128)(2,1)S(1)} %pad_maximum_fusion.refs_0_), channel_id=1, source_target_pairs={{0,32},{32,64},{64,96},{96,0},{1,33},{33,65},{65,97},{97,1},{2,34}... | collective-permute-start | bytes 2359304 | tf_op jit(solution)/shard_map/ppermute | solution.py:242
  83.8 2.7 %collective-permute-start.5 = (bf16[4,4,64,384]{3,2,1,0:T(8,128)(2,1)S(1)}, bf16[4,4,64,384]{3,2,1,0:T(8,128)(2,1)S(1)}, u32[]{:S(2)}, u32[]{:S(2)}) collective-permute-start(bf16[4,4,64,384]{3,2,1,0:T(8,128)(2,1)S(1)} %pad_maximum_fusion.refs_0_), channel_id=1, source_target_pairs={{0,64},{32,96},{64,0},{96,32},{1,65},{33,97},{65,1},{97,33},{2,66}... | collective-permute-start | bytes 2359304 | tf_op jit(solution)/shard_map/ppermute | solution.py:242
  86.5 3.8 %collective-permute-start.6 = (bf16[4,4,64,384]{3,2,1,0:T(8,128)(2,1)S(1)}, bf16[4,4,64,384]{3,2,1,0:T(8,128)(2,1)}, u32[]{:S(2)}, u32[]{:S(2)}) collective-permute-start(bf16[4,4,64,384]{3,2,1,0:T(8,128)(2,1)S(1)} %pad_maximum_fusion.refs_0_), channel_id=1, source_target_pairs={{0,96},{32,0},{64,32},{96,64},{1,97},{33,1},{65,33},{97,65},{2,98}... | collective-permute-start | bytes 2359304 | tf_op jit(solution)/shard_map/ppermute | solution.py:242
  90.4 11.0 %collective-permute-done.4.refs_1_ = bf16[4,4,64,384]{3,2,1,0:T(8,128)(2,1)S(1)} collective-permute-done((bf16[4,4,64,384]{3,2,1,0:T(8,128)(2,1)S(1)}, bf16[4,4,64,384]{3,2,1,0:T(8,128)(2,1)S(1)}, u32[]{:S(2)}, u32[]{:S(2)}) %collective-permute-start.4) | collective-permute-done | bytes 786464 | tf_op jit(solution)/shard_map/ppermute | solution.py:242
  101.4 4.4 %collective-permute-done.5.refs_2_ = bf16[4,4,64,384]{3,2,1,0:T(8,128)(2,1)S(1)} collective-permute-done((bf16[4,4,64,384]{3,2,1,0:T(8,128)(2,1)S(1)}, bf16[4,4,64,384]{3,2,1,0:T(8,128)(2,1)S(1)}, u32[]{:S(2)}, u32[]{:S(2)}) %collective-permute-start.5) | collective-permute-done | bytes 786464 | tf_op jit(solution)/shard_map/ppermute | solution.py:242
  105.7 17.8 %collective-permute-done.6.refs_3_ = bf16[4,4,64,384]{3,2,1,0:T(8,128)(2,1)} collective-permute-done((bf16[4,4,64,384]{3,2,1,0:T(8,128)(2,1)S(1)}, bf16[4,4,64,384]{3,2,1,0:T(8,128)(2,1)}, u32[]{:S(2)}, u32[]{:S(2)}) %collective-permute-start.6) | collective-permute-done | bytes 786464 | tf_op jit(solution)/shard_map/ppermute | solution.py:242
  123.6 2.3 copy-done.6
  125.8 4.8 %shard_map.95 = (bf16[2,144,2176]{2,1,0:T(8,128)(2,1)S(1)}, bf16[2,144,2176]{2,1,0:T(8,128)(2,1)}) custom-call(s32[4]{0:T(128)S(1)} %pad_add_fusion.spot, bf16[8,128,2176]{2,1,0:T(8,128)(2,1)S(1)} %bitcast.31), custom_call_target="tpu_custom_call" | custom-call | flops 2600000000 | bytes 12582912 | tf_op jit(solution)/shard_map/pallas_call | solution.py:301
  130.7 1.1 copy-done.12
  131.8 2.6 collective-permute-start.7
  134.3 2.6 collective-permute-done.7.refs_5_
  136.9 1.1 copy-done.8
  138.1 1.3 copy-done.13
  139.4 16.5 %shard_map.96 = (bf16[4,4,64,384]{3,2,1,0:T(8,128)(2,1)S(1)}, bf16[4,4,64,384]{3,2,1,0:T(8,128)(2,1)S(1)}, bf16[4,4,64,384]{3,2,1,0:T(8,128)(2,1)S(1)}, bf16[4,4...) custom-call(s32[4]{0:T(128)S(1)} %pad_add_fusion.spot, bf16[4,4,64,384]{3,2,1,0:T(8,128)(2,1)S(1)} %pad_maximum_fusion.refs_0_, ...), custom_call_target="tpu_custom_call" | custom-call | flops 8999999488 | bytes 25165824 | tf_op jit(solution)/shard_map/pallas_call | solution.py:310
  155.9 0.9 copy-done
  156.8 0.9 copy-done.9
  157.6 0.9 copy-done.10
  158.8 7.2 %all-to-all-start.1 = ((bf16[16,2,80,512]{3,2,1,0:T(8,128)(2,1)}), bf16[16,2,80,512]{3,2,1,0:T(8,128)(2,1)S(1)}, u32[]{:S(2)}, u32[]{:S(2)}) async-start(bf16[16,2,80,512]{3,2,1,0:T(8,128)(2,1)} %bitcast.32), calls=%async_computation.1 | async-start | bytes 5242880 | tf_op jit(solution)/shard_map/all_to_all | solution.py:327
  166.3 2.8 %collective-permute-start.10 = (bf16[4,4,64,384]{3,2,1,0:T(8,128)(2,1)}, bf16[4,4,64,384]{3,2,1,0:T(8,128)(2,1)S(1)}, u32[]{:S(2)}, u32[]{:S(2)}) collective-permute-start(bf16[4,4,64,384]{3,2,1,0:T(8,128)(2,1)} %copy-done.11), channel_id=1, source_target_pairs={{0,64},{32,96},{64,0},{96,32},{1,65},{33,97},{65,1},{97,33},{2,66}... | collective-permute-start | bytes 2359304 | tf_op jit(solution)/shard_map/ppermute | solution.py:242
  169.1 3.2 %collective-permute-start.11 = (bf16[4,4,64,384]{3,2,1,0:T(8,128)(2,1)}, bf16[4,4,64,384]{3,2,1,0:T(8,128)(2,1)S(1)}, u32[]{:S(2)}, u32[]{:S(2)}) collective-permute-start(bf16[4,4,64,384]{3,2,1,0:T(8,128)(2,1)} %copy-done.10), channel_id=1, source_target_pairs={{0,96},{32,0},{64,32},{96,64},{1,97},{33,1},{65,33},{97,65},{2,98}... | collective-permute-start | bytes 2359304 | tf_op jit(solution)/shard_map/ppermute | solution.py:242
  172.3 2.3 collective-permute-start.9
  174.8 14.3 %collective-permute-done.10 = bf16[4,4,64,384]{3,2,1,0:T(8,128)(2,1)S(1)} collective-permute-done((bf16[4,4,64,384]{3,2,1,0:T(8,128)(2,1)}, bf16[4,4,64,384]{3,2,1,0:T(8,128)(2,1)S(1)}, u32[]{:S(2)}, u32[]{:S(2)}) %collective-permute-start.10) | collective-permute-done | bytes 786464 | tf_op jit(solution)/shard_map/ppermute | solution.py:242
  189.1 17.2 %collective-permute-done.11 = bf16[4,4,64,384]{3,2,1,0:T(8,128)(2,1)S(1)} collective-permute-done((bf16[4,4,64,384]{3,2,1,0:T(8,128)(2,1)}, bf16[4,4,64,384]{3,2,1,0:T(8,128)(2,1)S(1)}, u32[]{:S(2)}, u32[]{:S(2)}) %collective-permute-start.11) | collective-permute-done | bytes 786464 | tf_op jit(solution)/shard_map/ppermute | solution.py:242
  206.3 2.5 add_convert_fusion
  208.8 17.0 %all-to-all-done.1.got = bf16[16,2,80,512]{3,2,1,0:T(8,128)(2,1)S(1)} async-done(((bf16[16,2,80,512]{3,2,1,0:T(8,128)(2,1)}), bf16[16,2,80,512]{3,2,1,0:T(8,128)(2,1)S(1)}, u32[]{:S(2)}, u32[]{:S(2)}) %all-to-all-start.1) | async-done | bytes 2621472 | tf_op jit(solution)/shard_map/all_to_all | solution.py:327
  225.8 0.9 shard_map.97
  226.7 7.9 %collective-permute-start.8 = (bf16[128,1152]{1,0:T(8,128)(2,1)S(1)}, bf16[128,1152]{1,0:T(8,128)(2,1)S(1)}, u32[]{:S(2)}, u32[]{:S(2)}) collective-permute-start(bf16[128,1152]{1,0:T(8,128)(2,1)S(1)} %shard_map.97), channel_id=1, source_target_pairs={{0,2},{2,0},{1,3},{3,1},{4,6},{6,4},{5,7},{7,5},{8,10},{10,8},{9,1... | collective-permute-start | bytes 884744 | tf_op jit(solution)/shard_map/ppermute | solution.py:242
  234.8 1.9 collective-permute-start.12
  236.7 1.9 collective-permute-start.13
  238.6 3.4 %collective-permute-start.14 = (bf16[4,64,384]{2,1,0:T(8,128)(2,1)S(1)}, bf16[4,64,384]{2,1,0:T(8,128)(2,1)S(1)}, u32[]{:S(2)}, u32[]{:S(2)}) collective-permute-start(bf16[4,64,384]{2,1,0:T(8,128)(2,1)S(1)} %get-tuple-element.42), channel_id=1, source_target_pairs={{0,384},{128,0},{256,128},{384,256},{1,385},{129,1},{257,129},{385... | collective-permute-start | bytes 589832 | tf_op jit(solution)/shard_map/ppermute | solution.py:242
  242.0 7.6 %collective-permute-done.12.refs_1_ = bf16[4,64,384]{2,1,0:T(8,128)(2,1)S(1)} collective-permute-done((bf16[4,64,384]{2,1,0:T(8,128)(2,1)S(1)}, bf16[4,64,384]{2,1,0:T(8,128)(2,1)S(1)}, u32[]{:S(2)}, u32[]{:S(2)}) %collective-permute-start.12) | collective-permute-done | bytes 196640 | tf_op jit(solution)/shard_map/ppermute | solution.py:242
  249.7 11.6 %collective-permute-done.13.refs_2_ = bf16[4,64,384]{2,1,0:T(8,128)(2,1)S(1)} collective-permute-done((bf16[4,64,384]{2,1,0:T(8,128)(2,1)S(1)}, bf16[4,64,384]{2,1,0:T(8,128)(2,1)S(1)}, u32[]{:S(2)}, u32[]{:S(2)}) %collective-permute-start.13) | collective-permute-done | bytes 196640 | tf_op jit(solution)/shard_map/ppermute | solution.py:242
  261.2 3.4 %collective-permute-done.14.refs_3_ = bf16[4,64,384]{2,1,0:T(8,128)(2,1)S(1)} collective-permute-done((bf16[4,64,384]{2,1,0:T(8,128)(2,1)S(1)}, bf16[4,64,384]{2,1,0:T(8,128)(2,1)S(1)}, u32[]{:S(2)}, u32[]{:S(2)}) %collective-permute-start.14) | collective-permute-done | bytes 196640 | tf_op jit(solution)/shard_map/ppermute | solution.py:242
  264.7 0.8 shard_map.99
  265.4 1.6 shard_map.98
  (49 shorter events, 2.3 us)
Async XLA Ops:
  7.2 116.4 %all-gather.3.cloned.1.call-start = ((), (), s32[]{:S(2)}) async-start(), calls=%async_computation.2 | async-start | bytes 5013504 | tf_op jit(solution)/shard_map/all_gather | solution.py:271
  7.2 1.0 copy-start.1
  8.2 0.9 copy-start.2
  9.1 0.7 copy-start.3
  9.8 0.7 copy-start.5
  11.5 29.9 %collective-permute-start = (bf16[128,2176]{1,0:T(8,128)(2,1)}, bf16[128,2176]{1,0:T(8,128)(2,1)S(1)}, u32[]{:S(2)}, u32[]{:S(2)}) collective-permute-start(bf16[128,2176]{1,0:T(8,128)(2,1)} %get-tuple-element.23), channel_id=1, source_target_pairs={{0,2},{2,0},{1,3},{3,1},{4,6},{6,4},{5,7},{7,5},{8,10},{10,8},{9,1... | collective-permute-start | bytes 1671176 | tf_op jit(solution)/shard_map/ppermute | solution.py:242
  44.9 13.6 %copy-start.15 = (bf16[2,384,64]{1,2,0:T(8,128)(2,1)S(1)}, bf16[2,384,64]{1,2,0:T(8,128)(2,1)}, u32[]{:S(2)}) copy-start(bf16[2,384,64]{1,2,0:T(8,128)(2,1)} %param.11) | copy-start | bytes 294916
  44.9 13.6 %copy-start.16 = (bf16[2,64,384]{2,1,0:T(8,128)(2,1)S(1)}, bf16[2,64,384]{2,1,0:T(8,128)(2,1)}, u32[]{:S(2)}) copy-start(bf16[2,64,384]{2,1,0:T(8,128)(2,1)} %param.10) | copy-start | bytes 294916
  44.9 89.4 %all-to-all-start = ((bf16[16,80,1024]{2,1,0:T(8,128)(2,1)}), bf16[16,80,1024]{2,1,0:T(8,128)(2,1)}, u32[]{:S(2)}, u32[]{:S(2)}) async-start(bf16[16,80,1024]{2,1,0:T(8,128)(2,1)} %shard_map.94), calls=%async_computation | async-start | bytes 5242880 | tf_op jit(solution)/shard_map/all_to_all | solution.py:292
  58.6 8.4 %collective-permute-start.1 = (bf16[4,64,384]{2,1,0:T(8,128)(2,1)S(1)}, bf16[4,64,384]{2,1,0:T(8,128)(2,1)S(1)}, u32[]{:S(2)}, u32[]{:S(2)}) collective-permute-start(bf16[4,64,384]{2,1,0:T(8,128)(2,1)S(1)} %bitcast.33), channel_id=1, source_target_pairs={{0,128},{128,256},{256,384},{384,0},{1,129},{129,257},{257,385},{3... | collective-permute-start | bytes 589832 | tf_op jit(solution)/shard_map/ppermute | solution.py:242
  61.9 16.8 %collective-permute-start.2 = (bf16[4,64,384]{2,1,0:T(8,128)(2,1)S(1)}, bf16[4,64,384]{2,1,0:T(8,128)(2,1)S(1)}, u32[]{:S(2)}, u32[]{:S(2)}) collective-permute-start(bf16[4,64,384]{2,1,0:T(8,128)(2,1)S(1)} %bitcast.34), channel_id=1, source_target_pairs={{0,256},{128,384},{256,0},{384,128},{1,257},{129,385},{257,1},{385... | collective-permute-start | bytes 589832 | tf_op jit(solution)/shard_map/ppermute | solution.py:242
  64.3 16.2 %collective-permute-start.3 = (bf16[4,64,384]{2,1,0:T(8,128)(2,1)S(1)}, bf16[4,64,384]{2,1,0:T(8,128)(2,1)S(1)}, u32[]{:S(2)}, u32[]{:S(2)}) collective-permute-start(bf16[4,64,384]{2,1,0:T(8,128)(2,1)S(1)} %bitcast.35), channel_id=1, source_target_pairs={{0,384},{128,0},{256,128},{384,256},{1,385},{129,1},{257,129},{385... | collective-permute-start | bytes 589832 | tf_op jit(solution)/shard_map/ppermute | solution.py:242
  80.6 20.7 %collective-permute-start.4 = (bf16[4,4,64,384]{3,2,1,0:T(8,128)(2,1)S(1)}, bf16[4,4,64,384]{3,2,1,0:T(8,128)(2,1)S(1)}, u32[]{:S(2)}, u32[]{:S(2)}) collective-permute-start(bf16[4,4,64,384]{3,2,1,0:T(8,128)(2,1)S(1)} %pad_maximum_fusion.refs_0_), channel_id=1, source_target_pairs={{0,32},{32,64},{64,96},{96,0},{1,33},{33,65},{65,97},{97,1},{2,34}... | collective-permute-start | bytes 2359304 | tf_op jit(solution)/shard_map/ppermute | solution.py:242
  83.8 22.0 %collective-permute-start.5 = (bf16[4,4,64,384]{3,2,1,0:T(8,128)(2,1)S(1)}, bf16[4,4,64,384]{3,2,1,0:T(8,128)(2,1)S(1)}, u32[]{:S(2)}, u32[]{:S(2)}) collective-permute-start(bf16[4,4,64,384]{3,2,1,0:T(8,128)(2,1)S(1)} %pad_maximum_fusion.refs_0_), channel_id=1, source_target_pairs={{0,64},{32,96},{64,0},{96,32},{1,65},{33,97},{65,1},{97,33},{2,66}... | collective-permute-start | bytes 2359304 | tf_op jit(solution)/shard_map/ppermute | solution.py:242
  86.5 37.1 %collective-permute-start.6 = (bf16[4,4,64,384]{3,2,1,0:T(8,128)(2,1)S(1)}, bf16[4,4,64,384]{3,2,1,0:T(8,128)(2,1)}, u32[]{:S(2)}, u32[]{:S(2)}) collective-permute-start(bf16[4,4,64,384]{3,2,1,0:T(8,128)(2,1)S(1)} %pad_maximum_fusion.refs_0_), channel_id=1, source_target_pairs={{0,96},{32,0},{64,32},{96,64},{1,97},{33,1},{65,33},{97,65},{2,98}... | collective-permute-start | bytes 2359304 | tf_op jit(solution)/shard_map/ppermute | solution.py:242
  105.7 24.9 %copy-start.7 = (bf16[4,4,64,384]{3,2,1,0:T(8,128)(2,1)}, bf16[4,4,64,384]{3,2,1,0:T(8,128)(2,1)S(1)}, u32[]{:S(2)}) copy-start(bf16[4,4,64,384]{3,2,1,0:T(8,128)(2,1)S(1)} %collective-permute-done.5.refs_2_) | copy-start | bytes 2359300
  123.6 2.3 copy-start.6
  130.7 1.1 copy-start.12
  131.8 5.2 %collective-permute-start.7 = (bf16[2,144,2176]{2,1,0:T(8,128)(2,1)}, bf16[2,144,2176]{2,1,0:T(8,128)(2,1)S(1)}, u32[]{:S(2)}, u32[]{:S(2)}) collective-permute-start(bf16[2,144,2176]{2,1,0:T(8,128)(2,1)} %get-tuple-element.31), channel_id=1, source_target_pairs={{0,1},{1,0},{2,3},{3,2},{4,5},{5,4},{6,7},{7,6},{8,9},{9,8},{10,11... | collective-permute-start | bytes 3760136 | tf_op jit(solution)/shard_map/ppermute | solution.py:242
  136.9 1.1 copy-start.8
  138.1 1.3 copy-start.13
  155.9 0.9 copy-start
  156.8 0.9 copy-start.9
  157.6 0.9 copy-start.10
  157.6 1.2 copy-start.11
  158.8 67.0 %all-to-all-start.1 = ((bf16[16,2,80,512]{3,2,1,0:T(8,128)(2,1)}), bf16[16,2,80,512]{3,2,1,0:T(8,128)(2,1)S(1)}, u32[]{:S(2)}, u32[]{:S(2)}) async-start(bf16[16,2,80,512]{3,2,1,0:T(8,128)(2,1)} %bitcast.32), calls=%async_computation.1 | async-start | bytes 5242880 | tf_op jit(solution)/shard_map/all_to_all | solution.py:327
  166.3 22.8 %collective-permute-start.10 = (bf16[4,4,64,384]{3,2,1,0:T(8,128)(2,1)}, bf16[4,4,64,384]{3,2,1,0:T(8,128)(2,1)S(1)}, u32[]{:S(2)}, u32[]{:S(2)}) collective-permute-start(bf16[4,4,64,384]{3,2,1,0:T(8,128)(2,1)} %copy-done.11), channel_id=1, source_target_pairs={{0,64},{32,96},{64,0},{96,32},{1,65},{33,97},{65,1},{97,33},{2,66}... | collective-permute-start | bytes 2359304 | tf_op jit(solution)/shard_map/ppermute | solution.py:242
  169.1 37.2 %collective-permute-start.11 = (bf16[4,4,64,384]{3,2,1,0:T(8,128)(2,1)}, bf16[4,4,64,384]{3,2,1,0:T(8,128)(2,1)S(1)}, u32[]{:S(2)}, u32[]{:S(2)}) collective-permute-start(bf16[4,4,64,384]{3,2,1,0:T(8,128)(2,1)} %copy-done.10), channel_id=1, source_target_pairs={{0,96},{32,0},{64,32},{96,64},{1,97},{33,1},{65,33},{97,65},{2,98}... | collective-permute-start | bytes 2359304 | tf_op jit(solution)/shard_map/ppermute | solution.py:242
  172.3 34.0 %collective-permute-start.9 = (bf16[4,4,64,384]{3,2,1,0:T(8,128)(2,1)}, bf16[4,4,64,384]{3,2,1,0:T(8,128)(2,1)S(1)}, u32[]{:S(2)}, u32[]{:S(2)}) collective-permute-start(bf16[4,4,64,384]{3,2,1,0:T(8,128)(2,1)} %copy-done.9), channel_id=1, source_target_pairs={{0,32},{32,64},{64,96},{96,0},{1,33},{33,65},{65,97},{97,1},{2,34}... | collective-permute-start | bytes 2359304 | tf_op jit(solution)/shard_map/ppermute | solution.py:242
  225.8 8.9 %copy-start.14 = (bf16[4,4,64,384]{3,2,1,0:T(8,128)(2,1)S(1)}, bf16[4,4,64,384]{3,2,1,0:T(8,128)(2,1)}, u32[]{:S(2)}) copy-start(bf16[4,4,64,384]{3,2,1,0:T(8,128)(2,1)} %add_convert_fusion) | copy-start | bytes 2359300
  226.7 38.7 %copy-start.4 = (s32[128,8]{0,1:T(8,128)S(1)}, s32[128,8]{0,1:T(8,128)}, u32[]{:S(2)}) copy-start(s32[128,8]{0,1:T(8,128)} %param.9) | copy-start | bytes 12292
  226.7 38.7 %collective-permute-start.8 = (bf16[128,1152]{1,0:T(8,128)(2,1)S(1)}, bf16[128,1152]{1,0:T(8,128)(2,1)S(1)}, u32[]{:S(2)}, u32[]{:S(2)}) collective-permute-start(bf16[128,1152]{1,0:T(8,128)(2,1)S(1)} %shard_map.97), channel_id=1, source_target_pairs={{0,2},{2,0},{1,3},{3,1},{4,6},{6,4},{5,7},{7,5},{8,10},{10,8},{9,1... | collective-permute-start | bytes 884744 | tf_op jit(solution)/shard_map/ppermute | solution.py:242
  234.8 14.9 %collective-permute-start.12 = (bf16[4,64,384]{2,1,0:T(8,128)(2,1)S(1)}, bf16[4,64,384]{2,1,0:T(8,128)(2,1)S(1)}, u32[]{:S(2)}, u32[]{:S(2)}) collective-permute-start(bf16[4,64,384]{2,1,0:T(8,128)(2,1)S(1)} %get-tuple-element.44), channel_id=1, source_target_pairs={{0,128},{128,256},{256,384},{384,0},{1,129},{129,257},{257,385},{3... | collective-permute-start | bytes 589832 | tf_op jit(solution)/shard_map/ppermute | solution.py:242
  236.7 24.5 %collective-permute-start.13 = (bf16[4,64,384]{2,1,0:T(8,128)(2,1)S(1)}, bf16[4,64,384]{2,1,0:T(8,128)(2,1)S(1)}, u32[]{:S(2)}, u32[]{:S(2)}) collective-permute-start(bf16[4,64,384]{2,1,0:T(8,128)(2,1)S(1)} %get-tuple-element.43), channel_id=1, source_target_pairs={{0,256},{128,384},{256,0},{384,128},{1,257},{129,385},{257,1},{385... | collective-permute-start | bytes 589832 | tf_op jit(solution)/shard_map/ppermute | solution.py:242
  238.6 26.0 %collective-permute-start.14 = (bf16[4,64,384]{2,1,0:T(8,128)(2,1)S(1)}, bf16[4,64,384]{2,1,0:T(8,128)(2,1)S(1)}, u32[]{:S(2)}, u32[]{:S(2)}) collective-permute-start(bf16[4,64,384]{2,1,0:T(8,128)(2,1)S(1)} %get-tuple-element.42), channel_id=1, source_target_pairs={{0,384},{128,0},{256,128},{384,256},{1,385},{129,1},{257,129},{385... | collective-permute-start | bytes 589832 | tf_op jit(solution)/shard_map/ppermute | solution.py:242
Sparse Core Ops, SparseCore 0:
  11.6 101.4 all-gather.2

commit v6 on v5

--- a/solution.py
+++ b/solution.py
@@ -153,8 +153,9 @@
         at = lax.bitwise_xor(spot[2], b) if b < 2 else b - 2
         left = dot(masks[0], grads[b, :, :half]) + dot(masks[1], grads[b, :, half:])
         first = left[:, :128] + dot(masks[2], marks[b])
-        back[:, at, b // 2, :, :128] = first.astype(BF).reshape(n_z, many, 128)
-        back[:, at, b // 2, :, 128:] = left[:, 128:].astype(BF).reshape(n_z, many, half - 128)
+        half_at = spot[4] if b < 2 else 1 - spot[4]
+        back[:, half_at, at, :, :128] = first.astype(BF).reshape(n_z, many, 128)
+        back[:, half_at, at, :, 128:] = left[:, 128:].astype(BF).reshape(n_z, many, half - 128)
     for d in range(n_x):
         for i in range(n_y):
             g_out[d][i] = parts[lax.rem(spot[0] + i, n_y) * n_x + lax.rem(spot[1] + d, n_x)]
@@ -189,12 +190,12 @@
         down[e] = sum(r[2 * e + 1].astype(F32) for r in ends).astype(BF)
 
 
-def partial_sums(cap, got, which, at, lane_places, owners, slots, place_l, place_r):
-    n_dev, _, _, half = got.shape
-    data = got[:, which].reshape(n_dev * 2 * SLOTS, half)
+def sums(cap, got, at, lane_places, owners, slots, place_l, place_r):
+    n_dev, _, half = got.shape
+    data = got[...].reshape(n_dev * 2 * SLOTS, half)
     left = dot((at == place_l[...]).astype(F32).astype(BF), data)
     right = dot((at == place_r[...]).astype(F32).astype(BF), data)
-    lines = got[:, which, 32:48, :128].reshape(n_dev * 16, 128)
+    lines = got[:, 32:48, :128].reshape(n_dev * 16, 128)
     by_place = jnp.zeros((slots.shape[1], 128), F32)
     for m in range(2):
         by_place = by_place + dot(dot(slots[m], lines, 1, 1).astype(BF), owners[m])
@@ -209,24 +210,14 @@
     return dot(table, sel[...], 0, 0), dot(table, same, 0, 0)
 
 
-def partner_kernel(cap, got, pay, sel, owners, slots, place_l, place_r, out):
-    width = out.shape[1] - 128
-    half = width // 2
-    at, by_expert = places_of(pay[HALF:, 2 * width :], sel)
-    left, right, scores = partial_sums(cap, got, 1, at, by_expert, owners, slots, place_l, place_r)
-    out[:, :half] = left.astype(BF)
-    out[:, half:width] = right.astype(BF)
-    out[:, width:] = scores.astype(BF)
-
-
-def combine_kernel(cap, got, table, ids, sel, owners, slots, place_l, place_r, other, grad_tok, grad_gate):
+def combine_kernel(cap, got, table, ids, sel, owners, slots, place_l, place_r, grad_tok, grad_gate):
     rows, width = grad_tok.shape
     half = width // 2
     at, by_expert = places_of(table[...], sel)
-    left, right, scores = partial_sums(cap, got, 0, at, by_expert, owners, slots, place_l, place_r)
-    grad_tok[:, :half] = (left + other[:, :half].astype(F32)).astype(BF)
-    grad_tok[:, half:] = (right + other[:, half:width].astype(F32)).astype(BF)
-    scores = (scores + other[:, width:].astype(F32)).T
+    left, right, scores = sums(cap, got, at, by_expert, owners, slots, place_l, place_r)
+    grad_tok[:, :half] = left.astype(BF)
+    grad_tok[:, half:] = right.astype(BF)
+    scores = scores.T
     expert = iota((128, rows), 0)
     line = iota(ids.shape, 0)
     chosen = ids[...]
@@ -266,7 +257,7 @@
         cost_estimate=cost(0.1, 2),
         compiler_params=params(8),
     )(tokens, grad_out, gates.T, expert_ids.T)
-    spot = jnp.stack([yl, x, c, (z * 2 + yh) * 4]).astype(jnp.int32)
+    spot = jnp.stack([yl, x, c, (z * 2 + yh) * 4, yh]).astype(jnp.int32)
     smem = [pl.BlockSpec(memory_space=pltpu.SMEM)]
     gath = lax.all_gather(pay, "z", axis=0)
     pay_other = shift(pay, "yh", 1)
@@ -324,7 +315,7 @@
         cost_estimate=cost(9, 24),
         compiler_params=params(44),
     )(spot, *w_parts, a_own, a_got, got_rows.reshape(n_z, 2, many, width))
-    got = lax.all_to_all(back.reshape(n_dev, 2, many, half), ("z", "c"), 0, 0, tiled=True)
+    got = lax.all_to_all(back.reshape(2 * n_dev, many, half), ("z", "yh", "c"), 0, 0, tiled=True)
 
     lines = [parts[0]] + [shift(parts[d], "x", d) for d in range(1, n_x)]
     line = sum(u.astype(F32) for u in lines).astype(BF)
@@ -339,35 +330,30 @@
     )(*ends)
     grad_down = jnp.transpose(grad_down, (0, 2, 1))
 
+    p = jnp.arange(2 * n_dev * many)
+    s_p = p % many
+    q = s_p % SLOTS
+    e_p = p // many * 2 + (q >= cap)
+    tgt = jnp.where(q < 2 * cap, q % cap + 1, -1)
     sel_p = (jnp.arange(HALF)[:, None] == e_p[None, :]).astype(BF)
     place_l = jnp.where(s_p < SLOTS, tgt, -1).astype(F32)[None, :]
     place_r = jnp.where(s_p >= SLOTS, tgt, -1).astype(F32)[None, :]
-    line_o = jnp.arange(n_dev * 16)
-    first_o = ((line_o // 32 * 2 + yh) * 2 + line_o // 16 % 2) * 2
-    first_o = jnp.where(line_o % 16 == 2 * cap - 32, first_o, -2)
+    line_o = jnp.arange(2 * n_dev * 16)
+    first_o = jnp.where(line_o % 16 == 2 * cap - 32, line_o // 16 * 2, -2)
     parity = jnp.arange(2)[:, None, None]
     owners = (first_o[None, :, None] + parity == jnp.arange(128)[None, None, :]).astype(BF)
     at_slot = jnp.arange(24)[None, :, None]
     slots = (
         (at_slot < cap) & (jnp.arange(128)[None, None, :] == at_slot + parity * cap)
     ).astype(BF)
-    partner = pl.pallas_call(
-        functools.partial(partner_kernel, cap),
-        out_shape=shape((rows, width + 128), BF),
-        in_specs=vmem(7),
-        out_specs=vmem(1)[0],
-        cost_estimate=cost(0.4, 4),
-        compiler_params=params(12),
-    )(got, pay_other, sel_p, owners, slots, place_l, place_r)
-    other = shift(partner, "yh", 1)
     grad_tokens, grad_gates = pl.pallas_call(
         functools.partial(combine_kernel, cap),
         out_shape=(shape((rows, width), BF), shape((top, rows), BF)),
-        in_specs=vmem(9),
+        in_specs=vmem(8),
         out_specs=tuple(vmem(2)),
         cost_estimate=cost(0.4, 4),
         compiler_params=params(12),
-    )(got, table, expert_ids.T, sel_p, owners, slots, place_l, place_r, other)
+    )(got, table, expert_ids.T, sel_p, owners, slots, place_l, place_r)
     return (grad_tokens, grad_gates.T, grad_up, grad_down)
 
 

time: 275 us -> 272 us (0.989)
  the two profiles are of different devices: /device:TPU:11 before, /device:TPU:315 now
where the time goes in v6:
time: 272 us; the launch traced here: 271 us
  waiting for transfers between devices  148 us (54%)
  starting transfers between devices  65.6 us (24%)
  Pallas kernels  28.4 us (10%)
  between operations  14.3 us (5%)
  local copies, waits for them, and re-layouts  12.4 us (5%)
    ppermute x14, waiting for transfers between devices, shift(): return lax.ppermute(value, axis, [(i, (i + by) % n) for i in range(n)])  148 us
    ppermute x14, starting transfers between devices, shift(): return lax.ppermute(value, axis, [(i, (i + by) % n) for i in range(n)])  45.5 us
    pallas_call x1, Pallas kernels, per_device(): pl.pallas_call(functools.partial(expert_kernel, n_y, n_x, cap), out_shape...  16.5 us
    all_to_all x1, starting transfers between devices, per_device(): lax.all_to_all(back.reshape(2 * n_dev, many, half), ('z', 'yh', 'c'), 0,...  12.2 us
    unnamed x32, local copies, waits for them, and re-layouts  12 us
    all_to_all x1, starting transfers between devices, per_device(): got_rows = lax.all_to_all(sent, ('z', 'c'), 0, 0, tiled=True)  7.79 us
  transfers between devices with their start and end apart: 17, of which 10 were waited for; matrix products, arithmetic and copies ran while one was open for 1% of the time, Pallas kernels for 3%

profile of v6, /device:TPU:315, one launch (start us, length us, event | category | flops | bytes accessed | tf_op | source)
XLA Modules:
  0.0 271.2 jit_solution(2680995502978807199)
XLA Ops:
  7.2 0.9 copy-done.1
  8.2 0.9 copy-done.2
  9.1 0.7 copy-done.3
  9.8 0.7 copy-done.5
  10.5 1.0 shard_map.93
  11.5 4.4 %collective-permute-start = (bf16[128,2176]{1,0:T(8,128)(2,1)}, bf16[128,2176]{1,0:T(8,128)(2,1)S(1)}, u32[]{:S(2)}, u32[]{:S(2)}) collective-permute-start(bf16[128,2176]{1,0:T(8,128)(2,1)} %get-tuple-element.23), channel_id=1, source_target_pairs={{0,2},{2,0},{1,3},{3,1},{4,6},{6,4},{5,7},{7,5},{8,10},{10,8},{9,1... | collective-permute-start | bytes 1671176 | tf_op jit(solution)/shard_map/ppermute | solution.py:233
  16.0 0.2 fusion.sel
  16.2 27.2 %collective-permute-done.pay = bf16[128,2176]{1,0:T(8,128)(2,1)S(1)} collective-permute-done((bf16[128,2176]{1,0:T(8,128)(2,1)}, bf16[128,2176]{1,0:T(8,128)(2,1)S(1)}, u32[]{:S(2)}, u32[]{:S(2)}) %collective-permute-start) | collective-permute-done | bytes 557088 | tf_op jit(solution)/shard_map/ppermute | solution.py:233
  43.4 0.2 broadcast_in_dim.11.place
  43.6 3.3 %shard_map.94 = bf16[16,80,1024]{2,1,0:T(8,128)(2,1)} custom-call(bf16[128,2176]{1,0:T(8,128)(2,1)S(1)} %collective-permute-done.pay, bf16[1280,64]{1,0:T(8,128)(2,1)S(1)} %fusion.sel, f32[1280,128]{1,0:T(8,128)S(1)} %broadcast_in_dim.11.place), custom_call_target="tpu_custom_call" | custom-call | flops 1000000000 | bytes 6291456 | tf_op jit(solution)/shard_map/pallas_call | solution.py:275
  46.9 7.8 %all-to-all-start = ((bf16[16,80,1024]{2,1,0:T(8,128)(2,1)}), bf16[16,80,1024]{2,1,0:T(8,128)(2,1)}, u32[]{:S(2)}, u32[]{:S(2)}) async-start(bf16[16,80,1024]{2,1,0:T(8,128)(2,1)} %shard_map.94), calls=%async_computation | async-start | bytes 5242880 | tf_op jit(solution)/shard_map/all_to_all | solution.py:283
  54.8 5.0 %collective-permute-start.1 = (bf16[4,64,384]{2,1,0:T(8,128)(2,1)S(1)}, bf16[4,64,384]{2,1,0:T(8,128)(2,1)S(1)}, u32[]{:S(2)}, u32[]{:S(2)}) collective-permute-start(bf16[4,64,384]{2,1,0:T(8,128)(2,1)S(1)} %bitcast.34), channel_id=1, source_target_pairs={{0,128},{128,256},{256,384},{384,0},{1,129},{129,257},{257,385},{3... | collective-permute-start | bytes 589832 | tf_op jit(solution)/shard_map/ppermute | solution.py:233
  59.8 1.9 collective-permute-start.2
  61.7 2.5 collective-permute-start.3
  64.2 12.9 %collective-permute-done.2 = bf16[4,64,384]{2,1,0:T(8,128)(2,1)S(1)} collective-permute-done((bf16[4,64,384]{2,1,0:T(8,128)(2,1)S(1)}, bf16[4,64,384]{2,1,0:T(8,128)(2,1)S(1)}, u32[]{:S(2)}, u32[]{:S(2)}) %collective-permute-start.2) | collective-permute-done | bytes 196640 | tf_op jit(solution)/shard_map/ppermute | solution.py:233
  77.3 3.1 %collective-permute-start.4 = (bf16[4,4,64,384]{3,2,1,0:T(8,128)(2,1)S(1)}, bf16[4,4,64,384]{3,2,1,0:T(8,128)(2,1)S(1)}, u32[]{:S(2)}, u32[]{:S(2)}) collective-permute-start(bf16[4,4,64,384]{3,2,1,0:T(8,128)(2,1)S(1)} %pad_maximum_fusion.refs_0_), channel_id=1, source_target_pairs={{0,32},{32,64},{64,96},{96,0},{1,33},{33,65},{65,97},{97,1},{2,34}... | collective-permute-start | bytes 2359304 | tf_op jit(solution)/shard_map/ppermute | solution.py:233
  80.4 2.7 %collective-permute-start.5 = (bf16[4,4,64,384]{3,2,1,0:T(8,128)(2,1)S(1)}, bf16[4,4,64,384]{3,2,1,0:T(8,128)(2,1)S(1)}, u32[]{:S(2)}, u32[]{:S(2)}) collective-permute-start(bf16[4,4,64,384]{3,2,1,0:T(8,128)(2,1)S(1)} %pad_maximum_fusion.refs_0_), channel_id=1, source_target_pairs={{0,64},{32,96},{64,0},{96,32},{1,65},{33,97},{65,1},{97,33},{2,66}... | collective-permute-start | bytes 2359304 | tf_op jit(solution)/shard_map/ppermute | solution.py:233
  83.2 3.8 %collective-permute-start.6 = (bf16[4,4,64,384]{3,2,1,0:T(8,128)(2,1)S(1)}, bf16[4,4,64,384]{3,2,1,0:T(8,128)(2,1)}, u32[]{:S(2)}, u32[]{:S(2)}) collective-permute-start(bf16[4,4,64,384]{3,2,1,0:T(8,128)(2,1)S(1)} %pad_maximum_fusion.refs_0_), channel_id=1, source_target_pairs={{0,96},{32,0},{64,32},{96,64},{1,97},{33,1},{65,33},{97,65},{2,98}... | collective-permute-start | bytes 2359304 | tf_op jit(solution)/shard_map/ppermute | solution.py:233
  87.0 10.4 %collective-permute-done.4.refs_1_ = bf16[4,4,64,384]{3,2,1,0:T(8,128)(2,1)S(1)} collective-permute-done((bf16[4,4,64,384]{3,2,1,0:T(8,128)(2,1)S(1)}, bf16[4,4,64,384]{3,2,1,0:T(8,128)(2,1)S(1)}, u32[]{:S(2)}, u32[]{:S(2)}) %collective-permute-start.4) | collective-permute-done | bytes 786464 | tf_op jit(solution)/shard_map/ppermute | solution.py:233
  97.4 4.4 %collective-permute-done.5.refs_2_ = bf16[4,4,64,384]{3,2,1,0:T(8,128)(2,1)S(1)} collective-permute-done((bf16[4,4,64,384]{3,2,1,0:T(8,128)(2,1)S(1)}, bf16[4,4,64,384]{3,2,1,0:T(8,128)(2,1)S(1)}, u32[]{:S(2)}, u32[]{:S(2)}) %collective-permute-start.5) | collective-permute-done | bytes 786464 | tf_op jit(solution)/shard_map/ppermute | solution.py:233
  101.8 18.4 %collective-permute-done.6.refs_3_ = bf16[4,4,64,384]{3,2,1,0:T(8,128)(2,1)} collective-permute-done((bf16[4,4,64,384]{3,2,1,0:T(8,128)(2,1)S(1)}, bf16[4,4,64,384]{3,2,1,0:T(8,128)(2,1)}, u32[]{:S(2)}, u32[]{:S(2)}) %collective-permute-start.6) | collective-permute-done | bytes 786464 | tf_op jit(solution)/shard_map/ppermute | solution.py:233
  120.2 2.3 copy-done.6
  122.5 4.8 %shard_map.95 = (bf16[2,144,2176]{2,1,0:T(8,128)(2,1)S(1)}, bf16[2,144,2176]{2,1,0:T(8,128)(2,1)}) custom-call(s32[5]{0:T(128)S(1)} %stack.47.spot, bf16[8,128,2176]{2,1,0:T(8,128)(2,1)S(1)} %bitcast.32), custom_call_target="tpu_custom_call" | custom-call | flops 2600000000 | bytes 12582912 | tf_op jit(solution)/shard_map/pallas_call | solution.py:292
  127.3 1.1 copy-done.12
  128.4 2.6 collective-permute-start.7
  131.0 2.6 collective-permute-done.7.refs_5_
  133.5 1.1 copy-done.8
  134.7 1.3 copy-done.13
  136.0 16.5 %shard_map.96 = (bf16[4,4,64,384]{3,2,1,0:T(8,128)(2,1)S(1)}, bf16[4,4,64,384]{3,2,1,0:T(8,128)(2,1)S(1)}, bf16[4,4,64,384]{3,2,1,0:T(8,128)(2,1)S(1)}, bf16[4,4...) custom-call(s32[5]{0:T(128)S(1)} %stack.47.spot, bf16[4,4,64,384]{3,2,1,0:T(8,128)(2,1)S(1)} %pad_maximum_fusion.refs_0_, ...), custom_call_target="tpu_custom_call" | custom-call | flops 8999999488 | bytes 25165824 | tf_op jit(solution)/shard_map/pallas_call | solution.py:301
  152.5 0.9 copy-done
  153.4 0.9 copy-done.9
  154.3 0.9 copy-done.10
  155.2 0.3 copy-done.11
  155.4 12.2 %all-to-all-start.1 = ((bf16[32,80,512]{2,1,0:T(8,128)(2,1)}), bf16[32,80,512]{2,1,0:T(8,128)(2,1)S(1)}, u32[]{:S(2)}, u32[]{:S(2)}) async-start(bf16[32,80,512]{2,1,0:T(8,128)(2,1)} %bitcast.33), calls=%async_computation.1 | async-start | bytes 5242880 | tf_op jit(solution)/shard_map/all_to_all | solution.py:318
  167.8 0.2 fusion.2.owners
  168.1 1.9 collective-permute-start.10
  170.0 3.4 %collective-permute-start.8 = (bf16[4,4,64,384]{3,2,1,0:T(8,128)(2,1)}, bf16[4,4,64,384]{3,2,1,0:T(8,128)(2,1)S(1)}, u32[]{:S(2)}, u32[]{:S(2)}) collective-permute-start(bf16[4,4,64,384]{3,2,1,0:T(8,128)(2,1)} %copy-done.10), channel_id=1, source_target_pairs={{0,32},{32,64},{64,96},{96,0},{1,33},{33,65},{65,97},{97,1},{2,34}... | collective-permute-start | bytes 2359304 | tf_op jit(solution)/shard_map/ppermute | solution.py:233
  173.4 3.9 %collective-permute-start.9 = (bf16[4,4,64,384]{3,2,1,0:T(8,128)(2,1)}, bf16[4,4,64,384]{3,2,1,0:T(8,128)(2,1)S(1)}, u32[]{:S(2)}, u32[]{:S(2)}) collective-permute-start(bf16[4,4,64,384]{3,2,1,0:T(8,128)(2,1)} %copy-done.9), channel_id=1, source_target_pairs={{0,64},{32,96},{64,0},{96,32},{1,65},{33,97},{65,1},{97,33},{2,66}... | collective-permute-start | bytes 2359304 | tf_op jit(solution)/shard_map/ppermute | solution.py:233
  177.5 11.5 %collective-permute-done.10 = bf16[4,4,64,384]{3,2,1,0:T(8,128)(2,1)S(1)} collective-permute-done((bf16[4,4,64,384]{3,2,1,0:T(8,128)(2,1)}, bf16[4,4,64,384]{3,2,1,0:T(8,128)(2,1)S(1)}, u32[]{:S(2)}, u32[]{:S(2)}) %collective-permute-start.10) | collective-permute-done | bytes 786464 | tf_op jit(solution)/shard_map/ppermute | solution.py:233
  189.0 2.2 collective-permute-done.8
  191.2 14.7 %collective-permute-done.9 = bf16[4,4,64,384]{3,2,1,0:T(8,128)(2,1)S(1)} collective-permute-done((bf16[4,4,64,384]{3,2,1,0:T(8,128)(2,1)}, bf16[4,4,64,384]{3,2,1,0:T(8,128)(2,1)S(1)}, u32[]{:S(2)}, u32[]{:S(2)}) %collective-permute-start.9) | collective-permute-done | bytes 786464 | tf_op jit(solution)/shard_map/ppermute | solution.py:233
  205.9 1.6 add_convert_fusion
  207.6 1.9 collective-permute-start.11
  209.6 5.0 %collective-permute-start.12 = (bf16[4,64,384]{2,1,0:T(8,128)(2,1)S(1)}, bf16[4,64,384]{2,1,0:T(8,128)(2,1)S(1)}, u32[]{:S(2)}, u32[]{:S(2)}) collective-permute-start(bf16[4,64,384]{2,1,0:T(8,128)(2,1)S(1)} %get-tuple-element.43), channel_id=1, source_target_pairs={{0,256},{128,384},{256,0},{384,128},{1,257},{129,385},{257,1},{385... | collective-permute-start | bytes 589832 | tf_op jit(solution)/shard_map/ppermute | solution.py:233
  214.6 3.4 %collective-permute-start.13 = (bf16[4,64,384]{2,1,0:T(8,128)(2,1)S(1)}, bf16[4,64,384]{2,1,0:T(8,128)(2,1)S(1)}, u32[]{:S(2)}, u32[]{:S(2)}) collective-permute-start(bf16[4,64,384]{2,1,0:T(8,128)(2,1)S(1)} %get-tuple-element.42), channel_id=1, source_target_pairs={{0,384},{128,0},{256,128},{384,256},{1,385},{129,1},{257,129},{385... | collective-permute-start | bytes 589832 | tf_op jit(solution)/shard_map/ppermute | solution.py:233
  218.1 43.4 %collective-permute-done.11.refs_1_ = bf16[4,64,384]{2,1,0:T(8,128)(2,1)S(1)} collective-permute-done((bf16[4,64,384]{2,1,0:T(8,128)(2,1)S(1)}, bf16[4,64,384]{2,1,0:T(8,128)(2,1)S(1)}, u32[]{:S(2)}, u32[]{:S(2)}) %collective-permute-start.11) | collective-permute-done | bytes 196640 | tf_op jit(solution)/shard_map/ppermute | solution.py:233
  261.5 0.8 shard_map.98
  262.3 2.1 shard_map.97
  (45 shorter events, 0.9 us)
Async XLA Ops:
  7.2 113.1 %all-gather.3.cloned.1.call-start = ((), (), s32[]{:S(2)}) async-start(), calls=%async_computation.2 | async-start | bytes 5013504 | tf_op jit(solution)/shard_map/all_gather | solution.py:262
  7.2 1.0 copy-start.1
  8.2 0.9 copy-start.2
  9.1 0.7 copy-start.3
  9.8 0.7 copy-start.5
  11.5 31.9 %collective-permute-start = (bf16[128,2176]{1,0:T(8,128)(2,1)}, bf16[128,2176]{1,0:T(8,128)(2,1)S(1)}, u32[]{:S(2)}, u32[]{:S(2)}) collective-permute-start(bf16[128,2176]{1,0:T(8,128)(2,1)} %get-tuple-element.23), channel_id=1, source_target_pairs={{0,2},{2,0},{1,3},{3,1},{4,6},{6,4},{5,7},{7,5},{8,10},{10,8},{9,1... | collective-permute-start | bytes 1671176 | tf_op jit(solution)/shard_map/ppermute | solution.py:233
  46.9 7.8 %copy-start.14 = (bf16[2,384,64]{1,2,0:T(8,128)(2,1)S(1)}, bf16[2,384,64]{1,2,0:T(8,128)(2,1)}, u32[]{:S(2)}) copy-start(bf16[2,384,64]{1,2,0:T(8,128)(2,1)} %param.11) | copy-start | bytes 294916
  46.9 7.8 %copy-start.15 = (bf16[2,64,384]{2,1,0:T(8,128)(2,1)S(1)}, bf16[2,64,384]{2,1,0:T(8,128)(2,1)}, u32[]{:S(2)}) copy-start(bf16[2,64,384]{2,1,0:T(8,128)(2,1)} %param.10) | copy-start | bytes 294916
  46.9 84.0 %all-to-all-start = ((bf16[16,80,1024]{2,1,0:T(8,128)(2,1)}), bf16[16,80,1024]{2,1,0:T(8,128)(2,1)}, u32[]{:S(2)}, u32[]{:S(2)}) async-start(bf16[16,80,1024]{2,1,0:T(8,128)(2,1)} %shard_map.94), calls=%async_computation | async-start | bytes 5242880 | tf_op jit(solution)/shard_map/all_to_all | solution.py:283
  54.8 9.4 %collective-permute-start.1 = (bf16[4,64,384]{2,1,0:T(8,128)(2,1)S(1)}, bf16[4,64,384]{2,1,0:T(8,128)(2,1)S(1)}, u32[]{:S(2)}, u32[]{:S(2)}) collective-permute-start(bf16[4,64,384]{2,1,0:T(8,128)(2,1)S(1)} %bitcast.34), channel_id=1, source_target_pairs={{0,128},{128,256},{256,384},{384,0},{1,129},{129,257},{257,385},{3... | collective-permute-start | bytes 589832 | tf_op jit(solution)/shard_map/ppermute | solution.py:233
  59.8 17.4 %collective-permute-start.2 = (bf16[4,64,384]{2,1,0:T(8,128)(2,1)S(1)}, bf16[4,64,384]{2,1,0:T(8,128)(2,1)S(1)}, u32[]{:S(2)}, u32[]{:S(2)}) collective-permute-start(bf16[4,64,384]{2,1,0:T(8,128)(2,1)S(1)} %bitcast.35), channel_id=1, source_target_pairs={{0,256},{128,384},{256,0},{384,128},{1,257},{129,385},{257,1},{385... | collective-permute-start | bytes 589832 | tf_op jit(solution)/shard_map/ppermute | solution.py:233
  61.7 15.4 %collective-permute-start.3 = (bf16[4,64,384]{2,1,0:T(8,128)(2,1)S(1)}, bf16[4,64,384]{2,1,0:T(8,128)(2,1)S(1)}, u32[]{:S(2)}, u32[]{:S(2)}) collective-permute-start(bf16[4,64,384]{2,1,0:T(8,128)(2,1)S(1)} %bitcast.36), channel_id=1, source_target_pairs={{0,384},{128,0},{256,128},{384,256},{1,385},{129,1},{257,129},{385... | collective-permute-start | bytes 589832 | tf_op jit(solution)/shard_map/ppermute | solution.py:233
  77.3 20.2 %collective-permute-start.4 = (bf16[4,4,64,384]{3,2,1,0:T(8,128)(2,1)S(1)}, bf16[4,4,64,384]{3,2,1,0:T(8,128)(2,1)S(1)}, u32[]{:S(2)}, u32[]{:S(2)}) collective-permute-start(bf16[4,4,64,384]{3,2,1,0:T(8,128)(2,1)S(1)} %pad_maximum_fusion.refs_0_), channel_id=1, source_target_pairs={{0,32},{32,64},{64,96},{96,0},{1,33},{33,65},{65,97},{97,1},{2,34}... | collective-permute-start | bytes 2359304 | tf_op jit(solution)/shard_map/ppermute | solution.py:233
  80.4 21.4 %collective-permute-start.5 = (bf16[4,4,64,384]{3,2,1,0:T(8,128)(2,1)S(1)}, bf16[4,4,64,384]{3,2,1,0:T(8,128)(2,1)S(1)}, u32[]{:S(2)}, u32[]{:S(2)}) collective-permute-start(bf16[4,4,64,384]{3,2,1,0:T(8,128)(2,1)S(1)} %pad_maximum_fusion.refs_0_), channel_id=1, source_target_pairs={{0,64},{32,96},{64,0},{96,32},{1,65},{33,97},{65,1},{97,33},{2,66}... | collective-permute-start | bytes 2359304 | tf_op jit(solution)/shard_map/ppermute | solution.py:233
  83.2 37.1 %collective-permute-start.6 = (bf16[4,4,64,384]{3,2,1,0:T(8,128)(2,1)S(1)}, bf16[4,4,64,384]{3,2,1,0:T(8,128)(2,1)}, u32[]{:S(2)}, u32[]{:S(2)}) collective-permute-start(bf16[4,4,64,384]{3,2,1,0:T(8,128)(2,1)S(1)} %pad_maximum_fusion.refs_0_), channel_id=1, source_target_pairs={{0,96},{32,0},{64,32},{96,64},{1,97},{33,1},{65,33},{97,65},{2,98}... | collective-permute-start | bytes 2359304 | tf_op jit(solution)/shard_map/ppermute | solution.py:233
  101.8 25.5 %copy-start.7 = (bf16[4,4,64,384]{3,2,1,0:T(8,128)(2,1)}, bf16[4,4,64,384]{3,2,1,0:T(8,128)(2,1)S(1)}, u32[]{:S(2)}) copy-start(bf16[4,4,64,384]{3,2,1,0:T(8,128)(2,1)S(1)} %collective-permute-done.5.refs_2_) | copy-start | bytes 2359300
  120.2 2.3 copy-start.6
  127.3 1.1 copy-start.12
  128.4 5.2 %collective-permute-start.7 = (bf16[2,144,2176]{2,1,0:T(8,128)(2,1)}, bf16[2,144,2176]{2,1,0:T(8,128)(2,1)S(1)}, u32[]{:S(2)}, u32[]{:S(2)}) collective-permute-start(bf16[2,144,2176]{2,1,0:T(8,128)(2,1)} %get-tuple-element.31), channel_id=1, source_target_pairs={{0,1},{1,0},{2,3},{3,2},{4,5},{5,4},{6,7},{7,6},{8,9},{9,8},{10,11... | collective-permute-start | bytes 3760136 | tf_op jit(solution)/shard_map/ppermute | solution.py:233
  133.5 1.1 copy-start.8
  134.7 1.3 copy-start.13
  152.5 0.9 copy-start
  153.4 0.9 copy-start.9
  154.2 0.9 copy-start.10
  154.2 1.2 copy-start.11
  155.4 106.8 %all-to-all-start.1 = ((bf16[32,80,512]{2,1,0:T(8,128)(2,1)}), bf16[32,80,512]{2,1,0:T(8,128)(2,1)S(1)}, u32[]{:S(2)}, u32[]{:S(2)}) async-start(bf16[32,80,512]{2,1,0:T(8,128)(2,1)} %bitcast.33), calls=%async_computation.1 | async-start | bytes 5242880 | tf_op jit(solution)/shard_map/all_to_all | solution.py:318
  168.1 20.9 %collective-permute-start.10 = (bf16[4,4,64,384]{3,2,1,0:T(8,128)(2,1)}, bf16[4,4,64,384]{3,2,1,0:T(8,128)(2,1)S(1)}, u32[]{:S(2)}, u32[]{:S(2)}) collective-permute-start(bf16[4,4,64,384]{3,2,1,0:T(8,128)(2,1)} %copy-done.11), channel_id=1, source_target_pairs={{0,96},{32,0},{64,32},{96,64},{1,97},{33,1},{65,33},{97,65},{2,98}... | collective-permute-start | bytes 2359304 | tf_op jit(solution)/shard_map/ppermute | solution.py:233
  170.0 21.1 %collective-permute-start.8 = (bf16[4,4,64,384]{3,2,1,0:T(8,128)(2,1)}, bf16[4,4,64,384]{3,2,1,0:T(8,128)(2,1)S(1)}, u32[]{:S(2)}, u32[]{:S(2)}) collective-permute-start(bf16[4,4,64,384]{3,2,1,0:T(8,128)(2,1)} %copy-done.10), channel_id=1, source_target_pairs={{0,32},{32,64},{64,96},{96,0},{1,33},{33,65},{65,97},{97,1},{2,34}... | collective-permute-start | bytes 2359304 | tf_op jit(solution)/shard_map/ppermute | solution.py:233
  173.4 32.5 %collective-permute-start.9 = (bf16[4,4,64,384]{3,2,1,0:T(8,128)(2,1)}, bf16[4,4,64,384]{3,2,1,0:T(8,128)(2,1)S(1)}, u32[]{:S(2)}, u32[]{:S(2)}) collective-permute-start(bf16[4,4,64,384]{3,2,1,0:T(8,128)(2,1)} %copy-done.9), channel_id=1, source_target_pairs={{0,64},{32,96},{64,0},{96,32},{1,65},{33,97},{65,1},{97,33},{2,66}... | collective-permute-start | bytes 2359304 | tf_op jit(solution)/shard_map/ppermute | solution.py:233
  207.5 54.7 %copy-start.4 = (s32[128,8]{0,1:T(8,128)S(1)}, s32[128,8]{0,1:T(8,128)}, u32[]{:S(2)}) copy-start(s32[128,8]{0,1:T(8,128)} %param.9) | copy-start | bytes 12292
  207.6 53.8 %collective-permute-start.11 = (bf16[4,64,384]{2,1,0:T(8,128)(2,1)S(1)}, bf16[4,64,384]{2,1,0:T(8,128)(2,1)S(1)}, u32[]{:S(2)}, u32[]{:S(2)}) collective-permute-start(bf16[4,64,384]{2,1,0:T(8,128)(2,1)S(1)} %get-tuple-element.44), channel_id=1, source_target_pairs={{0,128},{128,256},{256,384},{384,0},{1,129},{129,257},{257,385},{3... | collective-permute-start | bytes 589832 | tf_op jit(solution)/shard_map/ppermute | solution.py:233
  209.6 51.9 %collective-permute-start.12 = (bf16[4,64,384]{2,1,0:T(8,128)(2,1)S(1)}, bf16[4,64,384]{2,1,0:T(8,128)(2,1)S(1)}, u32[]{:S(2)}, u32[]{:S(2)}) collective-permute-start(bf16[4,64,384]{2,1,0:T(8,128)(2,1)S(1)} %get-tuple-element.43), channel_id=1, source_target_pairs={{0,256},{128,384},{256,0},{384,128},{1,257},{129,385},{257,1},{385... | collective-permute-start | bytes 589832 | tf_op jit(solution)/shard_map/ppermute | solution.py:233
  214.6 46.9 %collective-permute-start.13 = (bf16[4,64,384]{2,1,0:T(8,128)(2,1)S(1)}, bf16[4,64,384]{2,1,0:T(8,128)(2,1)S(1)}, u32[]{:S(2)}, u32[]{:S(2)}) collective-permute-start(bf16[4,64,384]{2,1,0:T(8,128)(2,1)S(1)} %get-tuple-element.42), channel_id=1, source_target_pairs={{0,384},{128,0},{256,128},{384,256},{1,385},{129,1},{257,129},{385... | collective-permute-start | bytes 589832 | tf_op jit(solution)/shard_map/ppermute | solution.py:233
Sparse Core Ops, SparseCore 0:
  11.6 99.7 all-gather.2

commit v7 on v5

--- a/solution.py
+++ b/solution.py
@@ -329,6 +329,7 @@
     lines = [parts[0]] + [shift(parts[d], "x", d) for d in range(1, n_x)]
     line = sum(u.astype(F32) for u in lines).astype(BF)
     ends = [line[0]] + [shift(line[d], "yl", d) for d in range(1, n_y)]
+    got, *ends = held(got, *ends)
     grad_up, grad_down = pl.pallas_call(
         total_kernel,
         out_shape=(shape((2, share, hidden_len), BF),) * 2,

time: 275 us -> 265 us (0.964)
  the two profiles are of different devices: /device:TPU:11 before, /device:TPU:9 now
where the time goes in v7:
time: 265 us; the launch traced here: 264 us
  waiting for transfers between devices  128 us (48%)
  starting transfers between devices  75.1 us (28%)
  Pallas kernels  28.8 us (11%)
  local copies, waits for them, and re-layouts  15.1 us (6%)
  between operations  14.4 us (5%)
    ppermute x15, waiting for transfers between devices, shift(): return lax.ppermute(value, axis, [(i, (i + by) % n) for i in range(n)])  128 us
    ppermute x15, starting transfers between devices, shift(): return lax.ppermute(value, axis, [(i, (i + by) % n) for i in range(n)])  54.2 us
    pallas_call x1, Pallas kernels, per_device(): pl.pallas_call(functools.partial(expert_kernel, n_y, n_x, cap), out_shape...  16.5 us
    unnamed x46, local copies, waits for them, and re-layouts  14.1 us
    all_to_all x1, starting transfers between devices, per_device(): got_rows = lax.all_to_all(sent, ('z', 'c'), 0, 0, tiled=True)  13.6 us
    all_to_all x1, starting transfers between devices, per_device(): lax.all_to_all(back.reshape(n_dev, 2, many, half), ('z', 'c'), 0, 0, tile...  7.22 us
  transfers between devices with their start and end apart: 18, of which 13 were waited for; matrix products, arithmetic and copies ran while one was open for 1% of the time, Pallas kernels for 3%

profile of v7, /device:TPU:9, one launch (start us, length us, event | category | flops | bytes accessed | tf_op | source)
XLA Modules:
  0.0 263.7 jit_solution(4611518145250016677)
XLA Ops:
  7.2 0.9 copy-done.2
  8.2 0.9 copy-done.3
  10.5 1.0 shard_map.93
  11.5 6.6 %collective-permute-start = (bf16[128,2176]{1,0:T(8,128)(2,1)}, bf16[128,2176]{1,0:T(8,128)(2,1)S(1)}, u32[]{:S(2)}, u32[]{:S(2)}) collective-permute-start(bf16[128,2176]{1,0:T(8,128)(2,1)} %get-tuple-element.28), channel_id=1, source_target_pairs={{0,2},{2,0},{1,3},{3,1},{4,6},{6,4},{5,7},{7,5},{8,10},{10,8},{9,1... | collective-permute-start | bytes 1671176 | tf_op jit(solution)/shard_map/ppermute | solution.py:242
  18.4 23.0 %collective-permute-done.pay = bf16[128,2176]{1,0:T(8,128)(2,1)S(1)} collective-permute-done((bf16[128,2176]{1,0:T(8,128)(2,1)}, bf16[128,2176]{1,0:T(8,128)(2,1)S(1)}, u32[]{:S(2)}, u32[]{:S(2)}) %collective-permute-start) | collective-permute-done | bytes 557088 | tf_op jit(solution)/shard_map/ppermute | solution.py:242
  41.6 3.3 %shard_map.94 = bf16[16,80,1024]{2,1,0:T(8,128)(2,1)} custom-call(bf16[128,2176]{1,0:T(8,128)(2,1)S(1)} %collective-permute-done.pay, bf16[1280,64]{1,0:T(8,128)(2,1)S(1)} %fusion.sel, f32[1280,128]{1,0:T(8,128)S(1)} %broadcast_in_dim.9.place), custom_call_target="tpu_custom_call" | custom-call | flops 1000000000 | bytes 6291456 | tf_op jit(solution)/shard_map/pallas_call | solution.py:284
  44.9 13.6 %all-to-all-start = ((bf16[16,80,1024]{2,1,0:T(8,128)(2,1)}), bf16[16,80,1024]{2,1,0:T(8,128)(2,1)}, u32[]{:S(2)}, u32[]{:S(2)}) async-start(bf16[16,80,1024]{2,1,0:T(8,128)(2,1)} %shard_map.94), calls=%async_computation | async-start | bytes 5242880 | tf_op jit(solution)/shard_map/all_to_all | solution.py:292
  58.5 3.4 %collective-permute-start.1 = (bf16[4,64,384]{2,1,0:T(8,128)(2,1)S(1)}, bf16[4,64,384]{2,1,0:T(8,128)(2,1)S(1)}, u32[]{:S(2)}, u32[]{:S(2)}) collective-permute-start(bf16[4,64,384]{2,1,0:T(8,128)(2,1)S(1)} %bitcast.33), channel_id=1, source_target_pairs={{0,128},{128,256},{256,384},{384,0},{1,129},{129,257},{257,385},{3... | collective-permute-start | bytes 589832 | tf_op jit(solution)/shard_map/ppermute | solution.py:242
  61.9 2.3 collective-permute-start.2
  64.3 2.7 %collective-permute-start.3 = (bf16[4,64,384]{2,1,0:T(8,128)(2,1)S(1)}, bf16[4,64,384]{2,1,0:T(8,128)(2,1)S(1)}, u32[]{:S(2)}, u32[]{:S(2)}) collective-permute-start(bf16[4,64,384]{2,1,0:T(8,128)(2,1)S(1)} %bitcast.35), channel_id=1, source_target_pairs={{0,384},{128,0},{256,128},{384,256},{1,385},{129,1},{257,129},{385... | collective-permute-start | bytes 589832 | tf_op jit(solution)/shard_map/ppermute | solution.py:242
  67.0 11.7 %collective-permute-done.2 = bf16[4,64,384]{2,1,0:T(8,128)(2,1)S(1)} collective-permute-done((bf16[4,64,384]{2,1,0:T(8,128)(2,1)S(1)}, bf16[4,64,384]{2,1,0:T(8,128)(2,1)S(1)}, u32[]{:S(2)}, u32[]{:S(2)}) %collective-permute-start.2) | collective-permute-done | bytes 196640 | tf_op jit(solution)/shard_map/ppermute | solution.py:242
  78.7 1.8 collective-permute-done.3
  80.6 3.1 %collective-permute-start.4 = (bf16[4,4,64,384]{3,2,1,0:T(8,128)(2,1)S(1)}, bf16[4,4,64,384]{3,2,1,0:T(8,128)(2,1)S(1)}, u32[]{:S(2)}, u32[]{:S(2)}) collective-permute-start(bf16[4,4,64,384]{3,2,1,0:T(8,128)(2,1)S(1)} %pad_maximum_fusion.refs_0_), channel_id=1, source_target_pairs={{0,32},{32,64},{64,96},{96,0},{1,33},{33,65},{65,97},{97,1},{2,34}... | collective-permute-start | bytes 2359304 | tf_op jit(solution)/shard_map/ppermute | solution.py:242
  83.7 4.4 %collective-permute-start.5 = (bf16[4,4,64,384]{3,2,1,0:T(8,128)(2,1)S(1)}, bf16[4,4,64,384]{3,2,1,0:T(8,128)(2,1)S(1)}, u32[]{:S(2)}, u32[]{:S(2)}) collective-permute-start(bf16[4,4,64,384]{3,2,1,0:T(8,128)(2,1)S(1)} %pad_maximum_fusion.refs_0_), channel_id=1, source_target_pairs={{0,64},{32,96},{64,0},{96,32},{1,65},{33,97},{65,1},{97,33},{2,66}... | collective-permute-start | bytes 2359304 | tf_op jit(solution)/shard_map/ppermute | solution.py:242
  88.1 3.1 %collective-permute-start.6 = (bf16[4,4,64,384]{3,2,1,0:T(8,128)(2,1)S(1)}, bf16[4,4,64,384]{3,2,1,0:T(8,128)(2,1)}, u32[]{:S(2)}, u32[]{:S(2)}) collective-permute-start(bf16[4,4,64,384]{3,2,1,0:T(8,128)(2,1)S(1)} %pad_maximum_fusion.refs_0_), channel_id=1, source_target_pairs={{0,96},{32,0},{64,32},{96,64},{1,97},{33,1},{65,33},{97,65},{2,98}... | collective-permute-start | bytes 2359304 | tf_op jit(solution)/shard_map/ppermute | solution.py:242
  91.3 11.3 %collective-permute-done.4.refs_1_ = bf16[4,4,64,384]{3,2,1,0:T(8,128)(2,1)S(1)} collective-permute-done((bf16[4,4,64,384]{3,2,1,0:T(8,128)(2,1)S(1)}, bf16[4,4,64,384]{3,2,1,0:T(8,128)(2,1)S(1)}, u32[]{:S(2)}, u32[]{:S(2)}) %collective-permute-start.4) | collective-permute-done | bytes 786464 | tf_op jit(solution)/shard_map/ppermute | solution.py:242
  102.6 17.8 %collective-permute-done.5.refs_2_ = bf16[4,4,64,384]{3,2,1,0:T(8,128)(2,1)S(1)} collective-permute-done((bf16[4,4,64,384]{3,2,1,0:T(8,128)(2,1)S(1)}, bf16[4,4,64,384]{3,2,1,0:T(8,128)(2,1)S(1)}, u32[]{:S(2)}, u32[]{:S(2)}) %collective-permute-start.5) | collective-permute-done | bytes 786464 | tf_op jit(solution)/shard_map/ppermute | solution.py:242
  120.4 1.2 collective-permute-done.6.refs_3_
  121.6 2.3 copy-done.13
  123.9 4.8 %shard_map.95 = (bf16[2,144,2176]{2,1,0:T(8,128)(2,1)S(1)}, bf16[2,144,2176]{2,1,0:T(8,128)(2,1)}) custom-call(s32[4]{0:T(128)S(1)} %pad_add_fusion.spot, bf16[8,128,2176]{2,1,0:T(8,128)(2,1)S(1)} %bitcast.31), custom_call_target="tpu_custom_call" | custom-call | flops 2600000000 | bytes 12582912 | tf_op jit(solution)/shard_map/pallas_call | solution.py:301
  128.7 1.1 copy-done.19
  129.8 3.6 %collective-permute-start.7 = (bf16[2,144,2176]{2,1,0:T(8,128)(2,1)}, bf16[2,144,2176]{2,1,0:T(8,128)(2,1)S(1)}, u32[]{:S(2)}, u32[]{:S(2)}) collective-permute-start(bf16[2,144,2176]{2,1,0:T(8,128)(2,1)} %get-tuple-element.36), channel_id=1, source_target_pairs={{0,1},{1,0},{2,3},{3,2},{4,5},{5,4},{6,7},{7,6},{8,9},{9,8},{10,11... | collective-permute-start | bytes 3760136 | tf_op jit(solution)/shard_map/ppermute | solution.py:242
  133.4 2.6 collective-permute-done.7.refs_5_
  136.0 1.1 copy-done.15
  137.1 1.3 copy-done.20
  138.4 16.5 %shard_map.96 = (bf16[4,4,64,384]{3,2,1,0:T(8,128)(2,1)S(1)}, bf16[4,4,64,384]{3,2,1,0:T(8,128)(2,1)S(1)}, bf16[4,4,64,384]{3,2,1,0:T(8,128)(2,1)S(1)}, bf16[4,4...) custom-call(s32[4]{0:T(128)S(1)} %pad_add_fusion.spot, bf16[4,4,64,384]{3,2,1,0:T(8,128)(2,1)S(1)} %pad_maximum_fusion.refs_0_, ...), custom_call_target="tpu_custom_call" | custom-call | flops 8999999488 | bytes 25165824 | tf_op jit(solution)/shard_map/pallas_call | solution.py:310
  155.0 0.9 copy-done.1
  155.9 0.9 copy-done.16
  156.7 0.9 copy-done.17
  157.9 7.2 %all-to-all-start.1 = ((bf16[16,2,80,512]{3,2,1,0:T(8,128)(2,1)}), bf16[16,2,80,512]{3,2,1,0:T(8,128)(2,1)S(1)}, u32[]{:S(2)}, u32[]{:S(2)}) async-start(bf16[16,2,80,512]{3,2,1,0:T(8,128)(2,1)} %bitcast.32), calls=%async_computation.1 | async-start | bytes 5242880 | tf_op jit(solution)/shard_map/all_to_all | solution.py:327
  165.3 4.3 %collective-permute-start.10 = (bf16[4,4,64,384]{3,2,1,0:T(8,128)(2,1)}, bf16[4,4,64,384]{3,2,1,0:T(8,128)(2,1)S(1)}, u32[]{:S(2)}, u32[]{:S(2)}) collective-permute-start(bf16[4,4,64,384]{3,2,1,0:T(8,128)(2,1)} %copy-done.18), channel_id=1, source_target_pairs={{0,96},{32,0},{64,32},{96,64},{1,97},{33,1},{65,33},{97,65},{2,98}... | collective-permute-start | bytes 2359304 | tf_op jit(solution)/shard_map/ppermute | solution.py:242
  169.6 1.9 collective-permute-start.8
  171.6 4.0 %collective-permute-start.9 = (bf16[4,4,64,384]{3,2,1,0:T(8,128)(2,1)}, bf16[4,4,64,384]{3,2,1,0:T(8,128)(2,1)S(1)}, u32[]{:S(2)}, u32[]{:S(2)}) collective-permute-start(bf16[4,4,64,384]{3,2,1,0:T(8,128)(2,1)} %copy-done.16), channel_id=1, source_target_pairs={{0,64},{32,96},{64,0},{96,32},{1,65},{33,97},{65,1},{97,33},{2,66}... | collective-permute-start | bytes 2359304 | tf_op jit(solution)/shard_map/ppermute | solution.py:242
  175.7 11.6 %collective-permute-done.10 = bf16[4,4,64,384]{3,2,1,0:T(8,128)(2,1)S(1)} collective-permute-done((bf16[4,4,64,384]{3,2,1,0:T(8,128)(2,1)}, bf16[4,4,64,384]{3,2,1,0:T(8,128)(2,1)S(1)}, u32[]{:S(2)}, u32[]{:S(2)}) %collective-permute-start.10) | collective-permute-done | bytes 786464 | tf_op jit(solution)/shard_map/ppermute | solution.py:242
  187.4 5.1 %collective-permute-done.8 = bf16[4,4,64,384]{3,2,1,0:T(8,128)(2,1)S(1)} collective-permute-done((bf16[4,4,64,384]{3,2,1,0:T(8,128)(2,1)}, bf16[4,4,64,384]{3,2,1,0:T(8,128)(2,1)S(1)}, u32[]{:S(2)}, u32[]{:S(2)}) %collective-permute-start.8) | collective-permute-done | bytes 786464 | tf_op jit(solution)/shard_map/ppermute | solution.py:242
  192.5 15.3 %collective-permute-done.9 = bf16[4,4,64,384]{3,2,1,0:T(8,128)(2,1)S(1)} collective-permute-done((bf16[4,4,64,384]{3,2,1,0:T(8,128)(2,1)}, bf16[4,4,64,384]{3,2,1,0:T(8,128)(2,1)S(1)}, u32[]{:S(2)}, u32[]{:S(2)}) %collective-permute-start.9) | collective-permute-done | bytes 786464 | tf_op jit(solution)/shard_map/ppermute | solution.py:242
  207.8 1.6 add_convert_fusion
  209.4 0.8 slice_bitcast_fusion
  210.2 1.9 collective-permute-start.11
  212.1 5.1 %collective-permute-start.12 = (bf16[4,64,384]{2,1,0:T(8,128)(2,1)S(1)}, bf16[4,64,384]{2,1,0:T(8,128)(2,1)S(1)}, u32[]{:S(2)}, u32[]{:S(2)}) collective-permute-start(bf16[4,64,384]{2,1,0:T(8,128)(2,1)S(1)} %get-tuple-element.53), channel_id=1, source_target_pairs={{0,256},{128,384},{256,0},{384,128},{1,257},{129,385},{257,1},{385... | collective-permute-start | bytes 589832 | tf_op jit(solution)/shard_map/ppermute | solution.py:242
  217.3 3.4 %collective-permute-start.13 = (bf16[4,64,384]{2,1,0:T(8,128)(2,1)S(1)}, bf16[4,64,384]{2,1,0:T(8,128)(2,1)S(1)}, u32[]{:S(2)}, u32[]{:S(2)}) collective-permute-start(bf16[4,64,384]{2,1,0:T(8,128)(2,1)S(1)} %get-tuple-element.52), channel_id=1, source_target_pairs={{0,384},{128,0},{256,128},{384,256},{1,385},{129,1},{257,129},{385... | collective-permute-start | bytes 589832 | tf_op jit(solution)/shard_map/ppermute | solution.py:242
  221.4 7.7 %collective-permute-done.12.refs_2_ = bf16[4,64,384]{2,1,0:T(8,128)(2,1)S(1)} collective-permute-done((bf16[4,64,384]{2,1,0:T(8,128)(2,1)S(1)}, bf16[4,64,384]{2,1,0:T(8,128)(2,1)S(1)}, u32[]{:S(2)}, u32[]{:S(2)}) %collective-permute-start.12) | collective-permute-done | bytes 196640 | tf_op jit(solution)/shard_map/ppermute | solution.py:242
  229.8 3.5 %collective-permute-done.13.refs_3_ = bf16[4,64,384]{2,1,0:T(8,128)(2,1)S(1)} collective-permute-done((bf16[4,64,384]{2,1,0:T(8,128)(2,1)S(1)}, bf16[4,64,384]{2,1,0:T(8,128)(2,1)S(1)}, u32[]{:S(2)}, u32[]{:S(2)}) %collective-permute-start.13) | collective-permute-done | bytes 196640 | tf_op jit(solution)/shard_map/ppermute | solution.py:242
  234.0 0.9 shard_map.97
  234.9 4.6 %collective-permute-start.14 = (bf16[128,1152]{1,0:T(8,128)(2,1)S(1)}, bf16[128,1152]{1,0:T(8,128)(2,1)S(1)}, u32[]{:S(2)}, u32[]{:S(2)}) collective-permute-start(bf16[128,1152]{1,0:T(8,128)(2,1)S(1)} %shard_map.97), channel_id=1, source_target_pairs={{0,2},{2,0},{1,3},{3,1},{4,6},{6,4},{5,7},{7,5},{8,10},{10,8},{9,1... | collective-permute-start | bytes 884744 | tf_op jit(solution)/shard_map/ppermute | solution.py:242
  239.5 0.8 shard_map.99
  240.3 15.0 %collective-permute-done.14.other = bf16[128,1152]{1,0:T(8,128)(2,1)S(1)} collective-permute-done((bf16[128,1152]{1,0:T(8,128)(2,1)S(1)}, bf16[128,1152]{1,0:T(8,128)(2,1)S(1)}, u32[]{:S(2)}, u32[]{:S(2)}) %collective-permute-start.14) | collective-permute-done | bytes 294944 | tf_op jit(solution)/shard_map/ppermute | solution.py:242
  255.3 1.6 shard_map.98
  (61 shorter events, 5.0 us)
Async XLA Ops:
  7.2 114.5 %all-gather.3.cloned.1.call-start = ((), (), s32[]{:S(2)}) async-start(), calls=%async_computation.2 | async-start | bytes 5013504 | tf_op jit(solution)/shard_map/all_gather | solution.py:271
  7.2 1.0 copy-start.2
  8.2 0.9 copy-start.3
  9.1 0.7 copy-start.10
  9.8 0.7 copy-start.12
  11.5 29.9 %collective-permute-start = (bf16[128,2176]{1,0:T(8,128)(2,1)}, bf16[128,2176]{1,0:T(8,128)(2,1)S(1)}, u32[]{:S(2)}, u32[]{:S(2)}) collective-permute-start(bf16[128,2176]{1,0:T(8,128)(2,1)} %get-tuple-element.28), channel_id=1, source_target_pairs={{0,2},{2,0},{1,3},{3,1},{4,6},{6,4},{5,7},{7,5},{8,10},{10,8},{9,1... | collective-permute-start | bytes 1671176 | tf_op jit(solution)/shard_map/ppermute | solution.py:242
  44.9 13.6 %copy-start.21 = (bf16[2,384,64]{1,2,0:T(8,128)(2,1)S(1)}, bf16[2,384,64]{1,2,0:T(8,128)(2,1)}, u32[]{:S(2)}) copy-start(bf16[2,384,64]{1,2,0:T(8,128)(2,1)} %param.11) | copy-start | bytes 294916
  44.9 13.6 %copy-start.22 = (bf16[2,64,384]{2,1,0:T(8,128)(2,1)S(1)}, bf16[2,64,384]{2,1,0:T(8,128)(2,1)}, u32[]{:S(2)}) copy-start(bf16[2,64,384]{2,1,0:T(8,128)(2,1)} %param.10) | copy-start | bytes 294916
  44.9 88.6 %all-to-all-start = ((bf16[16,80,1024]{2,1,0:T(8,128)(2,1)}), bf16[16,80,1024]{2,1,0:T(8,128)(2,1)}, u32[]{:S(2)}, u32[]{:S(2)}) async-start(bf16[16,80,1024]{2,1,0:T(8,128)(2,1)} %shard_map.94), calls=%async_computation | async-start | bytes 5242880 | tf_op jit(solution)/shard_map/all_to_all | solution.py:292
  58.5 8.4 %collective-permute-start.1 = (bf16[4,64,384]{2,1,0:T(8,128)(2,1)S(1)}, bf16[4,64,384]{2,1,0:T(8,128)(2,1)S(1)}, u32[]{:S(2)}, u32[]{:S(2)}) collective-permute-start(bf16[4,64,384]{2,1,0:T(8,128)(2,1)S(1)} %bitcast.33), channel_id=1, source_target_pairs={{0,128},{128,256},{256,384},{384,0},{1,129},{129,257},{257,385},{3... | collective-permute-start | bytes 589832 | tf_op jit(solution)/shard_map/ppermute | solution.py:242
  61.9 16.8 %collective-permute-start.2 = (bf16[4,64,384]{2,1,0:T(8,128)(2,1)S(1)}, bf16[4,64,384]{2,1,0:T(8,128)(2,1)S(1)}, u32[]{:S(2)}, u32[]{:S(2)}) collective-permute-start(bf16[4,64,384]{2,1,0:T(8,128)(2,1)S(1)} %bitcast.34), channel_id=1, source_target_pairs={{0,256},{128,384},{256,0},{384,128},{1,257},{129,385},{257,1},{385... | collective-permute-start | bytes 589832 | tf_op jit(solution)/shard_map/ppermute | solution.py:242
  64.3 16.2 %collective-permute-start.3 = (bf16[4,64,384]{2,1,0:T(8,128)(2,1)S(1)}, bf16[4,64,384]{2,1,0:T(8,128)(2,1)S(1)}, u32[]{:S(2)}, u32[]{:S(2)}) collective-permute-start(bf16[4,64,384]{2,1,0:T(8,128)(2,1)S(1)} %bitcast.35), channel_id=1, source_target_pairs={{0,384},{128,0},{256,128},{384,256},{1,385},{129,1},{257,129},{385... | collective-permute-start | bytes 589832 | tf_op jit(solution)/shard_map/ppermute | solution.py:242
  80.6 22.0 %collective-permute-start.4 = (bf16[4,4,64,384]{3,2,1,0:T(8,128)(2,1)S(1)}, bf16[4,4,64,384]{3,2,1,0:T(8,128)(2,1)S(1)}, u32[]{:S(2)}, u32[]{:S(2)}) collective-permute-start(bf16[4,4,64,384]{3,2,1,0:T(8,128)(2,1)S(1)} %pad_maximum_fusion.refs_0_), channel_id=1, source_target_pairs={{0,32},{32,64},{64,96},{96,0},{1,33},{33,65},{65,97},{97,1},{2,34}... | collective-permute-start | bytes 2359304 | tf_op jit(solution)/shard_map/ppermute | solution.py:242
  83.7 36.7 %collective-permute-start.5 = (bf16[4,4,64,384]{3,2,1,0:T(8,128)(2,1)S(1)}, bf16[4,4,64,384]{3,2,1,0:T(8,128)(2,1)S(1)}, u32[]{:S(2)}, u32[]{:S(2)}) collective-permute-start(bf16[4,4,64,384]{3,2,1,0:T(8,128)(2,1)S(1)} %pad_maximum_fusion.refs_0_), channel_id=1, source_target_pairs={{0,64},{32,96},{64,0},{96,32},{1,65},{33,97},{65,1},{97,33},{2,66}... | collective-permute-start | bytes 2359304 | tf_op jit(solution)/shard_map/ppermute | solution.py:242
  88.1 33.5 %collective-permute-start.6 = (bf16[4,4,64,384]{3,2,1,0:T(8,128)(2,1)S(1)}, bf16[4,4,64,384]{3,2,1,0:T(8,128)(2,1)}, u32[]{:S(2)}, u32[]{:S(2)}) collective-permute-start(bf16[4,4,64,384]{3,2,1,0:T(8,128)(2,1)S(1)} %pad_maximum_fusion.refs_0_), channel_id=1, source_target_pairs={{0,96},{32,0},{64,32},{96,64},{1,97},{33,1},{65,33},{97,65},{2,98}... | collective-permute-start | bytes 2359304 | tf_op jit(solution)/shard_map/ppermute | solution.py:242
  120.4 8.3 %copy-start.14 = (bf16[4,4,64,384]{3,2,1,0:T(8,128)(2,1)}, bf16[4,4,64,384]{3,2,1,0:T(8,128)(2,1)S(1)}, u32[]{:S(2)}) copy-start(bf16[4,4,64,384]{3,2,1,0:T(8,128)(2,1)S(1)} %collective-permute-done.5.refs_2_) | copy-start | bytes 2359300
  121.6 2.3 copy-start.13
  128.7 1.1 copy-start.19
  129.8 6.2 %collective-permute-start.7 = (bf16[2,144,2176]{2,1,0:T(8,128)(2,1)}, bf16[2,144,2176]{2,1,0:T(8,128)(2,1)S(1)}, u32[]{:S(2)}, u32[]{:S(2)}) collective-permute-start(bf16[2,144,2176]{2,1,0:T(8,128)(2,1)} %get-tuple-element.36), channel_id=1, source_target_pairs={{0,1},{1,0},{2,3},{3,2},{4,5},{5,4},{6,7},{7,6},{8,9},{9,8},{10,11... | collective-permute-start | bytes 3760136 | tf_op jit(solution)/shard_map/ppermute | solution.py:242
  136.0 1.1 copy-start.15
  137.1 1.3 copy-start.20
  155.0 0.9 copy-start.1
  155.9 0.9 copy-start.16
  156.7 0.9 copy-start.17
  156.7 1.2 copy-start.18
  157.9 76.1 %all-to-all-start.1 = ((bf16[16,2,80,512]{3,2,1,0:T(8,128)(2,1)}), bf16[16,2,80,512]{3,2,1,0:T(8,128)(2,1)S(1)}, u32[]{:S(2)}, u32[]{:S(2)}) async-start(bf16[16,2,80,512]{3,2,1,0:T(8,128)(2,1)} %bitcast.32), calls=%async_computation.1 | async-start | bytes 5242880 | tf_op jit(solution)/shard_map/all_to_all | solution.py:327
  165.3 22.0 %collective-permute-start.10 = (bf16[4,4,64,384]{3,2,1,0:T(8,128)(2,1)}, bf16[4,4,64,384]{3,2,1,0:T(8,128)(2,1)S(1)}, u32[]{:S(2)}, u32[]{:S(2)}) collective-permute-start(bf16[4,4,64,384]{3,2,1,0:T(8,128)(2,1)} %copy-done.18), channel_id=1, source_target_pairs={{0,96},{32,0},{64,32},{96,64},{1,97},{33,1},{65,33},{97,65},{2,98}... | collective-permute-start | bytes 2359304 | tf_op jit(solution)/shard_map/ppermute | solution.py:242
  169.6 22.9 %collective-permute-start.8 = (bf16[4,4,64,384]{3,2,1,0:T(8,128)(2,1)}, bf16[4,4,64,384]{3,2,1,0:T(8,128)(2,1)S(1)}, u32[]{:S(2)}, u32[]{:S(2)}) collective-permute-start(bf16[4,4,64,384]{3,2,1,0:T(8,128)(2,1)} %copy-done.17), channel_id=1, source_target_pairs={{0,32},{32,64},{64,96},{96,0},{1,33},{33,65},{65,97},{97,1},{2,34}... | collective-permute-start | bytes 2359304 | tf_op jit(solution)/shard_map/ppermute | solution.py:242
  171.6 36.2 %collective-permute-start.9 = (bf16[4,4,64,384]{3,2,1,0:T(8,128)(2,1)}, bf16[4,4,64,384]{3,2,1,0:T(8,128)(2,1)S(1)}, u32[]{:S(2)}, u32[]{:S(2)}) collective-permute-start(bf16[4,4,64,384]{3,2,1,0:T(8,128)(2,1)} %copy-done.16), channel_id=1, source_target_pairs={{0,64},{32,96},{64,0},{96,32},{1,65},{33,97},{65,1},{97,33},{2,66}... | collective-permute-start | bytes 2359304 | tf_op jit(solution)/shard_map/ppermute | solution.py:242
  210.2 10.5 %collective-permute-start.11 = (bf16[4,64,384]{2,1,0:T(8,128)(2,1)S(1)}, bf16[4,64,384]{2,1,0:T(8,128)(2,1)S(1)}, u32[]{:S(2)}, u32[]{:S(2)}) collective-permute-start(bf16[4,64,384]{2,1,0:T(8,128)(2,1)S(1)} %get-tuple-element.54), channel_id=1, source_target_pairs={{0,128},{128,256},{256,384},{384,0},{1,129},{129,257},{257,385},{3... | collective-permute-start | bytes 589832 | tf_op jit(solution)/shard_map/ppermute | solution.py:242
  212.1 17.0 %collective-permute-start.12 = (bf16[4,64,384]{2,1,0:T(8,128)(2,1)S(1)}, bf16[4,64,384]{2,1,0:T(8,128)(2,1)S(1)}, u32[]{:S(2)}, u32[]{:S(2)}) collective-permute-start(bf16[4,64,384]{2,1,0:T(8,128)(2,1)S(1)} %get-tuple-element.53), channel_id=1, source_target_pairs={{0,256},{128,384},{256,0},{384,128},{1,257},{129,385},{257,1},{385... | collective-permute-start | bytes 589832 | tf_op jit(solution)/shard_map/ppermute | solution.py:242
  217.3 16.1 %collective-permute-start.13 = (bf16[4,64,384]{2,1,0:T(8,128)(2,1)S(1)}, bf16[4,64,384]{2,1,0:T(8,128)(2,1)S(1)}, u32[]{:S(2)}, u32[]{:S(2)}) collective-permute-start(bf16[4,64,384]{2,1,0:T(8,128)(2,1)S(1)} %get-tuple-element.52), channel_id=1, source_target_pairs={{0,384},{128,0},{256,128},{384,256},{1,385},{129,1},{257,129},{385... | collective-permute-start | bytes 589832 | tf_op jit(solution)/shard_map/ppermute | solution.py:242
  220.7 0.7 copy-start.4
  229.1 0.7 copy-start.6
  233.3 0.7 copy-start.8
  234.0 5.5 %copy-start = (bf16[4,64,384]{2,1,0:T(8,128)(2,1)S(1)}, bf16[4,64,384]{2,1,0:T(8,128)(2,1)}, u32[]{:S(2)}) copy-start(bf16[4,64,384]{2,1,0:T(8,128)(2,1)} %get-tuple-element.46.refs_0_) | copy-start | bytes 589828
  234.0 5.5 %copy-start.5 = (bf16[4,64,384]{2,1,0:T(8,128)(2,1)S(1)}, bf16[4,64,384]{2,1,0:T(8,128)(2,1)}, u32[]{:S(2)}) copy-start(bf16[4,64,384]{2,1,0:T(8,128)(2,1)} %copy-done.4) | copy-start | bytes 589828
  234.0 5.5 %copy-start.7 = (bf16[4,64,384]{2,1,0:T(8,128)(2,1)S(1)}, bf16[4,64,384]{2,1,0:T(8,128)(2,1)}, u32[]{:S(2)}) copy-start(bf16[4,64,384]{2,1,0:T(8,128)(2,1)} %copy-done.6) | copy-start | bytes 589828
  234.0 5.5 %copy-start.9 = (bf16[4,64,384]{2,1,0:T(8,128)(2,1)S(1)}, bf16[4,64,384]{2,1,0:T(8,128)(2,1)}, u32[]{:S(2)}) copy-start(bf16[4,64,384]{2,1,0:T(8,128)(2,1)} %copy-done.8) | copy-start | bytes 589828
  234.0 21.3 %copy-start.11 = (s32[128,8]{0,1:T(8,128)S(1)}, s32[128,8]{0,1:T(8,128)}, u32[]{:S(2)}) copy-start(s32[128,8]{0,1:T(8,128)} %param.9) | copy-start | bytes 12292
  234.9 20.4 %collective-permute-start.14 = (bf16[128,1152]{1,0:T(8,128)(2,1)S(1)}, bf16[128,1152]{1,0:T(8,128)(2,1)S(1)}, u32[]{:S(2)}, u32[]{:S(2)}) collective-permute-start(bf16[128,1152]{1,0:T(8,128)(2,1)S(1)} %shard_map.97), channel_id=1, source_target_pairs={{0,2},{2,0},{1,3},{3,1},{4,6},{6,4},{5,7},{7,5},{8,10},{10,8},{9,1... | collective-permute-start | bytes 884744 | tf_op jit(solution)/shard_map/ppermute | solution.py:242
Sparse Core Ops, SparseCore 0:
  11.6 101.6 all-gather.2
